TPU v7x, 32 devices: a whole 2x2x4 slice. The times are simulated.
32 devices in a mesh: ex: 8 (over y, x, core), ey: 4 (over z).
Axes of the slice: x: 2, y: 2, z: 4, core: 2. Of those that a mesh axis runs over, the one named last changes fastest.
Arguments:
- tokens: bfloat16 [2048, 3584], P(('ex', 'ey')), may hold values from -6 to 6
- route_ids: int32 [2048, 8], P(('ex', 'ey')), may hold values from 0 to 31, all different within a row; in each aligned block of 64 rows (0 to 63, 64 to 127, ...) at most 32 rows name the same one
- route_weight: bfloat16 [2048, 8], P(('ex', 'ey')), may hold values from 0.19921875 to 1
- w_gate: bfloat16 [32, 3584, 1024], P(('ex', 'ey')), may hold values from -0.09375 to 0.09375
- w_up: bfloat16 [32, 3584, 1024], P(('ex', 'ey')), may hold values from -0.09375 to 0.09375
- w_down: bfloat16 [32, 1024, 3584], P(('ex', 'ey')), may hold values from -0.1875 to 0.1875
- shared_gate: bfloat16 [3584, 2048], P(None, 'ex'), may hold values from -0.09375 to 0.09375
- shared_up: bfloat16 [3584, 2048], P(None, 'ex'), may hold values from -0.09375 to 0.09375
- shared_down: bfloat16 [2048, 3584], P('ex'), may hold values from -0.125 to 0.125
Outputs:
- layer_out: bfloat16 [2048, 3584], P(('ex', 'ey'))
Inputs may be any that keep to these rules, and one draw needn't show every extreme that they name: `route_ids`: each row names 8 different experts; within the rows of one device no expert is named more than 32 times, a bound that some block reaches.
All inputs are finite; a program needn't handle non-finite values.
Results may differ from a plain program's by a relative error of at most 0.009.
Values may be sent and summed in bfloat16 or wider, within the bound.
No kernel may reach another device: no remote copies, remote signals or barrier semaphores. Data moves between devices by JAX's collectives and lax.ppermute only.
A program may use at most 128 MiB of HBM per device.

v0:
```python
import jax
import jax.numpy as jnp
from jax import lax
from jax.sharding import PartitionSpec as P


def swiglu(chosen, gate_weight, up_weight, down_weight):
    gate_act = jnp.dot(chosen, gate_weight, preferred_element_type=jnp.float32)
    up_act = jnp.dot(chosen, up_weight, preferred_element_type=jnp.float32)
    hidden = (jax.nn.silu(gate_act) * up_act).astype(jnp.bfloat16)
    return jnp.dot(hidden, down_weight, preferred_element_type=jnp.float32)


def shared_expert(tokens, shared_gate, shared_up, shared_down):
    gathered = lax.all_gather(tokens, "ex", axis=0, tiled=True)
    return lax.psum_scatter(
        swiglu(gathered, shared_gate, shared_up, shared_down).astype(jnp.bfloat16),
        "ex",
        scatter_dimension=0,
        tiled=True,
    ).astype(jnp.float32)


def shards(
    tokens, route_ids, route_weight, w_gate, w_up, w_down, shared_gate, shared_up, shared_down
):
    tok_rows = tokens.shape[0]
    top_count = route_ids.shape[1]
    width = tokens.shape[1]
    experts = lax.axis_size("ex") * lax.axis_size("ey")
    slot_most = max(2, 2 * tok_rows * top_count // experts)
    capacity = experts * slot_most
    flat_ids = route_ids.reshape(-1)
    onehot = (flat_ids[:, None] == jnp.arange(experts, dtype=jnp.int32)[None, :]).astype(jnp.int32)
    slot_rank = jnp.sum((jnp.cumsum(onehot, axis=0) - onehot) * onehot, axis=1)
    slot_place = flat_ids * slot_most + slot_rank
    matches = (slot_place[:, None] == jnp.arange(capacity, dtype=jnp.int32)[None, :]).astype(
        jnp.float32
    )
    matches = matches.reshape(tok_rows, top_count, capacity)
    placing = jnp.sum(matches, axis=1).astype(jnp.bfloat16)
    combine_mat = jnp.sum(matches * route_weight.astype(jnp.float32)[:, :, None], axis=1).astype(
        jnp.bfloat16
    )
    outgoing = jnp.einsum("tc,td->cd", placing, tokens, preferred_element_type=jnp.float32).astype(
        jnp.bfloat16
    )
    outgoing = outgoing.reshape(experts, slot_most, width)
    arrived = lax.all_to_all(outgoing, ("ex", "ey"), split_axis=0, concat_axis=0, tiled=True)
    layout = arrived.shape
    result = swiglu(arrived.reshape(-1, width), w_gate[0], w_up[0], w_down[0])
    produced = result.astype(jnp.bfloat16).reshape(layout)
    returned = lax.all_to_all(produced, ("ex", "ey"), split_axis=0, concat_axis=0, tiled=True)
    returned = returned.reshape(capacity, width)
    routed = jnp.dot(combine_mat, returned, preferred_element_type=jnp.float32)
    shared = shared_expert(tokens, shared_gate, shared_up, shared_down)
    return (shared + routed).astype(jnp.bfloat16)


def solution(mesh):
    in_specs = (
        P(("ex", "ey"), None),
        P(("ex", "ey"), None),
        P(("ex", "ey"), None),
        P(("ex", "ey"), None, None),
        P(("ex", "ey"), None, None),
        P(("ex", "ey"), None, None),
        P(None, "ex"),
        P(None, "ex"),
        P("ex", None),
    )
    out_specs = P(("ex", "ey"), None)
    return jax.shard_map(shards, mesh=mesh, in_specs=in_specs, out_specs=out_specs, check_vma=False)
```

profile of v0, /device:TPU:8, one launch (start us, length us, event | category | flops | bytes accessed | tf_op | source)
XLA Modules:
  0.0 392.4 jit_solution(973142995086762152)
XLA Ops:
  6.5 0.9 copy.24
  7.4 0.1 eq.43
  7.5 0.1 eq.39
  7.6 0.8 copy.29
  8.4 1.2 reduce-window.6
  9.6 0.2 slice_reduce_fusion
  9.8 0.1 fusion.19
  9.9 0.1 reduce_sum.30
  10.1 0.7 multiply_add_fusion
  10.9 1.3 select_reduce_fusion
  12.3 3.3 convolution_convert_fusion.1
  15.6 167.1 %all_to_all.10 = bf16[32,32,3584]{2,1,0:T(8,128)(2,1)S(1)} all-to-all(bf16[32,32,3584]{2,1,0:T(8,128)(2,1)S(1)} %bitcast.46), channel_id=1, replica_groups=mesh['ex'=8,'ey'=4] {'ex','ey'}, dimensions={0} | all-to-all | bytes 14680064 | tf_op jit(solution)/shard_map/all_to_all | solution.py:49
  182.6 9.3 %fusion.1 = f32[1024,1024]{1,0:T(8,128)} fusion(bf16[1024,3584]{1,0:T(8,128)(2,1)S(1)} %bitcast.48, bf16[1,3584,1024]{2,1,0:T(8,128)(2,1)S(1)} %bitcast.51), kind=kOutput, calls=%fused_computation.3 | convolution fusion | flops 7516192768 | bytes 18874368 | tf_op jit(solution)/shard_map/dot_general | solution.py:9
  191.9 10.3 %multiply_convert_fusion = bf16[1024,1024]{1,0:T(8,128)(2,1)S(1)} fusion(f32[1024,1024]{1,0:T(8,128)} %fusion.1, bf16[1024,3584]{1,0:T(8,128)(2,1)S(1)} %bitcast.49, bf16[1,3584,1024]{2,1,0:T(8,128)(2,1)S(1)} %bitcast.53), kind=kOutput, calls=%fused_computation.10 | convolution fusion | flops 7522484224 | bytes 20971520 | tf_op jit(solution)/shard_map/dot_general | solution.py:8
  202.2 9.7 %convolution_convert_fusion = bf16[1024,3584]{1,0:T(8,128)(2,1)} fusion(bf16[1024,1024]{1,0:T(8,128)(2,1)S(1)} %multiply_convert_fusion, bf16[1,1024,3584]{2,1,0:T(8,128)(2,1)S(1)} %bitcast.55), kind=kOutput, calls=%fused_computation | convolution fusion | flops 7519862784 | bytes 16777216 | tf_op jit(solution)/shard_map/dot_general | solution.py:11
  211.9 3.4 all-to-all-start.1
  215.4 0.7 all-gather.2.cloned.1.call-update
  216.1 0.2 reduce-scatter.2.cloned.1.call-start
  216.3 77.4 %all-gather.2.cloned.1.call-done = bf16[512,3584]{1,0:T(8,128)(2,1)} async-done(((bf16[64,3584]{1,0:T(8,128)(2,1)}), bf16[512,3584]{1,0:T(8,128)(2,1)}) %all-gather.2.cloned.1.call-update) | async-done | bytes 3670032 | tf_op jit(solution)/shard_map/all_gather | solution.py:15
  293.7 3.7 fusion.22
  297.4 8.3 %convolution_convert_fusion.2 = bf16[512,3584]{1,0:T(8,128)(2,1)} fusion(bf16[256,3584]{1,0:T(8,128)(2,1)S(1)} %copy-done, bf16[512,3584]{1,0:T(8,128)(2,1)} %all-gather.2.cloned.1.call-done, bf16[3584,256]{1,0:T(8,128)(2,1)} %param.16, f32[512,256]{1,0:T(8,128)S(1)} %fusion.22), kind=kOutput, calls=%fused_computation.7 | convolution fusion | flops 1881669632 | bytes 11534336 | tf_op jit(solution)/shard_map/dot_general | solution.py:11
  305.8 67.5 %reduce-scatter.2.cloned.1.call-done = bf16[64,3584]{1,0:T(8,128)(2,1)} async-done(((bf16[512,3584]{1,0:T(8,128)(2,1)}), bf16[64,3584]{1,0:T(8,128)(2,1)}) %reduce-scatter.2.cloned.1.call-update) | async-done | bytes 458768 | tf_op jit(solution)/shard_map/reduce_scatter | solution.py:16
  373.3 7.0 %all-to-all-done.1 = bf16[32,32,3584]{2,1,0:T(8,128)(2,1)} async-done(((bf16[32,32,3584]{2,1,0:T(8,128)(2,1)}), bf16[32,32,3584]{2,1,0:T(8,128)(2,1)}, u32[]{:S(2)}, u32[]{:S(2)}) %all-to-all-start.1) | async-done | bytes 7340064 | tf_op jit(solution)/shard_map/all_to_all | solution.py:53
  380.3 5.3 %fusion.5 = bf16[64,3584]{1,0:T(8,128)(2,1)} fusion(bf16[1024,3584]{1,0:T(8,128)(2,1)} %bitcast.7, bf16[64,3584]{1,0:T(8,128)(2,1)} %reduce-scatter.2.cloned.1.call-done, bf16[64,1024]{1,0:T(8,128)(2,1)S(1)} %get-tuple-element.5), kind=kOutput, calls=%fused_computation.9 | convolution fusion | flops 470450176 | bytes 8388608 | tf_op jit(solution)/shard_map/dot_general | solution.py:55
  (24 shorter events, 0.3 us)
Async XLA Ops:
  6.5 290.9 %copy-start = (bf16[256,3584]{1,0:T(8,128)(2,1)S(1)}, bf16[256,3584]{1,0:T(8,128)(2,1)}, u32[]{:S(2)}) copy-start(bf16[256,3584]{1,0:T(8,128)(2,1)} %param.17) | copy-start | bytes 5505028
  12.3 170.4 %slice-start = ((s8[7340032]{0:T(1024)(128)(4,1)}), s8[4194304]{0:T(1024)(128)(4,1)S(1)}, s32[]{:S(2)}) async-start(s8[7340032]{0:T(1024)(128)(4,1)} %bitcast.50), calls=%async_computation.5 | async-start | bytes 8388608
  15.5 167.1 %slice-start.1 = ((s8[7340032]{0:T(1024)(128)(4,1)}), s8[3145728]{0:T(1024)(128)(4,1)S(1)}, s32[]{:S(2)}) async-start(s8[7340032]{0:T(1024)(128)(4,1)} %bitcast.50), calls=%async_computation.6 | async-start | bytes 6291456
  15.5 176.4 %slice-start.2 = ((s8[7340032]{0:T(1024)(128)(4,1)}), s8[4194304]{0:T(1024)(128)(4,1)S(1)}, s32[]{:S(2)}) async-start(s8[7340032]{0:T(1024)(128)(4,1)} %bitcast.52), calls=%async_computation.7 | async-start | bytes 8388608
  182.6 9.3 %slice-start.3 = ((s8[7340032]{0:T(1024)(128)(4,1)}), s8[3145728]{0:T(1024)(128)(4,1)S(1)}, s32[]{:S(2)}) async-start(s8[7340032]{0:T(1024)(128)(4,1)} %bitcast.52), calls=%async_computation.8 | async-start | bytes 6291456
  182.6 19.6 %slice-start.4 = ((s8[7340032]{0:T(1024)(128)(4,1)}), s8[4194304]{0:T(1024)(128)(4,1)S(1)}, s32[]{:S(2)}) async-start(s8[7340032]{0:T(1024)(128)(4,1)} %bitcast.54), calls=%async_computation.9 | async-start | bytes 8388608
  191.9 10.3 %slice-start.5 = ((s8[7340032]{0:T(1024)(128)(4,1)}), s8[3145728]{0:T(1024)(128)(4,1)S(1)}, s32[]{:S(2)}) async-start(s8[7340032]{0:T(1024)(128)(4,1)} %bitcast.54), calls=%async_computation.10 | async-start | bytes 6291456
  211.9 168.4 %all-to-all-start.1 = ((bf16[32,32,3584]{2,1,0:T(8,128)(2,1)}), bf16[32,32,3584]{2,1,0:T(8,128)(2,1)}, u32[]{:S(2)}, u32[]{:S(2)}) async-start(bf16[32,32,3584]{2,1,0:T(8,128)(2,1)} %bitcast.47), calls=%async_computation.2 | async-start | bytes 14680064 | tf_op jit(solution)/shard_map/all_to_all | solution.py:53
  215.3 78.4 %all-gather.2.cloned.1.call-start = ((), (), s32[]{:S(2)}) async-start(), calls=%async_computation.3 | async-start | bytes 4128768 | tf_op jit(solution)/shard_map/all_gather | solution.py:15
  216.1 157.3 %reduce-scatter.2.cloned.1.call-start = ((), (), s32[]{:S(2)}) async-start(), calls=%async_computation.4 | async-start | bytes 4128768 | tf_op jit(solution)/shard_map/reduce_scatter | solution.py:16
Sparse Core Ops, SparseCore 0:
  218.0 75.5 all-gather.1
  305.9 67.3 reduce-scatter.1
where the time goes:
time: 393 us; the launch traced here: 392 us
  blocking collectives  167 us (42%)
  waiting for transfers between devices  153 us (39%)
  matrix products  49.8 us (13%)
  between operations  13.5 us (3%)
    all_to_all x1, blocking collectives, shards(): lax.all_to_all(outgoing, ('ex', 'ey'), split_axis=0, concat_axis=0, tiled...  167 us
    all_gather x1, waiting for transfers between devices, shared_expert(): gathered = lax.all_gather(tokens, 'ex', axis=0, tiled=True)  77.4 us
    reduce_scatter x1, waiting for transfers between devices, shared_expert(): lax.psum_scatter(swiglu(gathered, shared_gate, shared_up, shared_down).as...  67.5 us
    dot_general x2, matrix products, swiglu(): return jnp.dot(hidden, down_weight, preferred_element_type=jnp.float32)  18 us
    dot_general x2, matrix products, swiglu(): gate_act = jnp.dot(chosen, gate_weight, preferred_element_type=jnp.float32)  14 us
    dot_general x1, matrix products, swiglu(): up_act = jnp.dot(chosen, up_weight, preferred_element_type=jnp.float32)  9.27 us
  transfers between devices with their start and end apart: 3, of which 3 were waited for; matrix products, arithmetic and copies ran while one was open for 3% of the time, Pallas kernels for 0%

commit v1 on v0

--- a/solution.py
+++ b/solution.py
@@ -1,6 +1,10 @@
+import functools
+
 import jax
 import jax.numpy as jnp
 from jax import lax
+from jax.experimental import pallas as pl
+from jax.experimental.pallas import tpu as pltpu
 from jax.sharding import PartitionSpec as P
 
 
@@ -21,7 +25,7 @@
     ).astype(jnp.float32)
 
 
-def shards(
+def exchange_slots(
     tokens, route_ids, route_weight, w_gate, w_up, w_down, shared_gate, shared_up, shared_down
 ):
     tok_rows = tokens.shape[0]
@@ -57,7 +61,261 @@
     return (shared + routed).astype(jnp.bfloat16)
 
 
+PAIR, RIGHT, DOWN = 1, 2, 4
+
+
+def swap(value, axis, mask):
+    size = lax.axis_size(axis)
+    return lax.ppermute(value, axis, [(i, i ^ mask) for i in range(size)])
+
+
+def gather_plane(own, turn):
+    right = swap(own, "ex", RIGHT)
+    down = swap(own, "ex", DOWN)
+    across = swap(down, "ex", RIGHT) if turn else swap(right, "ex", DOWN)
+    return [own, right, down, across]
+
+
+def reduce_plane(mine, other, turn):
+    rows = mine.shape[0] // 4
+    f32 = jnp.float32
+    got = swap(other, "ex", PAIR)
+
+    def pair_sum(piece):
+        low = piece * rows
+        return mine[low : low + rows].astype(f32) + got[low : low + rows].astype(f32)
+
+    across = swap(pair_sum(3).astype(jnp.bfloat16), "ex", RIGHT if turn else DOWN).astype(f32)
+    right, down = pair_sum(1), pair_sum(2)
+    if turn:
+        down = down + across
+    else:
+        right = right + across
+    got_right = swap(right.astype(jnp.bfloat16), "ex", RIGHT)
+    got_down = swap(down.astype(jnp.bfloat16), "ex", DOWN)
+    return pair_sum(0) + got_right.astype(f32) + got_down.astype(f32)
+
+
+LANES = 128
+
+
+def tile_of(size, goal):
+    return max(t for t in range(LANES, goal + 1, LANES) if size % t == 0)
+
+
+def expert_body(dims, *refs):
+    count, block, most, width, hidden, shared_hidden, tile, span = dims
+    rows, slots = count * block, count * most
+    refs = list(refs)
+
+    def take(number):
+        out = refs[:number]
+        del refs[:number]
+        return out
+
+    pieces = take(2 * count)
+    w_gate, w_up, w_down = take(3)
+    shared = take(3) if shared_hidden else None
+    outs = take(2)
+    held, chosen, gate, up, down, act, back, result = take(8)
+    if shared:
+        s_gate, s_up, s_down, s_act = take(4)
+    piece_sem, gate_sem, up_sem, down_sem, out_sem = take(5)
+    if shared:
+        (shared_sem,) = take(1)
+    copy = pltpu.make_async_copy
+    steps, spans = hidden // tile, width // span
+    f32, bf16 = jnp.float32, jnp.bfloat16
+
+    def piece_copy(k):
+        return copy(pieces[k], held.at[pl.ds(k * block, block), :], piece_sem.at[k])
+
+    def gate_copy(k):
+        return copy(w_gate.at[0, :, pl.ds(k * tile, tile)], gate.at[k], gate_sem.at[k])
+
+    def up_copy(k):
+        return copy(w_up.at[0, :, pl.ds(k * tile, tile)], up.at[k], up_sem.at[k])
+
+    def down_copy(k):
+        return copy(w_down.at[0, :, pl.ds(k * span, span)], down.at[k], down_sem.at[k])
+
+    def shared_copy(k):
+        return copy(shared[k], (s_gate, s_up, s_down)[k], shared_sem.at[k])
+
+    def out_copy(side, k):
+        return copy(
+            result.at[side, k], outs[side].at[:, pl.ds(k * span, span)], out_sem.at[side, k]
+        )
+
+    for k in range(2 * count):
+        piece_copy(k).start()
+    if shared:
+        shared_copy(0).start()
+        shared_copy(1).start()
+    for k in range(steps):
+        gate_copy(k).start()
+        up_copy(k).start()
+    if shared:
+        shared_copy(2).start()
+    for k in range(spans):
+        down_copy(k).start()
+
+    me = lax.axis_index("ex") * lax.axis_size("ey") + lax.axis_index("ey")
+    pick = (lax.broadcasted_iota(jnp.int32, (16, LANES), 1) == me).astype(f32).astype(bf16)
+    early = lax.broadcasted_iota(jnp.int32, (rows, rows), 0)
+    late = lax.broadcasted_iota(jnp.int32, (rows, rows), 1)
+    before = ((early < late) & (early // block == late // block)).astype(f32).astype(bf16)
+    base = (lax.broadcasted_iota(jnp.int32, (1, rows), 1) // block * most).astype(f32)
+    slot = lax.broadcasted_iota(jnp.int32, (slots, rows), 0).astype(f32)
+    for side in range(2):
+        for k in range(side * count, (side + 1) * count):
+            piece_copy(k).wait()
+        low = side * rows
+        table = held[low : low + rows, width : width + LANES]
+        rate = lax.dot_general(
+            pick, table, (((1,), (1,)), ((), ())), preferred_element_type=f32
+        )
+        named = (rate > 0).astype(f32)
+        rank = jnp.dot(named.astype(bf16), before, preferred_element_type=f32)
+        where = jnp.where(named[0:1] > 0, rank[0:1] + base, -1.0)
+        place = slot == where
+        back[side] = jnp.where(place, rate[0:1], 0.0).T.astype(bf16)
+        onehot = place.astype(f32).astype(bf16)
+
+        @pl.loop(0, spans)
+        def _(k):
+            columns = pl.ds(pl.multiple_of(k * span, span), span)
+            chosen[side * slots : (side + 1) * slots, columns] = jnp.dot(
+                onehot, held[low : low + rows, columns], preferred_element_type=f32
+            ).astype(bf16)
+
+    if shared:
+        shared_copy(0).wait()
+        shared_copy(1).wait()
+        tokens = held[:, :width]
+        g = jnp.dot(tokens, s_gate[...], preferred_element_type=f32)
+        u = jnp.dot(tokens, s_up[...], preferred_element_type=f32)
+        s_act[...] = (jax.nn.silu(g) * u).astype(bf16)
+
+    @pl.loop(0, steps)
+    def _(k):
+        gate_copy(k).wait()
+        up_copy(k).wait()
+        g = jnp.dot(chosen[...], gate[k], preferred_element_type=f32)
+        u = jnp.dot(chosen[...], up[k], preferred_element_type=f32)
+        act[:, pl.ds(pl.multiple_of(k * tile, tile), tile)] = (jax.nn.silu(g) * u).astype(bf16)
+
+    if shared:
+        shared_copy(2).wait()
+
+    @pl.loop(0, spans)
+    def _(k):
+        down_copy(k).wait()
+        y = jnp.dot(act[...], down[k], preferred_element_type=f32).astype(bf16)
+        for side in (1, 0):
+            out = jnp.dot(
+                back[side], y[side * slots : (side + 1) * slots], preferred_element_type=f32
+            )
+            if shared:
+                out += jnp.dot(
+                    s_act[side * rows : (side + 1) * rows],
+                    s_down[:, pl.ds(pl.multiple_of(k * span, span), span)],
+                    preferred_element_type=f32,
+                )
+            result[side, k] = out.astype(bf16)
+            out_copy(side, k).start()
+
+    for k in range(spans):
+        out_copy(0, k).wait()
+        out_copy(1, k).wait()
+
+
+def run_expert(mine, other, most, weights, shared):
+    count, (block, wide) = len(mine), mine[0].shape
+    width, hidden = wide - LANES, weights[0].shape[2]
+    shared_hidden = shared[0].shape[1] if shared else 0
+    tile, span = tile_of(hidden, 256), tile_of(width, 1024)
+    rows, slots = count * block, count * most
+    dims = (count, block, most, width, hidden, shared_hidden, tile, span)
+    bf16 = jnp.bfloat16
+    vmem, sems = pltpu.VMEM, pltpu.SemaphoreType.DMA
+    scratch = [
+        vmem((2 * rows, wide), bf16),
+        vmem((2 * slots, width), bf16),
+        vmem((hidden // tile, width, tile), bf16),
+        vmem((hidden // tile, width, tile), bf16),
+        vmem((width // span, hidden, span), bf16),
+        vmem((2 * slots, hidden), bf16),
+        vmem((2, rows, slots), bf16),
+        vmem((2, width // span, rows, span), bf16),
+    ]
+    if shared:
+        scratch += [vmem(part.shape, bf16) for part in shared]
+        scratch += [vmem((2 * rows, shared_hidden), bf16)]
+    scratch += [
+        sems((2 * count,)),
+        sems((hidden // tile,)),
+        sems((hidden // tile,)),
+        sems((width // span,)),
+        sems((2, width // span)),
+    ]
+    if shared:
+        scratch += [sems((3,))]
+    operands = [*mine, *other, *weights, *(shared or ())]
+    flops = 2 * (6 * slots * width * hidden + 4 * rows * slots * width)
+    flops += 2 * 6 * rows * width * shared_hidden
+    moved = 2 * (sum(part.size for part in operands) + 2 * rows * width)
+    return pl.pallas_call(
+        functools.partial(expert_body, dims),
+        out_shape=[jax.ShapeDtypeStruct((rows, width), bf16)] * 2,
+        in_specs=[pl.BlockSpec(memory_space=pl.ANY)] * len(operands),
+        out_specs=[pl.BlockSpec(memory_space=pl.ANY)] * 2,
+        scratch_shapes=scratch,
+        compiler_params=pltpu.CompilerParams(vmem_limit_bytes=52 * 1024 * 1024),
+        cost_estimate=pl.CostEstimate(flops=flops, bytes_accessed=moved, transcendentals=0),
+    )(*operands)
+
+
+def gather_all(
+    tokens, route_ids, route_weight, w_gate, w_up, w_down, shared_gate, shared_up, shared_down
+):
+    block = tokens.shape[0]
+    planes = lax.axis_size("ey")
+    experts = lax.axis_size("ex") * planes
+    most = max(2, 2 * block * route_ids.shape[1] // experts)
+    hit = route_ids[:, :, None] == jnp.arange(LANES, dtype=jnp.int32)
+    table = jnp.sum(jnp.where(hit, route_weight[:, :, None], 0).astype(jnp.float32), axis=1)
+    own = jnp.concatenate([tokens, table.astype(tokens.dtype)], axis=1)
+    columns = [own] + [swap(own, "ey", mask) for mask in range(1, planes)]
+    order = list(range(1, planes)) + [0]
+    sums = []
+    for mask in order:
+        mine = gather_plane(columns[mask], mask % 2)
+        other = [swap(piece, "ex", PAIR) for piece in mine]
+        shared = None if mask else (shared_gate, shared_up, shared_down)
+        mine, other = run_expert(mine, other, most, (w_gate, w_up, w_down), shared)
+        part = reduce_plane(mine, other, mask % 2)
+        if mask:
+            part = swap(part.astype(jnp.bfloat16), "ey", mask).astype(jnp.float32)
+        sums.append(part)
+    total = sums[0]
+    for part in sums[1:]:
+        total = total + part
+    return total.astype(jnp.bfloat16)
+
+
 def solution(mesh):
+    sizes = dict(mesh.shape)
+
+    def shards(*args):
+        tokens, route_ids = args[0], args[1]
+        slots = max(2, 2 * tokens.shape[0] * route_ids.shape[1] // (sizes["ex"] * sizes["ey"]))
+        cube = sizes["ex"] == 2 * DOWN and sizes["ey"] & (sizes["ey"] - 1) == 0
+        cube = cube and sizes["ex"] * sizes["ey"] <= LANES
+        if cube and 4 * slots > tokens.shape[0]:
+            return gather_all(*args)
+        return exchange_slots(*args)
+
     in_specs = (
         P(("ex", "ey"), None),
         P(("ex", "ey"), None),

time: 393 us -> 280 us (0.71)
  blocking collectives: 167 us -> 0 us
  Pallas kernels: 0 us -> 78.1 us
  matrix products: 49.8 us -> 0 us
  starting transfers between devices: 3.64 us -> 40.4 us
  between operations: 13.5 us -> 0.34 us
  waiting for transfers between devices: 153 us -> 148 us
  other arithmetic: 3.38 us -> 7.96 us
    all_to_all x1 -> x0, blocking collectives: 167 us -> none  [shards(): lax.all_to_all(outgoing, ('ex', 'ey'), split_axis=0, concat_axis=0, tiled...]
    ppermute x0 -> x50, waiting for transfers between devices: none -> 148 us  [swap(): return lax.ppermute(value, axis, [(i, i ^ mask) for i in range(size)])]
    pallas_call x0 -> x4, Pallas kernels: none -> 78.1 us  [run_expert(): pl.pallas_call(functools.partial(expert_body, dims), out_shape=[jax.Shape...]
    all_gather x1 -> x0, waiting for transfers between devices: 77.4 us -> none  [shared_expert(): gathered = lax.all_gather(tokens, 'ex', axis=0, tiled=True)]
    reduce_scatter x1 -> x0, waiting for transfers between devices: 67.5 us -> none  [shared_expert(): lax.psum_scatter(swiglu(gathered, shared_gate, shared_up, shared_down).as...]
    dot_general x7 -> x0, matrix products: 49.8 us -> none  [the longest x2 18 us: swiglu(): return jnp.dot(hidden, down_weight, preferred_element_type=jnp.float32)]
    ppermute x0 -> x50, starting transfers between devices: none -> 40.4 us  [swap(): return lax.ppermute(value, axis, [(i, i ^ mask) for i in range(size)])]
    all_to_all x1 -> x0, waiting for transfers between devices: 6.95 us -> none  [shards(): lax.all_to_all(produced, ('ex', 'ey'), split_axis=0, concat_axis=0, tiled...]
  transfers between devices with their start and end apart: 3 -> 50, of which waited for: 3 -> 17; matrix products, arithmetic and copies ran while one was open for 3% -> 2% of each run, Pallas kernels for 0% -> 28%
where the time goes in v1:
time: 280 us; the launch traced here: 279 us
  waiting for transfers between devices  148 us (53%)
  Pallas kernels  78.1 us (28%)
  starting transfers between devices  40.4 us (14%)
  other arithmetic  7.96 us (3%)
  local copies, waits for them, and re-layouts  4.53 us (2%)
    ppermute x50, waiting for transfers between devices, swap(): return lax.ppermute(value, axis, [(i, i ^ mask) for i in range(size)])  148 us
    pallas_call x4, Pallas kernels, run_expert(): pl.pallas_call(functools.partial(expert_body, dims), out_shape=[jax.Shape...  78.1 us
    ppermute x50, starting transfers between devices, swap(): return lax.ppermute(value, axis, [(i, i ^ mask) for i in range(size)])  40.4 us
  transfers between devices with their start and end apart: 50, of which 17 were waited for; matrix products, arithmetic and copies ran while one was open for 2% of the time, Pallas kernels for 28%

profile of v1, /device:TPU:8, one launch (start us, length us, event | category | flops | bytes accessed | tf_op | source)
XLA Modules:
  0.0 279.2 jit_solution(7427430205823330460)
XLA Ops:
  2.9 3.0 %collective-permute-start.13 = (bf16[64,3712]{1,0:T(8,128)(2,1)S(1)}, bf16[64,3712]{1,0:T(8,128)(2,1)S(1)}, u32[]{:S(2)}, u32[]{:S(2)}) collective-permute-start(bf16[64,3712]{1,0:T(8,128)(2,1)S(1)} %pad_maximum_fusion.refs_0_), channel_id=1, source_target_pairs={{0,2},{1,3},{2,0},{3,1},{4,6},{5,7},{6,4},{7,5},{8,10},{9,11},{10,... | collective-permute-start | bytes 1425416 | tf_op jit(solution)/shard_map/ppermute | solution.py:69
  9.4 13.3 %collective-permute-done.refs_0_ = bf16[64,3712]{1,0:T(8,128)(2,1)S(1)} collective-permute-done((bf16[64,3712]{1,0:T(8,128)(2,1)S(1)}, bf16[64,3712]{1,0:T(8,128)(2,1)S(1)}, u32[]{:S(2)}, u32[]{:S(2)}) %collective-permute-start) | collective-permute-done | bytes 475168 | tf_op jit(solution)/shard_map/ppermute | solution.py:69
  22.7 14.9 %collective-permute-done.13.refs_0_ = bf16[64,3712]{1,0:T(8,128)(2,1)S(1)} collective-permute-done((bf16[64,3712]{1,0:T(8,128)(2,1)S(1)}, bf16[64,3712]{1,0:T(8,128)(2,1)S(1)}, u32[]{:S(2)}, u32[]{:S(2)}) %collective-permute-start.13) | collective-permute-done | bytes 475168 | tf_op jit(solution)/shard_map/ppermute | solution.py:69
  39.1 8.2 %collective-permute-done.26.refs_0_ = bf16[64,3712]{1,0:T(8,128)(2,1)S(1)} collective-permute-done((bf16[64,3712]{1,0:T(8,128)(2,1)S(1)}, bf16[64,3712]{1,0:T(8,128)(2,1)S(1)}, u32[]{:S(2)}, u32[]{:S(2)}) %collective-permute-start.26) | collective-permute-done | bytes 475168 | tf_op jit(solution)/shard_map/ppermute | solution.py:69
  51.1 10.0 %collective-permute-done.1.refs_1_ = bf16[64,3712]{1,0:T(8,128)(2,1)S(1)} collective-permute-done((bf16[64,3712]{1,0:T(8,128)(2,1)S(1)}, bf16[64,3712]{1,0:T(8,128)(2,1)S(1)}, u32[]{:S(2)}, u32[]{:S(2)}) %collective-permute-start.1) | collective-permute-done | bytes 475168 | tf_op jit(solution)/shard_map/ppermute | solution.py:69
  63.1 5.8 %collective-permute-done.14.refs_1_ = bf16[64,3712]{1,0:T(8,128)(2,1)S(1)} collective-permute-done((bf16[64,3712]{1,0:T(8,128)(2,1)S(1)}, bf16[64,3712]{1,0:T(8,128)(2,1)S(1)}, u32[]{:S(2)}, u32[]{:S(2)}) %collective-permute-start.14) | collective-permute-done | bytes 475168 | tf_op jit(solution)/shard_map/ppermute | solution.py:69
  68.9 1.6 collective-permute-start.28
  72.8 22.4 %shard_map.94 = (bf16[256,3584]{1,0:T(8,128)(2,1)}, bf16[256,3584]{1,0:T(8,128)(2,1)}) custom-call(bf16[64,3712]{1,0:T(8,128)(2,1)S(1)} %pad_maximum_fusion.refs_0_, bf16[64,3712]{1,0:T(8,128)(2,1)S(1)} %collective-permute-done.39.refs_1_, bf16[64,3712]{1,0:T(8,128)(2,1)S(1)} %collective-permute-done.40.refs_2_, ...), custom_call_target="tpu_custom_call" | custom-call | flops 9395240960 | bytes 34996224 | tf_op jit(solution)/shard_map/pallas_call | solution.py:268
  96.6 2.8 %collective-permute-done.6.refs_6_ = bf16[64,3712]{1,0:T(8,128)(2,1)S(1)} collective-permute-done((bf16[64,3712]{1,0:T(8,128)(2,1)S(1)}, bf16[64,3712]{1,0:T(8,128)(2,1)S(1)}, u32[]{:S(2)}, u32[]{:S(2)}) %collective-permute-start.6) | collective-permute-done | bytes 475168 | tf_op jit(solution)/shard_map/ppermute | solution.py:69
  100.5 8.7 %collective-permute-done.16.refs_3_ = bf16[64,3712]{1,0:T(8,128)(2,1)S(1)} collective-permute-done((bf16[64,3712]{1,0:T(8,128)(2,1)S(1)}, bf16[64,3712]{1,0:T(8,128)(2,1)S(1)}, u32[]{:S(2)}, u32[]{:S(2)}) %collective-permute-start.16) | collective-permute-done | bytes 475168 | tf_op jit(solution)/shard_map/ppermute | solution.py:69
  111.2 18.5 %shard_map.91 = (bf16[256,3584]{1,0:T(8,128)(2,1)}, bf16[256,3584]{1,0:T(8,128)(2,1)}) custom-call(bf16[64,3712]{1,0:T(8,128)(2,1)S(1)} %collective-permute-done.refs_0_, bf16[64,3712]{1,0:T(8,128)(2,1)S(1)} %collective-permute-done.1.refs_1_, bf16[64,3712]{1,0:T(8,128)(2,1)S(1)} %collective-permute-done.2.refs_2_, ...), custom_call_target="tpu_custom_call" | custom-call | flops 6576668672 | bytes 29491200 | tf_op jit(solution)/shard_map/pallas_call | solution.py:268
  131.2 18.6 %shard_map.92 = (bf16[256,3584]{1,0:T(8,128)(2,1)}, bf16[256,3584]{1,0:T(8,128)(2,1)}) custom-call(bf16[64,3712]{1,0:T(8,128)(2,1)S(1)} %collective-permute-done.13.refs_0_, bf16[64,3712]{1,0:T(8,128)(2,1)S(1)} %collective-permute-done.14.refs_1_, bf16[64,3712]{1,0:T(8,128)(2,1)S(1)} %collective-permute-done.15.refs_2_, ...), custom_call_target="tpu_custom_call" | custom-call | flops 6576668672 | bytes 29491200 | tf_op jit(solution)/shard_map/pallas_call | solution.py:268
  152.7 18.5 %shard_map.93 = (bf16[256,3584]{1,0:T(8,128)(2,1)}, bf16[256,3584]{1,0:T(8,128)(2,1)}) custom-call(bf16[64,3712]{1,0:T(8,128)(2,1)S(1)} %collective-permute-done.26.refs_0_, bf16[64,3712]{1,0:T(8,128)(2,1)S(1)} %collective-permute-done.27.refs_1_, bf16[64,3712]{1,0:T(8,128)(2,1)S(1)} %collective-permute-done.28.refs_2_, ...), custom_call_target="tpu_custom_call" | custom-call | flops 6576668672 | bytes 29491200 | tf_op jit(solution)/shard_map/pallas_call | solution.py:268
  178.7 16.3 %collective-permute-done.22 = bf16[64,3584]{1,0:T(8,128)(2,1)S(1)} collective-permute-done((bf16[64,3584]{1,0:T(8,128)(2,1)S(1)}, bf16[64,3584]{1,0:T(8,128)(2,1)S(1)}, u32[]{:S(2)}, u32[]{:S(2)}) %collective-permute-start.22) | collective-permute-done | bytes 458784 | tf_op jit(solution)/shard_map/ppermute | solution.py:69
  198.5 16.2 %collective-permute-done.36 = bf16[64,3584]{1,0:T(8,128)(2,1)S(1)} collective-permute-done((bf16[64,3584]{1,0:T(8,128)(2,1)S(1)}, bf16[64,3584]{1,0:T(8,128)(2,1)S(1)}, u32[]{:S(2)}, u32[]{:S(2)}) %collective-permute-start.36) | collective-permute-done | bytes 458784 | tf_op jit(solution)/shard_map/ppermute | solution.py:69
  217.2 8.9 %collective-permute-done.11 = bf16[64,3584]{1,0:T(8,128)(2,1)S(1)} collective-permute-done((bf16[64,3584]{1,0:T(8,128)(2,1)S(1)}, bf16[64,3584]{1,0:T(8,128)(2,1)S(1)}, u32[]{:S(2)}, u32[]{:S(2)}) %collective-permute-start.11) | collective-permute-done | bytes 458784 | tf_op jit(solution)/shard_map/ppermute | solution.py:69
  228.9 4.9 %collective-permute-done.23 = bf16[64,3584]{1,0:T(8,128)(2,1)S(1)} collective-permute-done((bf16[64,3584]{1,0:T(8,128)(2,1)S(1)}, bf16[64,3584]{1,0:T(8,128)(2,1)S(1)}, u32[]{:S(2)}, u32[]{:S(2)}) %collective-permute-start.23) | collective-permute-done | bytes 458784 | tf_op jit(solution)/shard_map/ppermute | solution.py:69
  235.3 1.8 collective-permute-done.24
  237.4 3.1 %collective-permute-start.25 = (bf16[64,3584]{1,0:T(8,128)(2,1)S(1)}, bf16[64,3584]{1,0:T(8,128)(2,1)S(1)}, u32[]{:S(2)}, u32[]{:S(2)}) collective-permute-start(bf16[64,3584]{1,0:T(8,128)(2,1)S(1)} %add_convert_fusion.8), channel_id=1, source_target_pairs={{0,2},{1,3},{2,0},{3,1},{4,6},{5,7},{6,4},{7,5},{8,10},{9,11},{10,... | collective-permute-start | bytes 1376264 | tf_op jit(solution)/shard_map/ppermute | solution.py:69
  240.5 5.9 %collective-permute-done.37 = bf16[64,3584]{1,0:T(8,128)(2,1)S(1)} collective-permute-done((bf16[64,3584]{1,0:T(8,128)(2,1)S(1)}, bf16[64,3584]{1,0:T(8,128)(2,1)S(1)}, u32[]{:S(2)}, u32[]{:S(2)}) %collective-permute-start.37) | collective-permute-done | bytes 458784 | tf_op jit(solution)/shard_map/ppermute | solution.py:69
  246.6 1.6 collective-permute-start.38
  248.3 5.3 %collective-permute-done.12 = bf16[64,3584]{1,0:T(8,128)(2,1)S(1)} collective-permute-done((bf16[64,3584]{1,0:T(8,128)(2,1)S(1)}, bf16[64,3584]{1,0:T(8,128)(2,1)S(1)}, u32[]{:S(2)}, u32[]{:S(2)}) %collective-permute-start.12) | collective-permute-done | bytes 458784 | tf_op jit(solution)/shard_map/ppermute | solution.py:69
  253.5 16.3 %collective-permute-done.25 = bf16[64,3584]{1,0:T(8,128)(2,1)S(1)} collective-permute-done((bf16[64,3584]{1,0:T(8,128)(2,1)S(1)}, bf16[64,3584]{1,0:T(8,128)(2,1)S(1)}, u32[]{:S(2)}, u32[]{:S(2)}) %collective-permute-start.25) | collective-permute-done | bytes 458784 | tf_op jit(solution)/shard_map/ppermute | solution.py:69
  269.8 8.2 %collective-permute-done.38 = bf16[64,3584]{1,0:T(8,128)(2,1)S(1)} collective-permute-done((bf16[64,3584]{1,0:T(8,128)(2,1)S(1)}, bf16[64,3584]{1,0:T(8,128)(2,1)S(1)}, u32[]{:S(2)}, u32[]{:S(2)}) %collective-permute-start.38) | collective-permute-done | bytes 458784 | tf_op jit(solution)/shard_map/ppermute | solution.py:69
  (136 shorter events, 44.0 us)
Async XLA Ops:
  2.9 34.7 %collective-permute-start.13 = (bf16[64,3712]{1,0:T(8,128)(2,1)S(1)}, bf16[64,3712]{1,0:T(8,128)(2,1)S(1)}, u32[]{:S(2)}, u32[]{:S(2)}) collective-permute-start(bf16[64,3712]{1,0:T(8,128)(2,1)S(1)} %pad_maximum_fusion.refs_0_), channel_id=1, source_target_pairs={{0,2},{1,3},{2,0},{3,1},{4,6},{5,7},{6,4},{7,5},{8,10},{9,11},{10,... | collective-permute-start | bytes 1425416 | tf_op jit(solution)/shard_map/ppermute | solution.py:69
  5.9 41.3 %collective-permute-start.26 = (bf16[64,3712]{1,0:T(8,128)(2,1)S(1)}, bf16[64,3712]{1,0:T(8,128)(2,1)S(1)}, u32[]{:S(2)}, u32[]{:S(2)}) collective-permute-start(bf16[64,3712]{1,0:T(8,128)(2,1)S(1)} %pad_maximum_fusion.refs_0_), channel_id=1, source_target_pairs={{0,3},{1,2},{2,1},{3,0},{4,7},{5,6},{6,5},{7,4},{8,11},{9,10},{10,... | collective-permute-start | bytes 1425416 | tf_op jit(solution)/shard_map/ppermute | solution.py:69
  6.4 42.4 %collective-permute-start.39 = (bf16[64,3712]{1,0:T(8,128)(2,1)S(1)}, bf16[64,3712]{1,0:T(8,128)(2,1)S(1)}, u32[]{:S(2)}, u32[]{:S(2)}) collective-permute-start(bf16[64,3712]{1,0:T(8,128)(2,1)S(1)} %pad_maximum_fusion.refs_0_), channel_id=1, source_target_pairs={{0,8},{4,12},{8,0},{12,4},{16,24},{20,28},{24,16},{28,20},{1,9},{5... | collective-permute-start | bytes 1425416 | tf_op jit(solution)/shard_map/ppermute | solution.py:69
  7.9 42.4 %collective-permute-start.40 = (bf16[64,3712]{1,0:T(8,128)(2,1)S(1)}, bf16[64,3712]{1,0:T(8,128)(2,1)S(1)}, u32[]{:S(2)}, u32[]{:S(2)}) collective-permute-start(bf16[64,3712]{1,0:T(8,128)(2,1)S(1)} %pad_maximum_fusion.refs_0_), channel_id=1, source_target_pairs={{0,16},{4,20},{8,24},{12,28},{16,0},{20,4},{24,8},{28,12},{1,17},{... | collective-permute-start | bytes 1425416 | tf_op jit(solution)/shard_map/ppermute | solution.py:69
  22.7 27.6 %collective-permute-start.42 = (bf16[64,3712]{1,0:T(8,128)(2,1)S(1)}, bf16[64,3712]{1,0:T(8,128)(2,1)S(1)}, u32[]{:S(2)}, u32[]{:S(2)}) collective-permute-start(bf16[64,3712]{1,0:T(8,128)(2,1)S(1)} %pad_maximum_fusion.refs_0_), channel_id=1, source_target_pairs={{0,4},{4,0},{8,12},{12,8},{16,20},{20,16},{24,28},{28,24},{1,5},{5... | collective-permute-start | bytes 1425416 | tf_op jit(solution)/shard_map/ppermute | solution.py:69
  61.6 33.7 %collective-permute-start.15 = (bf16[64,3712]{1,0:T(8,128)(2,1)S(1)}, bf16[64,3712]{1,0:T(8,128)(2,1)S(1)}, u32[]{:S(2)}, u32[]{:S(2)}) collective-permute-start(bf16[64,3712]{1,0:T(8,128)(2,1)S(1)} %collective-permute-done.13.refs_0_), channel_id=1, source_target_pairs={{0,16},{4,20},{8,24},{12,28},{16,0},{20,4},{24,8},{28,12},{1,17},{... | collective-permute-start | bytes 1425416 | tf_op jit(solution)/shard_map/ppermute | solution.py:69
  68.9 26.4 %collective-permute-start.17 = (bf16[64,3712]{1,0:T(8,128)(2,1)S(1)}, bf16[64,3712]{1,0:T(8,128)(2,1)S(1)}, u32[]{:S(2)}, u32[]{:S(2)}) collective-permute-start(bf16[64,3712]{1,0:T(8,128)(2,1)S(1)} %collective-permute-done.13.refs_0_), channel_id=1, source_target_pairs={{0,4},{4,0},{8,12},{12,8},{16,20},{20,16},{24,28},{28,24},{1,5},{5... | collective-permute-start | bytes 1425416 | tf_op jit(solution)/shard_map/ppermute | solution.py:69
  68.9 26.9 %collective-permute-start.28 = (bf16[64,3712]{1,0:T(8,128)(2,1)S(1)}, bf16[64,3712]{1,0:T(8,128)(2,1)S(1)}, u32[]{:S(2)}, u32[]{:S(2)}) collective-permute-start(bf16[64,3712]{1,0:T(8,128)(2,1)S(1)} %collective-permute-done.26.refs_0_), channel_id=1, source_target_pairs={{0,16},{4,20},{8,24},{12,28},{16,0},{20,4},{24,8},{28,12},{1,17},{... | collective-permute-start | bytes 1425416 | tf_op jit(solution)/shard_map/ppermute | solution.py:69
  70.5 25.4 %collective-permute-start.27 = (bf16[64,3712]{1,0:T(8,128)(2,1)S(1)}, bf16[64,3712]{1,0:T(8,128)(2,1)S(1)}, u32[]{:S(2)}, u32[]{:S(2)}) collective-permute-start(bf16[64,3712]{1,0:T(8,128)(2,1)S(1)} %collective-permute-done.26.refs_0_), channel_id=1, source_target_pairs={{0,8},{4,12},{8,0},{12,4},{16,24},{20,28},{24,16},{28,20},{1,9},{5... | collective-permute-start | bytes 1425416 | tf_op jit(solution)/shard_map/ppermute | solution.py:69
  72.0 24.5 %collective-permute-start.3 = (bf16[64,3712]{1,0:T(8,128)(2,1)S(1)}, bf16[64,3712]{1,0:T(8,128)(2,1)S(1)}, u32[]{:S(2)}, u32[]{:S(2)}) collective-permute-start(bf16[64,3712]{1,0:T(8,128)(2,1)S(1)} %collective-permute-done.2.refs_2_), channel_id=1, source_target_pairs={{0,8},{4,12},{8,0},{12,4},{16,24},{20,28},{24,16},{28,20},{1,9},{5... | collective-permute-start | bytes 1425416 | tf_op jit(solution)/shard_map/ppermute | solution.py:69
  95.3 54.5 %collective-permute-start.46 = (bf16[256,3584]{1,0:T(8,128)(2,1)}, bf16[256,3584]{1,0:T(8,128)(2,1)S(1)}, u32[]{:S(2)}, u32[]{:S(2)}) collective-permute-start(bf16[256,3584]{1,0:T(8,128)(2,1)} %get-tuple-element.20), channel_id=1, source_target_pairs={{0,4},{4,0},{8,12},{12,8},{16,20},{20,16},{24,28},{28,24},{1,5},{5... | collective-permute-start | bytes 5505032 | tf_op jit(solution)/shard_map/ppermute | solution.py:69
  99.4 30.3 %collective-permute-start.18 = (bf16[64,3712]{1,0:T(8,128)(2,1)S(1)}, bf16[64,3712]{1,0:T(8,128)(2,1)S(1)}, u32[]{:S(2)}, u32[]{:S(2)}) collective-permute-start(bf16[64,3712]{1,0:T(8,128)(2,1)S(1)} %collective-permute-done.14.refs_1_), channel_id=1, source_target_pairs={{0,4},{4,0},{8,12},{12,8},{16,20},{20,16},{24,28},{28,24},{1,5},{5... | collective-permute-start | bytes 1425416 | tf_op jit(solution)/shard_map/ppermute | solution.py:69
  100.2 29.6 %collective-permute-start.19 = (bf16[64,3712]{1,0:T(8,128)(2,1)S(1)}, bf16[64,3712]{1,0:T(8,128)(2,1)S(1)}, u32[]{:S(2)}, u32[]{:S(2)}) collective-permute-start(bf16[64,3712]{1,0:T(8,128)(2,1)S(1)} %collective-permute-done.15.refs_2_), channel_id=1, source_target_pairs={{0,4},{4,0},{8,12},{12,8},{16,20},{20,16},{24,28},{28,24},{1,5},{5... | collective-permute-start | bytes 1425416 | tf_op jit(solution)/shard_map/ppermute | solution.py:69
  109.2 21.2 %collective-permute-start.29 = (bf16[64,3712]{1,0:T(8,128)(2,1)S(1)}, bf16[64,3712]{1,0:T(8,128)(2,1)S(1)}, u32[]{:S(2)}, u32[]{:S(2)}) collective-permute-start(bf16[64,3712]{1,0:T(8,128)(2,1)S(1)} %collective-permute-done.28.refs_2_), channel_id=1, source_target_pairs={{0,8},{4,12},{8,0},{12,4},{16,24},{20,28},{24,16},{28,20},{1,9},{5... | collective-permute-start | bytes 1425416 | tf_op jit(solution)/shard_map/ppermute | solution.py:69
  149.8 24.3 %collective-permute-start.8 = (bf16[256,3584]{1,0:T(8,128)(2,1)}, bf16[256,3584]{1,0:T(8,128)(2,1)}, u32[]{:S(2)}, u32[]{:S(2)}) collective-permute-start(bf16[256,3584]{1,0:T(8,128)(2,1)} %get-tuple-element.14), channel_id=1, source_target_pairs={{0,4},{4,0},{8,12},{12,8},{16,20},{20,16},{24,28},{28,24},{1,5},{5... | collective-permute-start | bytes 5505032 | tf_op jit(solution)/shard_map/ppermute | solution.py:69
  150.4 26.6 %collective-permute-start.21 = (bf16[256,3584]{1,0:T(8,128)(2,1)}, bf16[256,3584]{1,0:T(8,128)(2,1)S(1)}, u32[]{:S(2)}, u32[]{:S(2)}) collective-permute-start(bf16[256,3584]{1,0:T(8,128)(2,1)} %get-tuple-element.16), channel_id=1, source_target_pairs={{0,4},{4,0},{8,12},{12,8},{16,20},{20,16},{24,28},{28,24},{1,5},{5... | collective-permute-start | bytes 5505032 | tf_op jit(solution)/shard_map/ppermute | solution.py:69
  150.6 20.9 %collective-permute-start.47 = (bf16[64,3584]{1,0:T(8,128)(2,1)S(1)}, bf16[64,3584]{1,0:T(8,128)(2,1)S(1)}, u32[]{:S(2)}, u32[]{:S(2)}) collective-permute-start(bf16[64,3584]{1,0:T(8,128)(2,1)S(1)} %add_convert_fusion.3), channel_id=1, source_target_pairs={{0,16},{4,20},{8,24},{12,28},{16,0},{20,4},{24,8},{28,12},{1,17},{... | collective-permute-start | bytes 1376264 | tf_op jit(solution)/shard_map/ppermute | solution.py:69
  171.8 76.5 %collective-permute-start.48 = (bf16[64,3584]{1,0:T(8,128)(2,1)S(1)}, bf16[64,3584]{1,0:T(8,128)(2,1)S(1)}, u32[]{:S(2)}, u32[]{:S(2)}) collective-permute-start(bf16[64,3584]{1,0:T(8,128)(2,1)S(1)} %get-tuple-element.27), channel_id=1, source_target_pairs={{0,8},{4,12},{8,0},{12,4},{16,24},{20,28},{24,16},{28,20},{1,9},{5... | collective-permute-start | bytes 1376264 | tf_op jit(solution)/shard_map/ppermute | solution.py:69
  172.6 75.6 %collective-permute-start.49 = (bf16[64,3584]{1,0:T(8,128)(2,1)S(1)}, bf16[64,3584]{1,0:T(8,128)(2,1)S(1)}, u32[]{:S(2)}, u32[]{:S(2)}) collective-permute-start(bf16[64,3584]{1,0:T(8,128)(2,1)S(1)} %get-tuple-element.28), channel_id=1, source_target_pairs={{0,16},{4,20},{8,24},{12,28},{16,0},{20,4},{24,8},{28,12},{1,17},{... | collective-permute-start | bytes 1376264 | tf_op jit(solution)/shard_map/ppermute | solution.py:69
  175.7 20.8 %collective-permute-start.10 = (bf16[64,3584]{1,0:T(8,128)(2,1)S(1)}, bf16[64,3584]{1,0:T(8,128)(2,1)S(1)}, u32[]{:S(2)}, u32[]{:S(2)}) collective-permute-start(bf16[64,3584]{1,0:T(8,128)(2,1)S(1)} %get-tuple-element.22), channel_id=1, source_target_pairs={{0,8},{4,12},{8,0},{12,4},{16,24},{20,28},{24,16},{28,20},{1,9},{5... | collective-permute-start | bytes 1376264 | tf_op jit(solution)/shard_map/ppermute | solution.py:69
  177.0 39.4 %collective-permute-start.9 = (bf16[64,3584]{1,0:T(8,128)(2,1)S(1)}, bf16[64,3584]{1,0:T(8,128)(2,1)S(1)}, u32[]{:S(2)}, u32[]{:S(2)}) collective-permute-start(bf16[64,3584]{1,0:T(8,128)(2,1)S(1)} %get-tuple-element.21), channel_id=1, source_target_pairs={{0,8},{4,12},{8,0},{12,4},{16,24},{20,28},{24,16},{28,20},{1,9},{5... | collective-permute-start | bytes 1376264 | tf_op jit(solution)/shard_map/ppermute | solution.py:69
  196.5 40.9 %collective-permute-start.35 = (bf16[64,3584]{1,0:T(8,128)(2,1)S(1)}, bf16[64,3584]{1,0:T(8,128)(2,1)S(1)}, u32[]{:S(2)}, u32[]{:S(2)}) collective-permute-start(bf16[64,3584]{1,0:T(8,128)(2,1)S(1)} %get-tuple-element.25), channel_id=1, source_target_pairs={{0,8},{4,12},{8,0},{12,4},{16,24},{20,28},{24,16},{28,20},{1,9},{5... | collective-permute-start | bytes 1376264 | tf_op jit(solution)/shard_map/ppermute | solution.py:69
  237.4 32.4 %collective-permute-start.25 = (bf16[64,3584]{1,0:T(8,128)(2,1)S(1)}, bf16[64,3584]{1,0:T(8,128)(2,1)S(1)}, u32[]{:S(2)}, u32[]{:S(2)}) collective-permute-start(bf16[64,3584]{1,0:T(8,128)(2,1)S(1)} %add_convert_fusion.8), channel_id=1, source_target_pairs={{0,2},{1,3},{2,0},{3,1},{4,6},{5,7},{6,4},{7,5},{8,10},{9,11},{10,... | collective-permute-start | bytes 1376264 | tf_op jit(solution)/shard_map/ppermute | solution.py:69
  246.6 31.4 %collective-permute-start.38 = (bf16[64,3584]{1,0:T(8,128)(2,1)S(1)}, bf16[64,3584]{1,0:T(8,128)(2,1)S(1)}, u32[]{:S(2)}, u32[]{:S(2)}) collective-permute-start(bf16[64,3584]{1,0:T(8,128)(2,1)S(1)} %add_convert_fusion.4), channel_id=1, source_target_pairs={{0,3},{1,2},{2,1},{3,0},{4,7},{5,6},{6,5},{7,4},{8,11},{9,10},{10,... | collective-permute-start | bytes 1376264 | tf_op jit(solution)/shard_map/ppermute | solution.py:69
  (46 other events, 536.8 us)

commit v2 on v1

--- a/solution.py
+++ b/solution.py
@@ -2,6 +2,7 @@
 
 import jax
 import jax.numpy as jnp
+import numpy as np
 from jax import lax
 from jax.experimental import pallas as pl
 from jax.experimental.pallas import tpu as pltpu
@@ -76,24 +77,37 @@
     return [own, right, down, across]
 
 
-def reduce_plane(mine, other, turn):
-    rows = mine.shape[0] // 4
-    f32 = jnp.float32
-    got = swap(other, "ex", PAIR)
-
-    def pair_sum(piece):
-        low = piece * rows
-        return mine[low : low + rows].astype(f32) + got[low : low + rows].astype(f32)
-
-    across = swap(pair_sum(3).astype(jnp.bfloat16), "ex", RIGHT if turn else DOWN).astype(f32)
-    right, down = pair_sum(1), pair_sum(2)
-    if turn:
-        down = down + across
-    else:
-        right = right + across
-    got_right = swap(right.astype(jnp.bfloat16), "ex", RIGHT)
-    got_down = swap(down.astype(jnp.bfloat16), "ex", DOWN)
-    return pair_sum(0) + got_right.astype(f32) + got_down.astype(f32)
+def add_body(jobs, *refs):
+    outs = refs[len(refs) - len(jobs) :]
+    at = 0
+    for out, job in zip(outs, jobs):
+        total = refs[at][...].astype(jnp.float32)
+        for k in range(1, job):
+            total += refs[at + k][...].astype(jnp.float32)
+        out[...] = total.astype(out.dtype)
+        at += job
+
+
+def add_rows(rows, jobs):
+    width = jobs[0][0][0].shape[1]
+    steps = 2
+    span = width // steps
+
+    def spec(block):
+        return pl.BlockSpec((rows, span), lambda j: (block, j))
+
+    return pl.pallas_call(
+        functools.partial(add_body, tuple(len(job) for job in jobs)),
+        grid=(steps,),
+        out_shape=[jax.ShapeDtypeStruct((rows, width), jnp.bfloat16)] * len(jobs),
+        in_specs=[spec(block) for job in jobs for _, block in job],
+        out_specs=[spec(0)] * len(jobs),
+        cost_estimate=pl.CostEstimate(
+            flops=sum(map(len, jobs)) * rows * width,
+            bytes_accessed=2 * (sum(map(len, jobs)) + len(jobs)) * rows * width,
+            transcendentals=0,
+        ),
+    )(*[array for job in jobs for array, _ in job])
 
 
 LANES = 128
@@ -103,7 +117,7 @@
     return max(t for t in range(LANES, goal + 1, LANES) if size % t == 0)
 
 
-def expert_body(dims, *refs):
+def expert_body(dims, trailing, *refs):
     count, block, most, width, hidden, shared_hidden, tile, span = dims
     rows, slots = count * block, count * most
     refs = list(refs)
@@ -114,8 +128,10 @@
         return out
 
     pieces = take(2 * count)
+    (before_ref,) = take(1)
     w_gate, w_up, w_down = take(3)
     shared = take(3) if shared_hidden else None
+    take(len(refs) - trailing)
     outs = take(2)
     held, chosen, gate, up, down, act, back, result = take(8)
     if shared:
@@ -152,24 +168,23 @@
     if shared:
         shared_copy(0).start()
         shared_copy(1).start()
-    for k in range(steps):
-        gate_copy(k).start()
-        up_copy(k).start()
-    if shared:
-        shared_copy(2).start()
-    for k in range(spans):
-        down_copy(k).start()
 
     me = lax.axis_index("ex") * lax.axis_size("ey") + lax.axis_index("ey")
     pick = (lax.broadcasted_iota(jnp.int32, (16, LANES), 1) == me).astype(f32).astype(bf16)
-    early = lax.broadcasted_iota(jnp.int32, (rows, rows), 0)
-    late = lax.broadcasted_iota(jnp.int32, (rows, rows), 1)
-    before = ((early < late) & (early // block == late // block)).astype(f32).astype(bf16)
-    base = (lax.broadcasted_iota(jnp.int32, (1, rows), 1) // block * most).astype(f32)
+    before = before_ref[:rows]
+    base = before_ref[rows : rows + 16].astype(f32)[0:1]
     slot = lax.broadcasted_iota(jnp.int32, (slots, rows), 0).astype(f32)
     for side in range(2):
         for k in range(side * count, (side + 1) * count):
             piece_copy(k).wait()
+        if side == 1:
+            for k in range(steps):
+                gate_copy(k).start()
+                up_copy(k).start()
+            if shared:
+                shared_copy(2).start()
+            for k in range(spans):
+                down_copy(k).start()
         low = side * rows
         table = held[low : low + rows, width : width + LANES]
         rate = lax.dot_general(
@@ -182,12 +197,9 @@
         back[side] = jnp.where(place, rate[0:1], 0.0).T.astype(bf16)
         onehot = place.astype(f32).astype(bf16)
 
-        @pl.loop(0, spans)
-        def _(k):
-            columns = pl.ds(pl.multiple_of(k * span, span), span)
-            chosen[side * slots : (side + 1) * slots, columns] = jnp.dot(
-                onehot, held[low : low + rows, columns], preferred_element_type=f32
-            ).astype(bf16)
+        chosen[side * slots : (side + 1) * slots] = jnp.dot(
+            onehot, held[low : low + rows, :width], preferred_element_type=f32
+        ).astype(bf16)
 
     if shared:
         shared_copy(0).wait()
@@ -230,7 +242,7 @@
         out_copy(1, k).wait()
 
 
-def run_expert(mine, other, most, weights, shared):
+def run_expert(mine, other, most, weights, shared, after=()):
     count, (block, wide) = len(mine), mine[0].shape
     width, hidden = wide - LANES, weights[0].shape[2]
     shared_hidden = shared[0].shape[1] if shared else 0
@@ -261,14 +273,20 @@
     ]
     if shared:
         scratch += [sems((3,))]
-    operands = [*mine, *other, *weights, *(shared or ())]
+    token = np.arange(rows)
+    before = (token[:, None] < token) & (token[:, None] // block == token // block)
+    base = np.broadcast_to(token // block * most, (16, rows))
+    before = jnp.asarray(np.concatenate([before, base], axis=0), bf16)
+    operands = [*mine, *other, before, *weights, *(shared or ()), *after]
     flops = 2 * (6 * slots * width * hidden + 4 * rows * slots * width)
     flops += 2 * 6 * rows * width * shared_hidden
-    moved = 2 * (sum(part.size for part in operands) + 2 * rows * width)
+    moved = 2 * (sum(part.size for part in operands[: len(operands) - len(after)]) + 2 * rows * width)
     return pl.pallas_call(
-        functools.partial(expert_body, dims),
+        functools.partial(expert_body, dims, len(scratch) + 2),
         out_shape=[jax.ShapeDtypeStruct((rows, width), bf16)] * 2,
-        in_specs=[pl.BlockSpec(memory_space=pl.ANY)] * len(operands),
+        in_specs=[
+            pl.BlockSpec(memory_space=pltpu.VMEM if part is before else pl.ANY) for part in operands
+        ],
         out_specs=[pl.BlockSpec(memory_space=pl.ANY)] * 2,
         scratch_shapes=scratch,
         compiler_params=pltpu.CompilerParams(vmem_limit_bytes=52 * 1024 * 1024),
@@ -287,21 +305,53 @@
     table = jnp.sum(jnp.where(hit, route_weight[:, :, None], 0).astype(jnp.float32), axis=1)
     own = jnp.concatenate([tokens, table.astype(tokens.dtype)], axis=1)
     columns = [own] + [swap(own, "ey", mask) for mask in range(1, planes)]
-    order = list(range(1, planes)) + [0]
-    sums = []
-    for mask in order:
-        mine = gather_plane(columns[mask], mask % 2)
-        other = [swap(piece, "ex", PAIR) for piece in mine]
-        shared = None if mask else (shared_gate, shared_up, shared_down)
-        mine, other = run_expert(mine, other, most, (w_gate, w_up, w_down), shared)
-        part = reduce_plane(mine, other, mask % 2)
-        if mask:
-            part = swap(part.astype(jnp.bfloat16), "ey", mask).astype(jnp.float32)
-        sums.append(part)
-    total = sums[0]
-    for part in sums[1:]:
-        total = total + part
-    return total.astype(jnp.bfloat16)
+    order = [0] + list(range(2, planes)) + [1]
+    last = len(order) - 1
+    pieces = [gather_plane(columns[mask], turn % 2) for turn, mask in enumerate(order)]
+    mine, got, across, plain, full, parts = {}, {}, {}, {}, {}, {}
+
+    def job_across(k):
+        return [(mine[k], 3), (got[k], 3)]
+
+    def job_plain(k):
+        piece = 1 if k % 2 else 2
+        return [(mine[k], piece), (got[k], piece)]
+
+    def job_full(k):
+        piece = 2 if k % 2 else 1
+        return [(mine[k], piece), (got[k], piece), (across[k], 0)]
+
+    def job_part(k):
+        return [(mine[k], 0), (got[k], 0), (plain[k], 0), (full[k], 0)]
+
+    after = ()
+    for k in range(len(order) + 2):
+        jobs, sends = [], []
+        if k <= last:
+            own_pieces = pieces[k]
+            other = [swap(piece, "ex", PAIR) for piece in own_pieces]
+            shared = (shared_gate, shared_up, shared_down) if order[k] == 0 else None
+            mine[k], theirs = run_expert(
+                own_pieces, other, most, (w_gate, w_up, w_down), shared, after
+            )
+            got[k] = swap(theirs, "ex", PAIR)
+            jobs += [job_across(k), job_plain(k)]
+            sends += [
+                (across, k, "ex", RIGHT if k % 2 else DOWN),
+                (plain, k, "ex", RIGHT if k % 2 else DOWN),
+            ]
+        if 0 <= k - 1 <= last:
+            jobs.append(job_full(k - 1))
+            sends.append((full, k - 1, "ex", DOWN if (k - 1) % 2 else RIGHT))
+        if 0 < k - 2 <= last:
+            jobs.append(job_part(k - 2))
+            sends.append((parts, k - 2, "ey", order[k - 2]))
+        summed = add_rows(block, jobs)
+        after = (summed[0],)
+        for value, (store, phase, axis, mask) in zip(summed, sends):
+            store[phase] = swap(value, axis, mask)
+    jobs = [job_part(0) + [(parts[k], 0) for k in range(1, len(order))]]
+    return add_rows(block, jobs)[0]
 
 
 def solution(mesh):

time: 280 us -> 316 us (1.13)
  waiting for transfers between devices: 148 us -> 170 us
  local copies, waits for them, and re-layouts: 4.53 us -> 17.8 us
  Pallas kernels: 78.1 us -> 85.2 us
  other arithmetic: 7.96 us -> 1.27 us
    ppermute x50, waiting for transfers between devices: 148 us -> 170 us  [swap(): return lax.ppermute(value, axis, [(i, i ^ mask) for i in range(size)])]
    unnamed x42 -> x80, local copies, waits for them, and re-layouts: 4.53 us -> 17.8 us
    pallas_call x4 -> x11, Pallas kernels: 78.1 us -> 85.2 us  [the longest x4 64.7 us: run_expert(): pl.pallas_call(functools.partial(expert_body, dims, len(scratch) + 2), ou...]
    convert_element_type x12 -> x0, other arithmetic: 6.69 us -> none  [the longest x4 2.25 us: reduce_plane(): got_right = swap(right.astype(jnp.bfloat16), 'ex', RIGHT)]
  transfers between devices with their start and end apart: 50 -> 50, of which waited for: 17 -> 23; matrix products, arithmetic and copies ran while one was open for 2% -> 0% of each run, Pallas kernels for 28% -> 21%
where the time goes in v2:
time: 316 us
  waiting for transfers between devices  170 us (54%)
  Pallas kernels  85.2 us (27%)
  starting transfers between devices  41 us (13%)
  local copies, waits for them, and re-layouts  17.8 us (6%)
    ppermute x50, waiting for transfers between devices, swap(): return lax.ppermute(value, axis, [(i, i ^ mask) for i in range(size)])  170 us
    pallas_call x4, Pallas kernels, run_expert(): pl.pallas_call(functools.partial(expert_body, dims, len(scratch) + 2), ou...  64.7 us
    ppermute x50, starting transfers between devices, swap(): return lax.ppermute(value, axis, [(i, i ^ mask) for i in range(size)])  41 us
    pallas_call x7, Pallas kernels, add_rows(): pl.pallas_call(functools.partial(add_body, tuple((len(job) for job in job...  20.5 us
    unnamed x80, local copies, waits for them, and re-layouts  17.8 us
  transfers between devices with their start and end apart: 50, of which 23 were waited for; matrix products, arithmetic and copies ran while one was open for 0% of the time, Pallas kernels for 21%

profile of v2, /device:TPU:8, one launch (start us, length us, event | category | flops | bytes accessed | tf_op | source)
XLA Modules:
  0.0 315.9 jit_solution(14208502914730453929)
XLA Ops:
  5.9 9.6 %collective-permute-done.refs_1_ = bf16[64,3712]{1,0:T(8,128)(2,1)S(1)} collective-permute-done((bf16[64,3712]{1,0:T(8,128)(2,1)S(1)}, bf16[64,3712]{1,0:T(8,128)(2,1)S(1)}, u32[]{:S(2)}, u32[]{:S(2)}) %collective-permute-start) | collective-permute-done | bytes 475168 | tf_op jit(solution)/shard_map/ppermute | solution.py:70
  17.5 9.7 %collective-permute-done.2.refs_3_ = bf16[64,3712]{1,0:T(8,128)(2,1)S(1)} collective-permute-done((bf16[64,3712]{1,0:T(8,128)(2,1)S(1)}, bf16[64,3712]{1,0:T(8,128)(2,1)S(1)}, u32[]{:S(2)}, u32[]{:S(2)}) %collective-permute-start.2) | collective-permute-done | bytes 475168 | tf_op jit(solution)/shard_map/ppermute | solution.py:70
  32.6 17.2 %shard_map.127 = (bf16[256,3584]{1,0:T(8,128)(2,1)}, bf16[256,3584]{1,0:T(8,128)(2,1)}) custom-call(bf16[64,3712]{1,0:T(8,128)(2,1)S(1)} %pad_maximum_fusion.refs_0_, bf16[64,3712]{1,0:T(8,128)(2,1)S(1)} %collective-permute-done.refs_1_, bf16[64,3712]{1,0:T(8,128)(2,1)S(1)} %collective-permute-done.1.refs_2_, bf16[64,3712]{1,0:T(8,128)(2,1)} %copy-done.31, ...), custom_call_target="tpu_custom_call" | custom-call | flops 9395240960 | bytes 35135488 | tf_op jit(solution)/shard_map/pallas_call | solution.py:284
  53.7 9.8 %collective-permute-done.11.refs_2_ = bf16[64,3712]{1,0:T(8,128)(2,1)S(1)} collective-permute-done((bf16[64,3712]{1,0:T(8,128)(2,1)S(1)}, bf16[64,3712]{1,0:T(8,128)(2,1)S(1)}, u32[]{:S(2)}, u32[]{:S(2)}) %collective-permute-start.11) | collective-permute-done | bytes 475168 | tf_op jit(solution)/shard_map/ppermute | solution.py:70
  65.6 10.0 %collective-permute-done.12.refs_3_ = bf16[64,3712]{1,0:T(8,128)(2,1)S(1)} collective-permute-done((bf16[64,3712]{1,0:T(8,128)(2,1)S(1)}, bf16[64,3712]{1,0:T(8,128)(2,1)S(1)}, u32[]{:S(2)}, u32[]{:S(2)}) %collective-permute-start.12) | collective-permute-done | bytes 475168 | tf_op jit(solution)/shard_map/ppermute | solution.py:70
  81.1 15.8 %shard_map.129 = (bf16[256,3584]{1,0:T(8,128)(2,1)}, bf16[256,3584]{1,0:T(8,128)(2,1)}) custom-call(bf16[64,3712]{1,0:T(8,128)(2,1)S(1)} %collective-permute-done.9.refs_0_, bf16[64,3712]{1,0:T(8,128)(2,1)S(1)} %collective-permute-done.10.refs_1_, bf16[64,3712]{1,0:T(8,128)(2,1)S(1)} %collective-permute-done.11.refs_2_, bf16[64,3712]{1,0:T(8,128)(2,1)} %copy-done.11, ...), custom_call_target="tpu_custom_call" | custom-call | flops 6576668672 | bytes 29630464 | tf_op jit(solution)/shard_map/pallas_call | solution.py:284
  102.0 9.4 %collective-permute-done.29.refs_1_ = bf16[64,3712]{1,0:T(8,128)(2,1)S(1)} collective-permute-done((bf16[64,3712]{1,0:T(8,128)(2,1)S(1)}, bf16[64,3712]{1,0:T(8,128)(2,1)S(1)}, u32[]{:S(2)}, u32[]{:S(2)}) %collective-permute-start.29) | collective-permute-done | bytes 475168 | tf_op jit(solution)/shard_map/ppermute | solution.py:70
  114.0 11.3 %collective-permute-done.31.refs_3_ = bf16[64,3712]{1,0:T(8,128)(2,1)S(1)} collective-permute-done((bf16[64,3712]{1,0:T(8,128)(2,1)S(1)}, bf16[64,3712]{1,0:T(8,128)(2,1)S(1)}, u32[]{:S(2)}, u32[]{:S(2)}) %collective-permute-start.31) | collective-permute-done | bytes 475168 | tf_op jit(solution)/shard_map/ppermute | solution.py:70
  125.3 7.6 %collective-permute-done.18.refs_6_ = bf16[64,3584]{1,0:T(8,128)(2,1)S(1)} collective-permute-done((bf16[64,3584]{1,0:T(8,128)(2,1)S(1)}, bf16[64,3584]{1,0:T(8,128)(2,1)S(1)}, u32[]{:S(2)}, u32[]{:S(2)}) %collective-permute-start.18) | collective-permute-done | bytes 458784 | tf_op jit(solution)/shard_map/ppermute | solution.py:70
  133.6 3.2 %collective-permute-start.20 = (bf16[64,3712]{1,0:T(8,128)(2,1)S(1)}, bf16[64,3712]{1,0:T(8,128)(2,1)S(1)}, u32[]{:S(2)}, u32[]{:S(2)}) collective-permute-start(bf16[64,3712]{1,0:T(8,128)(2,1)S(1)} %pad_maximum_fusion.refs_0_), channel_id=1, source_target_pairs={{0,1},{1,0},{2,3},{3,2},{4,5},{5,4},{6,7},{7,6},{8,9},{9,8},{10,11... | collective-permute-start | bytes 1425416 | tf_op jit(solution)/shard_map/ppermute | solution.py:70
  141.7 15.8 %shard_map.131 = (bf16[256,3584]{1,0:T(8,128)(2,1)}, bf16[256,3584]{1,0:T(8,128)(2,1)}) custom-call(bf16[64,3712]{1,0:T(8,128)(2,1)S(1)} %collective-permute-done.28.refs_0_, bf16[64,3712]{1,0:T(8,128)(2,1)S(1)} %collective-permute-done.29.refs_1_, bf16[64,3712]{1,0:T(8,128)(2,1)S(1)} %collective-permute-done.30.refs_2_, bf16[64,3712]{1,0:T(8,128)(2,1)} %copy-done.8, ...), custom_call_target="tpu_custom_call" | custom-call | flops 6576668672 | bytes 29630464 | tf_op jit(solution)/shard_map/pallas_call | solution.py:284
  160.7 10.2 %collective-permute-done.22.refs_2_ = bf16[64,3712]{1,0:T(8,128)(2,1)S(1)} collective-permute-done((bf16[64,3712]{1,0:T(8,128)(2,1)S(1)}, bf16[64,3712]{1,0:T(8,128)(2,1)S(1)}, u32[]{:S(2)}, u32[]{:S(2)}) %collective-permute-start.22) | collective-permute-done | bytes 475168 | tf_op jit(solution)/shard_map/ppermute | solution.py:70
  173.4 11.2 %collective-permute-done.23.refs_3_ = bf16[64,3712]{1,0:T(8,128)(2,1)S(1)} collective-permute-done((bf16[64,3712]{1,0:T(8,128)(2,1)S(1)}, bf16[64,3712]{1,0:T(8,128)(2,1)S(1)}, u32[]{:S(2)}, u32[]{:S(2)}) %collective-permute-start.23) | collective-permute-done | bytes 475168 | tf_op jit(solution)/shard_map/ppermute | solution.py:70
  184.7 8.5 %collective-permute-done.37.refs_6_ = bf16[64,3584]{1,0:T(8,128)(2,1)S(1)} collective-permute-done((bf16[64,3584]{1,0:T(8,128)(2,1)S(1)}, bf16[64,3584]{1,0:T(8,128)(2,1)S(1)}, u32[]{:S(2)}, u32[]{:S(2)}) %collective-permute-start.37) | collective-permute-done | bytes 458784 | tf_op jit(solution)/shard_map/ppermute | solution.py:70
  193.9 3.2 %shard_map.132 = (bf16[64,3584]{1,0:T(8,128)(2,1)}, bf16[64,3584]{1,0:T(8,128)(2,1)}, bf16[64,3584]{1,0:T(8,128)(2,1)}) custom-call(bf16[256,3584]{1,0:T(8,128)(2,1)} %get-tuple-element.35.refs_0_.refs_2_.refs_4_.refs_3_, bf16[256,3584]{1,0:T(8,128)(2,1)} %collective-permute-done.36.refs_1_.refs_3_.refs_5_.refs_4_, ...), custom_call_target="tpu_custom_call" | custom-call | flops 1605632 | bytes 4587520 | tf_op jit(solution)/shard_map/pallas_call | solution.py:99
  199.3 15.8 %shard_map.133 = (bf16[256,3584]{1,0:T(8,128)(2,1)}, bf16[256,3584]{1,0:T(8,128)(2,1)}) custom-call(bf16[64,3712]{1,0:T(8,128)(2,1)S(1)} %collective-permute-done.20.refs_0_, bf16[64,3712]{1,0:T(8,128)(2,1)S(1)} %collective-permute-done.21.refs_1_, bf16[64,3712]{1,0:T(8,128)(2,1)S(1)} %collective-permute-done.22.refs_2_, bf16[64,3712]{1,0:T(8,128)(2,1)} %copy-done.9, ...), custom_call_target="tpu_custom_call" | custom-call | flops 6576668672 | bytes 29630464 | tf_op jit(solution)/shard_map/pallas_call | solution.py:284
  220.7 7.5 %collective-permute-done.40.refs_9_ = bf16[64,3584]{1,0:T(8,128)(2,1)S(1)} collective-permute-done((bf16[64,3584]{1,0:T(8,128)(2,1)S(1)}, bf16[64,3584]{1,0:T(8,128)(2,1)S(1)}, u32[]{:S(2)}, u32[]{:S(2)}) %collective-permute-start.40) | collective-permute-done | bytes 458784 | tf_op jit(solution)/shard_map/ppermute | solution.py:70
  230.6 9.8 %collective-permute-done.39.refs_6_ = bf16[64,3584]{1,0:T(8,128)(2,1)S(1)} collective-permute-done((bf16[64,3584]{1,0:T(8,128)(2,1)S(1)}, bf16[64,3584]{1,0:T(8,128)(2,1)S(1)}, u32[]{:S(2)}, u32[]{:S(2)}) %collective-permute-start.39) | collective-permute-done | bytes 458784 | tf_op jit(solution)/shard_map/ppermute | solution.py:70
  242.4 3.7 %shard_map.134 = (bf16[64,3584]{1,0:T(8,128)(2,1)}, bf16[64,3584]{1,0:T(8,128)(2,1)}, bf16[64,3584]{1,0:T(8,128)(2,1)}, bf16[64,3584]{1,0:T(8,128)(2,1)}) custom-call(bf16[256,3584]{1,0:T(8,128)(2,1)} %get-tuple-element.38.refs_0_.refs_2_, bf16[256,3584]{1,0:T(8,128)(2,1)} %copy-done.6, bf16[256,3584]{1,0:T(8,128)(2,1)} %get-tuple-element.38.refs_0_.refs_2_, ...), custom_call_target="tpu_custom_call" | custom-call | flops 2523136 | bytes 6881280 | tf_op jit(solution)/shard_map/pallas_call | solution.py:99
  249.0 10.8 %collective-permute-done.43.refs_2_ = bf16[64,3584]{1,0:T(8,128)(2,1)S(1)} collective-permute-done((bf16[64,3584]{1,0:T(8,128)(2,1)}, bf16[64,3584]{1,0:T(8,128)(2,1)S(1)}, u32[]{:S(2)}, u32[]{:S(2)}) %collective-permute-start.43) | collective-permute-done | bytes 458784 | tf_op jit(solution)/shard_map/ppermute | solution.py:70
  259.9 9.8 %collective-permute-done.45.refs_6_ = bf16[64,3584]{1,0:T(8,128)(2,1)S(1)} collective-permute-done((bf16[64,3584]{1,0:T(8,128)(2,1)}, bf16[64,3584]{1,0:T(8,128)(2,1)S(1)}, u32[]{:S(2)}, u32[]{:S(2)}) %collective-permute-start.45) | collective-permute-done | bytes 458784 | tf_op jit(solution)/shard_map/ppermute | solution.py:70
  279.6 4.8 %collective-permute-done.48.refs_3_ = bf16[64,3584]{1,0:T(8,128)(2,1)S(1)} collective-permute-done((bf16[64,3584]{1,0:T(8,128)(2,1)}, bf16[64,3584]{1,0:T(8,128)(2,1)S(1)}, u32[]{:S(2)}, u32[]{:S(2)}) %collective-permute-start.48) | collective-permute-done | bytes 458784 | tf_op jit(solution)/shard_map/ppermute | solution.py:70
  289.4 10.5 %collective-permute-done.42.refs_4_ = bf16[64,3584]{1,0:T(8,128)(2,1)S(1)} collective-permute-done((bf16[64,3584]{1,0:T(8,128)(2,1)}, bf16[64,3584]{1,0:T(8,128)(2,1)S(1)}, u32[]{:S(2)}, u32[]{:S(2)}) %collective-permute-start.42) | collective-permute-done | bytes 458784 | tf_op jit(solution)/shard_map/ppermute | solution.py:70
  299.9 11.6 %collective-permute-done.46.refs_5_ = bf16[64,3584]{1,0:T(8,128)(2,1)S(1)} collective-permute-done((bf16[64,3584]{1,0:T(8,128)(2,1)}, bf16[64,3584]{1,0:T(8,128)(2,1)S(1)}, u32[]{:S(2)}, u32[]{:S(2)}) %collective-permute-start.46) | collective-permute-done | bytes 458784 | tf_op jit(solution)/shard_map/ppermute | solution.py:70
  (169 shorter events, 78.6 us)
Async XLA Ops:
  27.2 23.5 %collective-permute-start.9 = (bf16[64,3712]{1,0:T(8,128)(2,1)S(1)}, bf16[64,3712]{1,0:T(8,128)(2,1)S(1)}, u32[]{:S(2)}, u32[]{:S(2)}) collective-permute-start(bf16[64,3712]{1,0:T(8,128)(2,1)S(1)} %pad_maximum_fusion.refs_0_), channel_id=1, source_target_pairs={{0,2},{1,3},{2,0},{3,1},{4,6},{5,7},{6,4},{7,5},{8,10},{9,11},{10,... | collective-permute-start | bytes 1425416 | tf_op jit(solution)/shard_map/ppermute | solution.py:70
  49.9 25.7 %collective-permute-start.7 = (bf16[256,3584]{1,0:T(8,128)(2,1)}, bf16[256,3584]{1,0:T(8,128)(2,1)S(1)}, u32[]{:S(2)}, u32[]{:S(2)}) collective-permute-start(bf16[256,3584]{1,0:T(8,128)(2,1)} %get-tuple-element.28), channel_id=1, source_target_pairs={{0,4},{4,0},{8,12},{12,8},{16,20},{20,16},{24,28},{28,24},{1,5},{5... | collective-permute-start | bytes 5505032 | tf_op jit(solution)/shard_map/ppermute | solution.py:70
  65.0 14.3 %collective-permute-start.13 = (bf16[64,3712]{1,0:T(8,128)(2,1)S(1)}, bf16[64,3712]{1,0:T(8,128)(2,1)S(1)}, u32[]{:S(2)}, u32[]{:S(2)}) collective-permute-start(bf16[64,3712]{1,0:T(8,128)(2,1)S(1)} %collective-permute-done.9.refs_0_), channel_id=1, source_target_pairs={{0,4},{4,0},{8,12},{12,8},{16,20},{20,16},{24,28},{28,24},{1,5},{5... | collective-permute-start | bytes 1425416 | tf_op jit(solution)/shard_map/ppermute | solution.py:70
  65.0 14.3 %collective-permute-start.15 = (bf16[64,3712]{1,0:T(8,128)(2,1)S(1)}, bf16[64,3712]{1,0:T(8,128)(2,1)}, u32[]{:S(2)}, u32[]{:S(2)}) collective-permute-start(bf16[64,3712]{1,0:T(8,128)(2,1)S(1)} %collective-permute-done.11.refs_2_), channel_id=1, source_target_pairs={{0,4},{4,0},{8,12},{12,8},{16,20},{20,16},{24,28},{28,24},{1,5},{5... | collective-permute-start | bytes 1425416 | tf_op jit(solution)/shard_map/ppermute | solution.py:70
  75.6 23.5 %collective-permute-start.28 = (bf16[64,3712]{1,0:T(8,128)(2,1)S(1)}, bf16[64,3712]{1,0:T(8,128)(2,1)S(1)}, u32[]{:S(2)}, u32[]{:S(2)}) collective-permute-start(bf16[64,3712]{1,0:T(8,128)(2,1)S(1)} %pad_maximum_fusion.refs_0_), channel_id=1, source_target_pairs={{0,3},{1,2},{2,1},{3,0},{4,7},{5,6},{6,5},{7,4},{8,11},{9,10},{10,... | collective-permute-start | bytes 1425416 | tf_op jit(solution)/shard_map/ppermute | solution.py:70
  97.0 36.6 %collective-permute-start.17 = (bf16[256,3584]{1,0:T(8,128)(2,1)}, bf16[256,3584]{1,0:T(8,128)(2,1)S(1)}, u32[]{:S(2)}, u32[]{:S(2)}) collective-permute-start(bf16[256,3584]{1,0:T(8,128)(2,1)} %get-tuple-element.32), channel_id=1, source_target_pairs={{0,4},{4,0},{8,12},{12,8},{16,20},{20,16},{24,28},{28,24},{1,5},{5... | collective-permute-start | bytes 5505032 | tf_op jit(solution)/shard_map/ppermute | solution.py:70
  113.0 19.9 %collective-permute-start.18 = (bf16[64,3584]{1,0:T(8,128)(2,1)S(1)}, bf16[64,3584]{1,0:T(8,128)(2,1)S(1)}, u32[]{:S(2)}, u32[]{:S(2)}) collective-permute-start(bf16[64,3584]{1,0:T(8,128)(2,1)S(1)} %copy-done.3), channel_id=1, source_target_pairs={{0,16},{4,20},{8,24},{12,28},{16,0},{20,4},{24,8},{28,12},{1,17},{... | collective-permute-start | bytes 1376264 | tf_op jit(solution)/shard_map/ppermute | solution.py:70
  113.5 26.4 %collective-permute-start.32 = (bf16[64,3712]{1,0:T(8,128)(2,1)S(1)}, bf16[64,3712]{1,0:T(8,128)(2,1)S(1)}, u32[]{:S(2)}, u32[]{:S(2)}) collective-permute-start(bf16[64,3712]{1,0:T(8,128)(2,1)S(1)} %collective-permute-done.28.refs_0_), channel_id=1, source_target_pairs={{0,4},{4,0},{8,12},{12,8},{16,20},{20,16},{24,28},{28,24},{1,5},{5... | collective-permute-start | bytes 1425416 | tf_op jit(solution)/shard_map/ppermute | solution.py:70
  113.5 26.4 %collective-permute-start.33 = (bf16[64,3712]{1,0:T(8,128)(2,1)S(1)}, bf16[64,3712]{1,0:T(8,128)(2,1)}, u32[]{:S(2)}, u32[]{:S(2)}) collective-permute-start(bf16[64,3712]{1,0:T(8,128)(2,1)S(1)} %collective-permute-done.29.refs_1_), channel_id=1, source_target_pairs={{0,4},{4,0},{8,12},{12,8},{16,20},{20,16},{24,28},{28,24},{1,5},{5... | collective-permute-start | bytes 1425416 | tf_op jit(solution)/shard_map/ppermute | solution.py:70
  125.3 14.6 %collective-permute-start.34 = (bf16[64,3712]{1,0:T(8,128)(2,1)S(1)}, bf16[64,3712]{1,0:T(8,128)(2,1)}, u32[]{:S(2)}, u32[]{:S(2)}) collective-permute-start(bf16[64,3712]{1,0:T(8,128)(2,1)S(1)} %collective-permute-done.30.refs_2_), channel_id=1, source_target_pairs={{0,4},{4,0},{8,12},{12,8},{16,20},{20,16},{24,28},{28,24},{1,5},{5... | collective-permute-start | bytes 1425416 | tf_op jit(solution)/shard_map/ppermute | solution.py:70
  133.6 24.0 %collective-permute-start.20 = (bf16[64,3712]{1,0:T(8,128)(2,1)S(1)}, bf16[64,3712]{1,0:T(8,128)(2,1)S(1)}, u32[]{:S(2)}, u32[]{:S(2)}) collective-permute-start(bf16[64,3712]{1,0:T(8,128)(2,1)S(1)} %pad_maximum_fusion.refs_0_), channel_id=1, source_target_pairs={{0,1},{1,0},{2,3},{3,2},{4,5},{5,4},{6,7},{7,6},{8,9},{9,8},{10,11... | collective-permute-start | bytes 1425416 | tf_op jit(solution)/shard_map/ppermute | solution.py:70
  157.5 36.4 %collective-permute-start.36 = (bf16[256,3584]{1,0:T(8,128)(2,1)}, bf16[256,3584]{1,0:T(8,128)(2,1)}, u32[]{:S(2)}, u32[]{:S(2)}) collective-permute-start(bf16[256,3584]{1,0:T(8,128)(2,1)} %get-tuple-element.36), channel_id=1, source_target_pairs={{0,4},{4,0},{8,12},{12,8},{16,20},{20,16},{24,28},{28,24},{1,5},{5... | collective-permute-start | bytes 5505032 | tf_op jit(solution)/shard_map/ppermute | solution.py:70
  172.4 20.8 %collective-permute-start.37 = (bf16[64,3584]{1,0:T(8,128)(2,1)S(1)}, bf16[64,3584]{1,0:T(8,128)(2,1)S(1)}, u32[]{:S(2)}, u32[]{:S(2)}) collective-permute-start(bf16[64,3584]{1,0:T(8,128)(2,1)S(1)} %copy-done.2), channel_id=1, source_target_pairs={{0,8},{4,12},{8,0},{12,4},{16,24},{20,28},{24,16},{28,20},{1,9},{5... | collective-permute-start | bytes 1376264 | tf_op jit(solution)/shard_map/ppermute | solution.py:70
  172.9 24.2 %collective-permute-start.24 = (bf16[64,3712]{1,0:T(8,128)(2,1)S(1)}, bf16[64,3712]{1,0:T(8,128)(2,1)S(1)}, u32[]{:S(2)}, u32[]{:S(2)}) collective-permute-start(bf16[64,3712]{1,0:T(8,128)(2,1)S(1)} %collective-permute-done.20.refs_0_), channel_id=1, source_target_pairs={{0,4},{4,0},{8,12},{12,8},{16,20},{20,16},{24,28},{28,24},{1,5},{5... | collective-permute-start | bytes 1425416 | tf_op jit(solution)/shard_map/ppermute | solution.py:70
  172.9 24.2 %collective-permute-start.26 = (bf16[64,3712]{1,0:T(8,128)(2,1)S(1)}, bf16[64,3712]{1,0:T(8,128)(2,1)S(1)}, u32[]{:S(2)}, u32[]{:S(2)}) collective-permute-start(bf16[64,3712]{1,0:T(8,128)(2,1)S(1)} %collective-permute-done.22.refs_2_), channel_id=1, source_target_pairs={{0,4},{4,0},{8,12},{12,8},{16,20},{20,16},{24,28},{28,24},{1,5},{5... | collective-permute-start | bytes 1425416 | tf_op jit(solution)/shard_map/ppermute | solution.py:70
  215.1 25.3 %collective-permute-start.38 = (bf16[256,3584]{1,0:T(8,128)(2,1)}, bf16[256,3584]{1,0:T(8,128)(2,1)S(1)}, u32[]{:S(2)}, u32[]{:S(2)}) collective-permute-start(bf16[256,3584]{1,0:T(8,128)(2,1)} %get-tuple-element.39), channel_id=1, source_target_pairs={{0,4},{4,0},{8,12},{12,8},{16,20},{20,16},{24,28},{28,24},{1,5},{5... | collective-permute-start | bytes 5505032 | tf_op jit(solution)/shard_map/ppermute | solution.py:70
  218.7 21.7 %collective-permute-start.39 = (bf16[64,3584]{1,0:T(8,128)(2,1)S(1)}, bf16[64,3584]{1,0:T(8,128)(2,1)S(1)}, u32[]{:S(2)}, u32[]{:S(2)}) collective-permute-start(bf16[64,3584]{1,0:T(8,128)(2,1)S(1)} %copy-done.4), channel_id=1, source_target_pairs={{0,16},{4,20},{8,24},{12,28},{16,0},{20,4},{24,8},{28,12},{1,17},{... | collective-permute-start | bytes 1376264 | tf_op jit(solution)/shard_map/ppermute | solution.py:70
  219.2 29.9 %collective-permute-start.44 = (bf16[64,3584]{1,0:T(8,128)(2,1)}, bf16[64,3584]{1,0:T(8,128)(2,1)S(1)}, u32[]{:S(2)}, u32[]{:S(2)}) collective-permute-start(bf16[64,3584]{1,0:T(8,128)(2,1)} %get-tuple-element.44), channel_id=1, source_target_pairs={{0,16},{4,20},{8,24},{12,28},{16,0},{20,4},{24,8},{28,12},{1,17},{... | collective-permute-start | bytes 1376264 | tf_op jit(solution)/shard_map/ppermute | solution.py:70
  246.8 23.0 %collective-permute-start.45 = (bf16[64,3584]{1,0:T(8,128)(2,1)}, bf16[64,3584]{1,0:T(8,128)(2,1)S(1)}, u32[]{:S(2)}, u32[]{:S(2)}) collective-permute-start(bf16[64,3584]{1,0:T(8,128)(2,1)} %get-tuple-element.45), channel_id=1, source_target_pairs={{0,8},{4,12},{8,0},{12,4},{16,24},{20,28},{24,16},{28,20},{1,9},{5... | collective-permute-start | bytes 1376264 | tf_op jit(solution)/shard_map/ppermute | solution.py:70
  248.3 31.3 %collective-permute-start.47 = (bf16[64,3584]{1,0:T(8,128)(2,1)}, bf16[64,3584]{1,0:T(8,128)(2,1)S(1)}, u32[]{:S(2)}, u32[]{:S(2)}) collective-permute-start(bf16[64,3584]{1,0:T(8,128)(2,1)} %get-tuple-element.47), channel_id=1, source_target_pairs={{0,8},{4,12},{8,0},{12,4},{16,24},{20,28},{24,16},{28,20},{1,9},{5... | collective-permute-start | bytes 1376264 | tf_op jit(solution)/shard_map/ppermute | solution.py:70
  274.9 14.5 %collective-permute-start.8 = (bf16[64,3584]{1,0:T(8,128)(2,1)S(1)}, bf16[64,3584]{1,0:T(8,128)(2,1)S(1)}, u32[]{:S(2)}, u32[]{:S(2)}) collective-permute-start(bf16[64,3584]{1,0:T(8,128)(2,1)S(1)} %copy-done.36), channel_id=1, source_target_pairs={{0,16},{4,20},{8,24},{12,28},{16,0},{20,4},{24,8},{28,12},{1,17},{... | collective-permute-start | bytes 1376264 | tf_op jit(solution)/shard_map/ppermute | solution.py:70
  276.0 23.9 %collective-permute-start.42 = (bf16[64,3584]{1,0:T(8,128)(2,1)}, bf16[64,3584]{1,0:T(8,128)(2,1)S(1)}, u32[]{:S(2)}, u32[]{:S(2)}) collective-permute-start(bf16[64,3584]{1,0:T(8,128)(2,1)} %get-tuple-element.42), channel_id=1, source_target_pairs={{0,2},{1,3},{2,0},{3,1},{4,6},{5,7},{6,4},{7,5},{8,10},{9,11},{10,... | collective-permute-start | bytes 1376264 | tf_op jit(solution)/shard_map/ppermute | solution.py:70
  279.6 31.9 %collective-permute-start.46 = (bf16[64,3584]{1,0:T(8,128)(2,1)}, bf16[64,3584]{1,0:T(8,128)(2,1)S(1)}, u32[]{:S(2)}, u32[]{:S(2)}) collective-permute-start(bf16[64,3584]{1,0:T(8,128)(2,1)} %get-tuple-element.46), channel_id=1, source_target_pairs={{0,3},{1,2},{2,1},{3,0},{4,7},{5,6},{6,5},{7,4},{8,11},{9,10},{10,... | collective-permute-start | bytes 1376264 | tf_op jit(solution)/shard_map/ppermute | solution.py:70
  287.7 23.8 %collective-permute-start.49 = (bf16[64,3584]{1,0:T(8,128)(2,1)}, bf16[64,3584]{1,0:T(8,128)(2,1)S(1)}, u32[]{:S(2)}, u32[]{:S(2)}) collective-permute-start(bf16[64,3584]{1,0:T(8,128)(2,1)} %shard_map.136), channel_id=1, source_target_pairs={{0,1},{1,0},{2,3},{3,2},{4,5},{5,4},{6,7},{7,6},{8,9},{9,8},{10,11... | collective-permute-start | bytes 1376264 | tf_op jit(solution)/shard_map/ppermute | solution.py:70
  (65 other events, 537.2 us)

commit v3 on v0

--- a/solution.py
+++ b/solution.py
@@ -1,6 +1,11 @@
+import functools
+
 import jax
 import jax.numpy as jnp
+import numpy as np
 from jax import lax
+from jax.experimental import pallas as pl
+from jax.experimental.pallas import tpu as pltpu
 from jax.sharding import PartitionSpec as P
 
 
@@ -21,7 +26,7 @@
     ).astype(jnp.float32)
 
 
-def shards(
+def exchange_slots(
     tokens, route_ids, route_weight, w_gate, w_up, w_down, shared_gate, shared_up, shared_down
 ):
     tok_rows = tokens.shape[0]
@@ -57,7 +62,355 @@
     return (shared + routed).astype(jnp.bfloat16)
 
 
+PAIR, RIGHT, DOWN = 1, 2, 4
+
+
+def swap(value, axis, mask):
+    size = lax.axis_size(axis)
+    return lax.ppermute(value, axis, [(i, i ^ mask) for i in range(size)])
+
+
+def add_body(jobs, *refs):
+    outs = refs[len(refs) - len(jobs) :]
+    at = 0
+    for out, job in zip(outs, jobs):
+        total = refs[at][...].astype(jnp.float32)
+        for k in range(1, job):
+            total += refs[at + k][...].astype(jnp.float32)
+        out[...] = total.astype(out.dtype)
+        at += job
+
+
+def in_hbm(array):
+    return pltpu.with_memory_space_constraint(array, pltpu.HBM)
+
+
+def add_rows(rows, jobs):
+    width = jobs[0][0][0].shape[1]
+    steps = 2
+    span = width // steps
+
+    def spec(block):
+        return pl.BlockSpec((rows, span), lambda j: (block, j))
+
+    return pl.pallas_call(
+        functools.partial(add_body, tuple(len(job) for job in jobs)),
+        grid=(steps,),
+        out_shape=[pltpu.HBM((rows, width), jnp.bfloat16)] * len(jobs),
+        in_specs=[spec(block) for job in jobs for _, block in job],
+        out_specs=[spec(0)] * len(jobs),
+        cost_estimate=pl.CostEstimate(
+            flops=sum(map(len, jobs)) * rows * width,
+            bytes_accessed=2 * (sum(map(len, jobs)) + len(jobs)) * rows * width,
+            transcendentals=0,
+        ),
+    )(*[in_hbm(array) for job in jobs for array, _ in job])
+
+
+LANES = 128
+
+
+def tile_of(size, goal):
+    return max(t for t in range(LANES, goal + 1, LANES) if size % t == 0)
+
+
+def expert_body(dims, *refs):
+    sides, block, most, width, hidden, shared_hidden, tile, span, ring = dims
+    pieces_of = 4
+    rows = pieces_of * block
+    slots = pieces_of * most
+    refs = list(refs)
+
+    def take(number):
+        out = refs[:number]
+        del refs[:number]
+        return out
+
+    pieces = take(sides * pieces_of)
+    (before_ref,) = take(1)
+    experts = [take(3), take(3)]
+    shared = [take(3), take(3)] if shared_hidden else []
+    take(len(refs) - 15 - sides * pieces_of)
+    outs = take(sides * pieces_of)
+    held, chosen, gate, up, down, down_s, act, act_s, back, result = take(10)
+    piece_sem, step_sem, span_sem, span_s_sem, out_sem = take(5)
+    copy = pltpu.make_async_copy
+    f32, bf16 = jnp.float32, jnp.bfloat16
+
+    steps = [(part[0], part[1], None) for part in shared]
+    steps += [
+        (part[0].at[0], part[1].at[0], k * tile) for part in experts for k in range(hidden // tile)
+    ]
+    spans = width // span
+
+    def piece_copy(k):
+        return copy(pieces[k], held.at[pl.ds(k * block, block), :], piece_sem.at[k])
+
+    def step_copies(k):
+        at = k % ring
+        low = steps[k][2] or 0
+        return [
+            copy(steps[k][0].at[:, pl.ds(low, tile)], gate.at[at], step_sem.at[0, at]),
+            copy(steps[k][1].at[:, pl.ds(low, tile)], up.at[at], step_sem.at[1, at]),
+        ]
+
+    def span_copies(k):
+        at = k % ring
+        columns = pl.ds(k * span, span)
+        both = [
+            copy(part[2].at[0, :, columns], down.at[at, e], span_sem.at[at, e])
+            for e, part in enumerate(experts)
+        ]
+        return both + [
+            copy(part[2].at[:, columns], down_s.at[at, e], span_s_sem.at[at, e])
+            for e, part in enumerate(shared)
+        ]
+
+    def out_copy(side, piece, k):
+        return copy(
+            result.at[side, k, pl.ds(piece * block, block), :],
+            outs[side * pieces_of + piece].at[:, pl.ds(k * span, span)],
+            out_sem.at[side, piece, k],
+        )
+
+    def start(copies):
+        for one in copies:
+            one.start()
+
+    def wait(copies):
+        for one in copies:
+            one.wait()
+
+    start([piece_copy(k) for k in range(sides * pieces_of)])
+    start(step_copies(0))
+
+    ey = lax.axis_size("ey")
+    ex = lax.axis_index("ex")
+    me = ex * ey + lax.axis_index("ey")
+    partner = (ex + PAIR - 2 * PAIR * (ex % (2 * PAIR))) * ey + lax.axis_index("ey")
+    row = lax.broadcasted_iota(jnp.int32, (16, LANES), 0)
+    lane = lax.broadcasted_iota(jnp.int32, (16, LANES), 1)
+    pick = (lane == jnp.where(row == 0, me, partner)).astype(f32).astype(bf16)
+    before = before_ref[:rows]
+    base = before_ref[rows : rows + 16].astype(f32)[0:1]
+    slot = lax.broadcasted_iota(jnp.int32, (slots, rows), 0).astype(f32)
+    for side in range(sides):
+        wait([piece_copy(k) for k in range(side * pieces_of, (side + 1) * pieces_of)])
+        if side == 0:
+            for k in range(1, ring):
+                start(step_copies(k))
+        low = side * rows
+        table = held[low : low + rows, width : width + LANES]
+        rate = lax.dot_general(
+            pick, table, (((1,), (1,)), ((), ())), preferred_element_type=f32
+        )
+        named = (rate > 0).astype(f32)
+        rank = jnp.dot(named.astype(bf16), before, preferred_element_type=f32)
+        places = []
+        for e in range(2):
+            where = jnp.where(named[e : e + 1] > 0, rank[e : e + 1] + base, -1.0)
+            place = slot == where
+            back[side, :, e * slots : (e + 1) * slots] = jnp.where(
+                place, rate[e : e + 1], 0.0
+            ).T.astype(bf16)
+            places.append(place.astype(f32).astype(bf16))
+        picked = jnp.dot(
+            jnp.concatenate(places, axis=0),
+            held[low : low + rows, :width],
+            preferred_element_type=f32,
+        ).astype(bf16)
+        for e in range(2):
+            chosen[e, side * slots : (side + 1) * slots] = picked[e * slots : (e + 1) * slots]
+
+    per = hidden // tile
+    for k in range(len(steps)):
+        wait(step_copies(k))
+        e, at = divmod(k - len(shared), per)
+        source = held[:rows, :width] if k < len(shared) else chosen[e]
+        g = jnp.dot(source, gate[k % ring], preferred_element_type=f32)
+        u = jnp.dot(source, up[k % ring], preferred_element_type=f32)
+        h = (jax.nn.silu(g) * u).astype(bf16)
+        if k < len(shared):
+            act_s[k] = h
+        else:
+            act[e, :, at * tile : (at + 1) * tile] = h
+        if k + ring < len(steps):
+            start(step_copies(k + ring))
+        elif k + ring - len(steps) < min(ring, spans):
+            start(span_copies(k + ring - len(steps)))
+
+    for k in range(spans):
+        wait(span_copies(k))
+        y = [
+            jnp.dot(act[e], down[k % ring, e], preferred_element_type=f32).astype(bf16)
+            for e in range(2)
+        ]
+        for side in range(sides):
+            mine = [part[side * slots : (side + 1) * slots] for part in y]
+            out = jnp.dot(back[side], jnp.concatenate(mine, axis=0), preferred_element_type=f32)
+            if side == 0:
+                for e in range(len(shared)):
+                    out += jnp.dot(act_s[e], down_s[k % ring, e], preferred_element_type=f32)
+            result[side, k] = out.astype(bf16)
+            start([out_copy(side, piece, k) for piece in range(pieces_of)])
+        if k + ring < spans:
+            start(span_copies(k + ring))
+
+    wait(
+        [
+            out_copy(side, piece, k)
+            for side in range(sides)
+            for piece in range(pieces_of)
+            for k in range(spans)
+        ]
+    )
+
+
+def run_experts(sides, most, experts, shared, after=()):
+    block, wide = sides[0][0].shape
+    width, hidden = wide - LANES, experts[0][0].shape[2]
+    shared_hidden = shared[0][0].shape[1] if shared else 0
+    tile, span, ring = shared_hidden or tile_of(hidden, 256), tile_of(width, 512), 3
+    number, pieces_of = len(sides), len(sides[0])
+    rows, slots = pieces_of * block, pieces_of * most
+    dims = (number, block, most, width, hidden, shared_hidden, tile, span, ring)
+    bf16 = jnp.bfloat16
+    vmem, sems = pltpu.VMEM, pltpu.SemaphoreType.DMA
+    shared_rows = shared_hidden or 16
+    scratch = [
+        vmem((number * rows, wide), bf16),
+        vmem((2, number * slots, width), bf16),
+        vmem((ring, width, tile), bf16),
+        vmem((ring, width, tile), bf16),
+        vmem((ring, 2, hidden, span), bf16),
+        vmem((ring, 2, shared_rows, span), bf16),
+        vmem((2, number * slots, hidden), bf16),
+        vmem((2, rows, max(shared_rows, LANES)), bf16),
+        vmem((number, rows, 2 * slots), bf16),
+        vmem((number, width // span, rows, span), bf16),
+        sems((number * pieces_of,)),
+        sems((2, ring)),
+        sems((ring, 2)),
+        sems((ring, 2)),
+        sems((number, pieces_of, width // span)),
+    ]
+    token = np.arange(rows)
+    before = (token[:, None] < token) & (token[:, None] // block == token // block)
+    base = np.broadcast_to(token // block * most, (16, rows))
+    before = jnp.asarray(np.concatenate([before, base], axis=0), bf16)
+    operands = [part for side in sides for part in side] + [before]
+    operands += [part for weights in (*experts, *shared) for part in weights]
+    moved = 2 * (sum(part.size for part in operands) + number * rows * width)
+    flops = 2 * number * (6 * slots * width * hidden + 4 * rows * slots * width)
+    flops += 12 * rows * width * shared_hidden
+    operands += after
+    operands = [part if part is before else in_hbm(part) for part in operands]
+    return pl.pallas_call(
+        functools.partial(expert_body, dims),
+        out_shape=[pltpu.HBM((block, width), bf16)] * (number * pieces_of),
+        in_specs=[
+            pl.BlockSpec(memory_space=pltpu.VMEM if part is before else pl.ANY) for part in operands
+        ],
+        out_specs=[pl.BlockSpec(memory_space=pl.ANY)] * (number * pieces_of),
+        scratch_shapes=scratch,
+        compiler_params=pltpu.CompilerParams(vmem_limit_bytes=50 * 1024 * 1024),
+        cost_estimate=pl.CostEstimate(flops=flops, bytes_accessed=moved, transcendentals=0),
+    )(*operands)
+
+
+def pin(done, moving):
+    count = len(done)
+    both = lax.optimization_barrier((*done, *moving))
+    return list(both[:count]), list(both[count:])
+
+
+def gather_all(
+    tokens, route_ids, route_weight, w_gate, w_up, w_down, shared_gate, shared_up, shared_down
+):
+    block = tokens.shape[0]
+    experts = lax.axis_size("ex") * lax.axis_size("ey")
+    most = max(2, 2 * block * route_ids.shape[1] // experts)
+    hit = route_ids[:, :, None] == jnp.arange(LANES, dtype=jnp.int32)
+    table = jnp.sum(jnp.where(hit, route_weight[:, :, None], 0).astype(jnp.float32), axis=1)
+    own = jnp.concatenate([tokens, table.astype(tokens.dtype)], axis=1)
+    def right(value):
+        return swap(value, "ex", RIGHT)
+
+    def down(value):
+        return swap(value, "ex", DOWN)
+
+    def pair(value):
+        return swap(value, "ex", PAIR)
+
+    def far(value, mask):
+        return swap(value, "ey", mask)
+
+    tie = lax.optimization_barrier
+    z2, r0, d0, w_gate_o, w_up_o = far(own, 2), right(own), down(own), pair(w_gate), pair(w_up)
+    z2, r0, d0, w_gate_o, w_up_o, w_down_t, shared_down_t = tie(
+        (z2, r0, d0, w_gate_o, w_up_o, w_down, shared_down)
+    )
+    r2, d2, z3, w_down_o, shared_down_o = (
+        right(z2), down(z2), far(z2, 1), pair(w_down_t), pair(shared_down_t)
+    )
+    r0, r2, d2, z3, w_down_o, shared_down_o, shared_gate_t, shared_up_t, own_t = tie(
+        (r0, r2, d2, z3, w_down_o, shared_down_o, shared_gate, shared_up, own)
+    )
+    a2, a0, z1, shared_gate_o, shared_up_o = (
+        right(d2), down(r0), far(own_t, 1), pair(shared_gate_t), pair(shared_up_t)
+    )
+    a2, a0, z1, shared_gate_o, shared_up_o, z3 = tie(
+        (a2, a0, z1, shared_gate_o, shared_up_o, z3)
+    )
+    experts = [(w_gate, w_up, w_down), (w_gate_o, w_up_o, w_down_o)]
+    shared = [
+        (shared_gate, shared_up, shared_down),
+        (shared_gate_o, shared_up_o, shared_down_o),
+    ]
+    r3, d3, r1, d1 = right(z3), down(z3), right(z1), down(z1)
+    out = run_experts([[own, r0, d0, a0], [z2, r2, d2, a2]], most, experts, shared)
+    out, (r3, d3, r1, d1) = pin(out, (r3, d3, r1, d1))
+    sum0, sum2 = out[:4], out[4:]
+    a3, a1 = down(r3), right(d1)
+    across0, across2 = down(sum0[3]), right(sum2[3])
+    (a3, a1), (across0, across2) = pin((a3, a1), (across0, across2))
+    full0, full2 = add_rows(
+        block, [[(sum0[1], 0), (across0, 0)], [(sum2[2], 0), (across2, 0)]]
+    )
+    sent0, sent2 = right(full0), down(full2)
+    plain0, plain2 = down(sum0[2]), right(sum2[1])
+    out = run_experts([[z3, r3, d3, a3], [z1, r1, d1, a1]], most, experts, [], (full0,))
+    out, (full0, full2, plain0, plain2) = pin(out, (sent0, sent2, plain0, plain2))
+    sum3, sum1 = out[:4], out[4:]
+    across3, across1 = down(sum3[3]), right(sum1[3])
+    part2 = add_rows(block, [[(sum2[0], 0), (plain2, 0), (full2, 0)]])
+    (part2,), (across3, across1) = pin(part2, (across3, across1))
+    back2 = far(part2, 2)
+    full3, full1 = add_rows(
+        block, [[(sum3[1], 0), (across3, 0)], [(sum1[2], 0), (across1, 0)]]
+    )
+    full3, plain3 = right(full3), down(sum3[2])
+    (part3,) = add_rows(block, [[(sum3[0], 0), (plain3, 0), (full3, 0)]])
+    full1, plain1, part3 = lax.optimization_barrier((full1, sum1[1], part3))
+    full1, plain1, back3 = down(full1), right(plain1), far(part3, 3)
+    part1 = add_rows(block, [[(sum1[0], 0), (plain1, 0), (full1, 0)]])
+    part1, (back2,) = pin(part1, (back2,))
+    back1 = far(part1[0], 1)
+    total = [(sum0[0], 0), (plain0, 0), (full0, 0), (back2, 0), (back3, 0), (back1, 0)]
+    return add_rows(block, [total])[0]
+
+
 def solution(mesh):
+    sizes = dict(mesh.shape)
+
+    def shards(*args):
+        tokens, route_ids = args[0], args[1]
+        slots = max(2, 2 * tokens.shape[0] * route_ids.shape[1] // (sizes["ex"] * sizes["ey"]))
+        cube = sizes["ex"] == 2 * DOWN and sizes["ey"] == 4
+        if cube and 4 * slots > tokens.shape[0]:
+            return gather_all(*args)
+        return exchange_slots(*args)
+
     in_specs = (
         P(("ex", "ey"), None),
         P(("ex", "ey"), None),

time: 393 us -> 210 us (0.53)
  blocking collectives: 167 us -> 0 us
  Pallas kernels: 0 us -> 58.4 us
  matrix products: 49.8 us -> 0 us
  waiting for transfers between devices: 153 us -> 108 us
  starting transfers between devices: 3.64 us -> 31.3 us
  between operations: 13.5 us -> 0.31 us
  local copies, waits for them, and re-layouts: 2.36 us -> 7.99 us
    all_to_all x1 -> x0, blocking collectives: 167 us -> none  [shards(): lax.all_to_all(outgoing, ('ex', 'ey'), split_axis=0, concat_axis=0, tiled...]
    ppermute x0 -> x36, waiting for transfers between devices: none -> 108 us  [swap(): return lax.ppermute(value, axis, [(i, i ^ mask) for i in range(size)])]
    all_gather x1 -> x0, waiting for transfers between devices: 77.4 us -> none  [shared_expert(): gathered = lax.all_gather(tokens, 'ex', axis=0, tiled=True)]
    reduce_scatter x1 -> x0, waiting for transfers between devices: 67.5 us -> none  [shared_expert(): lax.psum_scatter(swiglu(gathered, shared_gate, shared_up, shared_down).as...]
    pallas_call x0 -> x8, Pallas kernels: none -> 58.4 us  [the longest x2 44 us: run_experts(): pl.pallas_call(functools.partial(expert_body, dims), out_shape=[pltpu.HBM...]
    dot_general x7 -> x0, matrix products: 49.8 us -> none  [the longest x2 18 us: swiglu(): return jnp.dot(hidden, down_weight, preferred_element_type=jnp.float32)]
    ppermute x0 -> x36, starting transfers between devices: none -> 31.3 us  [swap(): return lax.ppermute(value, axis, [(i, i ^ mask) for i in range(size)])]
    unnamed x15 -> x70, local copies, waits for them, and re-layouts: 0.95 us -> 7.99 us
  transfers between devices with their start and end apart: 3 -> 36, of which waited for: 3 -> 17; matrix products, arithmetic and copies ran while one was open for 3% -> 1% of each run, Pallas kernels for 0% -> 26%
where the time goes in v3:
time: 210 us; the launch traced here: 208 us
  waiting for transfers between devices  108 us (51%)
  Pallas kernels  58.4 us (28%)
  starting transfers between devices  31.3 us (15%)
  local copies, waits for them, and re-layouts  7.99 us (4%)
    ppermute x36, waiting for transfers between devices, swap(): return lax.ppermute(value, axis, [(i, i ^ mask) for i in range(size)])  108 us
    pallas_call x2, Pallas kernels, run_experts(): pl.pallas_call(functools.partial(expert_body, dims), out_shape=[pltpu.HBM...  44 us
    ppermute x36, starting transfers between devices, swap(): return lax.ppermute(value, axis, [(i, i ^ mask) for i in range(size)])  31.3 us
    pallas_call x6, Pallas kernels, add_rows(): pl.pallas_call(functools.partial(add_body, tuple((len(job) for job in job...  14.4 us
    unnamed x70, local copies, waits for them, and re-layouts  7.99 us
  transfers between devices with their start and end apart: 36, of which 17 were waited for; matrix products, arithmetic and copies ran while one was open for 1% of the time, Pallas kernels for 26%

profile of v3, /device:TPU:8, one launch (start us, length us, event | category | flops | bytes accessed | tf_op | source)
XLA Modules:
  0.0 207.8 jit_solution(463123051409245422)
XLA Ops:
  3.4 1.6 collective-permute-start.2
  6.5 2.6 %collective-permute-start = (bf16[64,3712]{1,0:T(8,128)(2,1)S(1)}, bf16[64,3712]{1,0:T(8,128)(2,1)S(1)}, u32[]{:S(2)}, u32[]{:S(2)}) collective-permute-start(bf16[64,3712]{1,0:T(8,128)(2,1)S(1)} %pad_maximum_fusion.refs_0_), channel_id=1, source_target_pairs={{0,2},{1,3},{2,0},{3,1},{4,6},{5,7},{6,4},{7,5},{8,10},{9,11},{10,... | collective-permute-start | bytes 1425416 | tf_op jit(solution)/shard_map/ppermute | solution.py:70
  9.1 7.2 %collective-permute-done.2.refs_2_ = bf16[64,3712]{1,0:T(8,128)(2,1)S(1)} collective-permute-done((bf16[64,3712]{1,0:T(8,128)(2,1)S(1)}, bf16[64,3712]{1,0:T(8,128)(2,1)S(1)}, u32[]{:S(2)}, u32[]{:S(2)}) %collective-permute-start.2) | collective-permute-done | bytes 475168 | tf_op jit(solution)/shard_map/ppermute | solution.py:70
  17.5 11.4 %collective-permute-done.refs_4_ = bf16[64,3712]{1,0:T(8,128)(2,1)S(1)} collective-permute-done((bf16[64,3712]{1,0:T(8,128)(2,1)S(1)}, bf16[64,3712]{1,0:T(8,128)(2,1)S(1)}, u32[]{:S(2)}, u32[]{:S(2)}) %collective-permute-start) | collective-permute-done | bytes 475168 | tf_op jit(solution)/shard_map/ppermute | solution.py:70
  31.8 10.5 %collective-permute-done.7.refs_0_ = bf16[64,3712]{1,0:T(8,128)(2,1)S(1)} collective-permute-done((bf16[64,3712]{1,0:T(8,128)(2,1)S(1)}, bf16[64,3712]{1,0:T(8,128)(2,1)S(1)}, u32[]{:S(2)}, u32[]{:S(2)}) %collective-permute-start.7) | collective-permute-done | bytes 475168 | tf_op jit(solution)/shard_map/ppermute | solution.py:70
  47.6 10.1 %collective-permute-done.12.refs_4_ = bf16[64,3712]{1,0:T(8,128)(2,1)S(1)} collective-permute-done((bf16[64,3712]{1,0:T(8,128)(2,1)S(1)}, bf16[64,3712]{1,0:T(8,128)(2,1)S(1)}, u32[]{:S(2)}, u32[]{:S(2)}) %collective-permute-start.12) | collective-permute-done | bytes 475168 | tf_op jit(solution)/shard_map/ppermute | solution.py:70
  64.6 23.4 %shard_map.109 = (bf16[64,3584]{1,0:T(8,128)(2,1)}, bf16[64,3584]{1,0:T(8,128)(2,1)}, bf16[64,3584]{1,0:T(8,128)(2,1)}, bf16[64,3584]{1,0:T(8,128)(2,1)}, bf16[6...) custom-call(bf16[64,3712]{1,0:T(8,128)(2,1)} %copy-done.2, ...), custom_call_target="tpu_custom_call" | custom-call | flops 15971909632 | bytes 62660608 | tf_op jit(solution)/shard_map/pallas_call | solution.py:308
  92.7 19.3 %collective-permute-done.21.refs_1_ = bf16[64,3584]{1,0:T(8,128)(2,1)S(1)} collective-permute-done((bf16[64,3584]{1,0:T(8,128)(2,1)}, bf16[64,3584]{1,0:T(8,128)(2,1)S(1)}, u32[]{:S(2)}, u32[]{:S(2)}) %collective-permute-start.21) | collective-permute-done | bytes 458784 | tf_op jit(solution)/shard_map/ppermute | solution.py:70
  113.3 2.6 %shard_map.110 = (bf16[64,3584]{1,0:T(8,128)(2,1)}, bf16[64,3584]{1,0:T(8,128)(2,1)}) custom-call(bf16[64,3584]{1,0:T(8,128)(2,1)} %get-tuple-element.122.refs_0_, bf16[64,3584]{1,0:T(8,128)(2,1)} %copy-done.10, bf16[64,3584]{1,0:T(8,128)(2,1)} %get-tuple-element.124.refs_2_, bf16[64,3584]{1,0:T(8,128)(2,1)} %copy-done.11), custom_call_target="tpu_custom_call" | custom-call | flops 917504 | bytes 2752512 | tf_op jit(solution)/shard_map/pallas_call | solution.py:96
  117.9 20.6 %shard_map.111 = (bf16[64,3584]{1,0:T(8,128)(2,1)}, bf16[64,3584]{1,0:T(8,128)(2,1)}, bf16[64,3584]{1,0:T(8,128)(2,1)}, bf16[64,3584]{1,0:T(8,128)(2,1)}, bf16[6...) custom-call(bf16[64,3712]{1,0:T(8,128)(2,1)} %copy-done.22, ...), custom_call_target="tpu_custom_call" | custom-call | flops 13153337344 | bytes 51650560 | tf_op jit(solution)/shard_map/pallas_call | solution.py:308
  138.6 1.6 collective-permute-start.27
  141.3 2.2 %shard_map.112 = bf16[64,3584]{1,0:T(8,128)(2,1)} custom-call(bf16[64,3584]{1,0:T(8,128)(2,1)} %get-tuple-element.142.refs_0_, bf16[64,3584]{1,0:T(8,128)(2,1)} %copy-done.5, bf16[64,3584]{1,0:T(8,128)(2,1)} %copy-done.6), custom_call_target="tpu_custom_call" | custom-call | flops 688128 | bytes 1835008 | tf_op jit(solution)/shard_map/pallas_call | solution.py:96
  143.5 5.1 %collective-permute-done.27.refs_1_ = bf16[64,3584]{1,0:T(8,128)(2,1)S(1)} collective-permute-done((bf16[64,3584]{1,0:T(8,128)(2,1)}, bf16[64,3584]{1,0:T(8,128)(2,1)S(1)}, u32[]{:S(2)}, u32[]{:S(2)}) %collective-permute-start.27) | collective-permute-done | bytes 458784 | tf_op jit(solution)/shard_map/ppermute | solution.py:70
  148.6 3.5 %collective-permute-done.28.refs_3_ = bf16[64,3584]{1,0:T(8,128)(2,1)S(1)} collective-permute-done((bf16[64,3584]{1,0:T(8,128)(2,1)}, bf16[64,3584]{1,0:T(8,128)(2,1)S(1)}, u32[]{:S(2)}, u32[]{:S(2)}) %collective-permute-start.28) | collective-permute-done | bytes 458784 | tf_op jit(solution)/shard_map/ppermute | solution.py:70
  152.9 2.4 %shard_map.113 = (bf16[64,3584]{1,0:T(8,128)(2,1)}, bf16[64,3584]{1,0:T(8,128)(2,1)}) custom-call(bf16[64,3584]{1,0:T(8,128)(2,1)} %get-tuple-element.141.refs_0_, bf16[64,3584]{1,0:T(8,128)(2,1)} %copy-done.12, bf16[64,3584]{1,0:T(8,128)(2,1)} %get-tuple-element.148.refs_2_, bf16[64,3584]{1,0:T(8,128)(2,1)} %copy-done.13), custom_call_target="tpu_custom_call" | custom-call | flops 917504 | bytes 2752512 | tf_op jit(solution)/shard_map/pallas_call | solution.py:96
  155.6 13.0 %collective-permute-done.30.refs_2_ = bf16[64,3584]{1,0:T(8,128)(2,1)S(1)} collective-permute-done((bf16[64,3584]{1,0:T(8,128)(2,1)}, bf16[64,3584]{1,0:T(8,128)(2,1)S(1)}, u32[]{:S(2)}, u32[]{:S(2)}) %collective-permute-start.30) | collective-permute-done | bytes 458784 | tf_op jit(solution)/shard_map/ppermute | solution.py:70
  169.4 2.2 %shard_map.114 = bf16[64,3584]{1,0:T(8,128)(2,1)} custom-call(bf16[64,3584]{1,0:T(8,128)(2,1)} %get-tuple-element.152.refs_0_, bf16[64,3584]{1,0:T(8,128)(2,1)} %copy-done.8, bf16[64,3584]{1,0:T(8,128)(2,1)} %copy-done.17), custom_call_target="tpu_custom_call" | custom-call | flops 688128 | bytes 1835008 | tf_op jit(solution)/shard_map/pallas_call | solution.py:96
  171.6 3.4 %collective-permute-start.33 = (bf16[64,3584]{1,0:T(8,128)(2,1)}, bf16[64,3584]{1,0:T(8,128)(2,1)S(1)}, u32[]{:S(2)}, u32[]{:S(2)}) collective-permute-start(bf16[64,3584]{1,0:T(8,128)(2,1)} %shard_map.112), channel_id=1, source_target_pairs={{0,2},{1,3},{2,0},{3,1},{4,6},{5,7},{6,4},{7,5},{8,10},{9,11},{10,... | collective-permute-start | bytes 1376264 | tf_op jit(solution)/shard_map/ppermute | solution.py:70
  175.1 5.3 %collective-permute-done.31.refs_1_ = bf16[64,3584]{1,0:T(8,128)(2,1)S(1)} collective-permute-done((bf16[64,3584]{1,0:T(8,128)(2,1)}, bf16[64,3584]{1,0:T(8,128)(2,1)S(1)}, u32[]{:S(2)}, u32[]{:S(2)}) %collective-permute-start.31) | collective-permute-done | bytes 458784 | tf_op jit(solution)/shard_map/ppermute | solution.py:70
  181.9 2.2 %shard_map.115 = bf16[64,3584]{1,0:T(8,128)(2,1)} custom-call(bf16[64,3584]{1,0:T(8,128)(2,1)} %get-tuple-element.140.refs_0_, bf16[64,3584]{1,0:T(8,128)(2,1)} %copy-done.14, bf16[64,3584]{1,0:T(8,128)(2,1)} %copy-done.15), custom_call_target="tpu_custom_call" | custom-call | flops 688128 | bytes 1835008 | tf_op jit(solution)/shard_map/pallas_call | solution.py:96
  184.1 11.4 %collective-permute-done.33.refs_3_ = bf16[64,3584]{1,0:T(8,128)(2,1)S(1)} collective-permute-done((bf16[64,3584]{1,0:T(8,128)(2,1)}, bf16[64,3584]{1,0:T(8,128)(2,1)S(1)}, u32[]{:S(2)}, u32[]{:S(2)}) %collective-permute-start.33) | collective-permute-done | bytes 458784 | tf_op jit(solution)/shard_map/ppermute | solution.py:70
  196.9 3.6 %collective-permute-done.34.refs_4_ = bf16[64,3584]{1,0:T(8,128)(2,1)S(1)} collective-permute-done((bf16[64,3584]{1,0:T(8,128)(2,1)}, bf16[64,3584]{1,0:T(8,128)(2,1)S(1)}, u32[]{:S(2)}, u32[]{:S(2)}) %collective-permute-start.34) | collective-permute-done | bytes 458784 | tf_op jit(solution)/shard_map/ppermute | solution.py:70
  200.5 3.7 %collective-permute-done.35.refs_5_ = bf16[64,3584]{1,0:T(8,128)(2,1)S(1)} collective-permute-done((bf16[64,3584]{1,0:T(8,128)(2,1)}, bf16[64,3584]{1,0:T(8,128)(2,1)S(1)}, u32[]{:S(2)}, u32[]{:S(2)}) %collective-permute-start.35) | collective-permute-done | bytes 458784 | tf_op jit(solution)/shard_map/ppermute | solution.py:70
  205.0 2.7 %shard_map.116 = bf16[64,3584]{1,0:T(8,128)(2,1)} custom-call(bf16[64,3584]{1,0:T(8,128)(2,1)} %get-tuple-element.113.refs_0_, bf16[64,3584]{1,0:T(8,128)(2,1)} %copy-done.3, bf16[64,3584]{1,0:T(8,128)(2,1)} %copy-done.4, bf16[64,3584]{1,0:T(8,128)(2,1)} %copy-done.7, bf16[64,3584]{1,0:T(8,128)(2,1)} %copy-done.9, bf16[64,3584]{1,0:T(8,128)(2,1)} %copy-done.16), custom_call_target="tpu_custom_call" | custom-call | flops 1376256 | bytes 3211264 | tf_op jit(solution)/shard_map/pallas_call | solution.py:96
  (128 shorter events, 35.7 us)
Async XLA Ops:
  0.0 28.9 %collective-permute-start.3 = (bf16[1,3584,1024]{2,1,0:T(8,128)(2,1)}, bf16[1,3584,1024]{2,1,0:T(8,128)(2,1)}, u32[]{:S(2)}, u32[]{:S(2)}) collective-permute-start(bf16[1,3584,1024]{2,1,0:T(8,128)(2,1)} %refs_9_.3), channel_id=1, source_target_pairs={{0,4},{4,0},{8,12},{12,8},{16,20},{20,16},{24,28},{28,24},{1,5},{5... | collective-permute-start | bytes 22020104 | tf_op jit(solution)/shard_map/ppermute | solution.py:70
  0.0 28.9 %collective-permute-start.4 = (bf16[1,3584,1024]{2,1,0:T(8,128)(2,1)}, bf16[1,3584,1024]{2,1,0:T(8,128)(2,1)}, u32[]{:S(2)}, u32[]{:S(2)}) collective-permute-start(bf16[1,3584,1024]{2,1,0:T(8,128)(2,1)} %refs_10_.3), channel_id=1, source_target_pairs={{0,4},{4,0},{8,12},{12,8},{16,20},{20,16},{24,28},{28,24},{1,5},{5... | collective-permute-start | bytes 22020104 | tf_op jit(solution)/shard_map/ppermute | solution.py:70
  6.5 22.4 %collective-permute-start = (bf16[64,3712]{1,0:T(8,128)(2,1)S(1)}, bf16[64,3712]{1,0:T(8,128)(2,1)S(1)}, u32[]{:S(2)}, u32[]{:S(2)}) collective-permute-start(bf16[64,3712]{1,0:T(8,128)(2,1)S(1)} %pad_maximum_fusion.refs_0_), channel_id=1, source_target_pairs={{0,2},{1,3},{2,0},{3,1},{4,6},{5,7},{6,4},{7,5},{8,10},{9,11},{10,... | collective-permute-start | bytes 1425416 | tf_op jit(solution)/shard_map/ppermute | solution.py:70
  28.9 15.5 %collective-permute-start.8 = (bf16[1,1024,3584]{2,1,0:T(8,128)(2,1)}, bf16[1,1024,3584]{2,1,0:T(8,128)(2,1)S(1)}, u32[]{:S(2)}, u32[]{:S(2)}) collective-permute-start(bf16[1,1024,3584]{2,1,0:T(8,128)(2,1)} %refs_11_.3), channel_id=1, source_target_pairs={{0,4},{4,0},{8,12},{12,8},{16,20},{20,16},{24,28},{28,24},{1,5},{5... | collective-permute-start | bytes 22020104 | tf_op jit(solution)/shard_map/ppermute | solution.py:70
  29.0 14.7 %collective-permute-start.9 = (bf16[256,3584]{1,0:T(8,128)(2,1)}, bf16[256,3584]{1,0:T(8,128)(2,1)S(1)}, u32[]{:S(2)}, u32[]{:S(2)}) collective-permute-start(bf16[256,3584]{1,0:T(8,128)(2,1)} %refs_17_.1), channel_id=1, source_target_pairs={{0,4},{4,0},{8,12},{12,8},{16,20},{20,16},{24,28},{28,24},{1,5},{5... | collective-permute-start | bytes 5505032 | tf_op jit(solution)/shard_map/ppermute | solution.py:70
  29.4 12.9 %collective-permute-start.7 = (bf16[64,3712]{1,0:T(8,128)(2,1)S(1)}, bf16[64,3712]{1,0:T(8,128)(2,1)S(1)}, u32[]{:S(2)}, u32[]{:S(2)}) collective-permute-start(bf16[64,3712]{1,0:T(8,128)(2,1)S(1)} %collective-permute-done.refs_4_), channel_id=1, source_target_pairs={{0,1},{1,0},{2,3},{3,2},{4,5},{5,4},{6,7},{7,6},{8,9},{9,8},{10,11... | collective-permute-start | bytes 1425416 | tf_op jit(solution)/shard_map/ppermute | solution.py:70
  44.4 15.0 %collective-permute-start.13 = (bf16[3584,256]{1,0:T(8,128)(2,1)}, bf16[3584,256]{1,0:T(8,128)(2,1)S(1)}, u32[]{:S(2)}, u32[]{:S(2)}) collective-permute-start(bf16[3584,256]{1,0:T(8,128)(2,1)} %refs_15_.1), channel_id=1, source_target_pairs={{0,4},{4,0},{8,12},{12,8},{16,20},{20,16},{24,28},{28,24},{1,5},{5... | collective-permute-start | bytes 5505032 | tf_op jit(solution)/shard_map/ppermute | solution.py:70
  44.4 15.0 %collective-permute-start.14 = (bf16[3584,256]{1,0:T(8,128)(2,1)}, bf16[3584,256]{1,0:T(8,128)(2,1)S(1)}, u32[]{:S(2)}, u32[]{:S(2)}) collective-permute-start(bf16[3584,256]{1,0:T(8,128)(2,1)} %refs_16_.1), channel_id=1, source_target_pairs={{0,4},{4,0},{8,12},{12,8},{16,20},{20,16},{24,28},{28,24},{1,5},{5... | collective-permute-start | bytes 5505032 | tf_op jit(solution)/shard_map/ppermute | solution.py:70
  59.4 28.6 %collective-permute-start.16 = (bf16[64,3712]{1,0:T(8,128)(2,1)S(1)}, bf16[64,3712]{1,0:T(8,128)(2,1)S(1)}, u32[]{:S(2)}, u32[]{:S(2)}) collective-permute-start(bf16[64,3712]{1,0:T(8,128)(2,1)S(1)} %collective-permute-done.7.refs_0_), channel_id=1, source_target_pairs={{0,16},{4,20},{8,24},{12,28},{16,0},{20,4},{24,8},{28,12},{1,17},{... | collective-permute-start | bytes 1425416 | tf_op jit(solution)/shard_map/ppermute | solution.py:70
  60.0 28.0 %collective-permute-start.15 = (bf16[64,3712]{1,0:T(8,128)(2,1)S(1)}, bf16[64,3712]{1,0:T(8,128)(2,1)}, u32[]{:S(2)}, u32[]{:S(2)}) collective-permute-start(bf16[64,3712]{1,0:T(8,128)(2,1)S(1)} %collective-permute-done.7.refs_0_), channel_id=1, source_target_pairs={{0,8},{4,12},{8,0},{12,4},{16,24},{20,28},{24,16},{28,20},{1,9},{5... | collective-permute-start | bytes 1425416 | tf_op jit(solution)/shard_map/ppermute | solution.py:70
  60.5 27.5 %collective-permute-start.18 = (bf16[64,3712]{1,0:T(8,128)(2,1)S(1)}, bf16[64,3712]{1,0:T(8,128)(2,1)}, u32[]{:S(2)}, u32[]{:S(2)}) collective-permute-start(bf16[64,3712]{1,0:T(8,128)(2,1)S(1)} %collective-permute-done.12.refs_4_), channel_id=1, source_target_pairs={{0,16},{4,20},{8,24},{12,28},{16,0},{20,4},{24,8},{28,12},{1,17},{... | collective-permute-start | bytes 1425416 | tf_op jit(solution)/shard_map/ppermute | solution.py:70
  62.1 26.0 %collective-permute-start.17 = (bf16[64,3712]{1,0:T(8,128)(2,1)S(1)}, bf16[64,3712]{1,0:T(8,128)(2,1)}, u32[]{:S(2)}, u32[]{:S(2)}) collective-permute-start(bf16[64,3712]{1,0:T(8,128)(2,1)S(1)} %collective-permute-done.12.refs_4_), channel_id=1, source_target_pairs={{0,8},{4,12},{8,0},{12,4},{16,24},{20,28},{24,16},{28,20},{1,9},{5... | collective-permute-start | bytes 1425416 | tf_op jit(solution)/shard_map/ppermute | solution.py:70
  88.0 24.5 %collective-permute-start.19 = (bf16[64,3712]{1,0:T(8,128)(2,1)}, bf16[64,3712]{1,0:T(8,128)(2,1)S(1)}, u32[]{:S(2)}, u32[]{:S(2)}) collective-permute-start(bf16[64,3712]{1,0:T(8,128)(2,1)} %collective-permute-done.15.refs_1_), channel_id=1, source_target_pairs={{0,16},{4,20},{8,24},{12,28},{16,0},{20,4},{24,8},{28,12},{1,17},{... | collective-permute-start | bytes 1425416 | tf_op jit(solution)/shard_map/ppermute | solution.py:70
  88.6 23.9 %collective-permute-start.20 = (bf16[64,3712]{1,0:T(8,128)(2,1)}, bf16[64,3712]{1,0:T(8,128)(2,1)S(1)}, u32[]{:S(2)}, u32[]{:S(2)}) collective-permute-start(bf16[64,3712]{1,0:T(8,128)(2,1)} %collective-permute-done.18.refs_6_), channel_id=1, source_target_pairs={{0,8},{4,12},{8,0},{12,4},{16,24},{20,28},{24,16},{28,20},{1,9},{5... | collective-permute-start | bytes 1425416 | tf_op jit(solution)/shard_map/ppermute | solution.py:70
  89.2 22.8 %collective-permute-start.21 = (bf16[64,3584]{1,0:T(8,128)(2,1)}, bf16[64,3584]{1,0:T(8,128)(2,1)S(1)}, u32[]{:S(2)}, u32[]{:S(2)}) collective-permute-start(bf16[64,3584]{1,0:T(8,128)(2,1)} %get-tuple-element.117), channel_id=1, source_target_pairs={{0,16},{4,20},{8,24},{12,28},{16,0},{20,4},{24,8},{28,12},{1,17},{... | collective-permute-start | bytes 1376264 | tf_op jit(solution)/shard_map/ppermute | solution.py:70
  90.7 21.8 %collective-permute-start.22 = (bf16[64,3584]{1,0:T(8,128)(2,1)}, bf16[64,3584]{1,0:T(8,128)(2,1)S(1)}, u32[]{:S(2)}, u32[]{:S(2)}) collective-permute-start(bf16[64,3584]{1,0:T(8,128)(2,1)} %get-tuple-element.118), channel_id=1, source_target_pairs={{0,8},{4,12},{8,0},{12,4},{16,24},{20,28},{24,16},{28,20},{1,9},{5... | collective-permute-start | bytes 1376264 | tf_op jit(solution)/shard_map/ppermute | solution.py:70
  92.2 46.4 %collective-permute-start.25 = (bf16[64,3584]{1,0:T(8,128)(2,1)}, bf16[64,3584]{1,0:T(8,128)(2,1)S(1)}, u32[]{:S(2)}, u32[]{:S(2)}) collective-permute-start(bf16[64,3584]{1,0:T(8,128)(2,1)} %get-tuple-element.136), channel_id=1, source_target_pairs={{0,16},{4,20},{8,24},{12,28},{16,0},{20,4},{24,8},{28,12},{1,17},{... | collective-permute-start | bytes 1376264 | tf_op jit(solution)/shard_map/ppermute | solution.py:70
  112.0 26.6 %collective-permute-start.26 = (bf16[64,3584]{1,0:T(8,128)(2,1)}, bf16[64,3584]{1,0:T(8,128)(2,1)S(1)}, u32[]{:S(2)}, u32[]{:S(2)}) collective-permute-start(bf16[64,3584]{1,0:T(8,128)(2,1)} %get-tuple-element.137), channel_id=1, source_target_pairs={{0,8},{4,12},{8,0},{12,4},{16,24},{20,28},{24,16},{28,20},{1,9},{5... | collective-permute-start | bytes 1376264 | tf_op jit(solution)/shard_map/ppermute | solution.py:70
  115.9 22.7 %collective-permute-start.24 = (bf16[64,3584]{1,0:T(8,128)(2,1)}, bf16[64,3584]{1,0:T(8,128)(2,1)S(1)}, u32[]{:S(2)}, u32[]{:S(2)}) collective-permute-start(bf16[64,3584]{1,0:T(8,128)(2,1)} %get-tuple-element.135), channel_id=1, source_target_pairs={{0,16},{4,20},{8,24},{12,28},{16,0},{20,4},{24,8},{28,12},{1,17},{... | collective-permute-start | bytes 1376264 | tf_op jit(solution)/shard_map/ppermute | solution.py:70
  116.4 22.2 %collective-permute-start.23 = (bf16[64,3584]{1,0:T(8,128)(2,1)}, bf16[64,3584]{1,0:T(8,128)(2,1)S(1)}, u32[]{:S(2)}, u32[]{:S(2)}) collective-permute-start(bf16[64,3584]{1,0:T(8,128)(2,1)} %get-tuple-element.126.refs_15_), channel_id=1, source_target_pairs={{0,8},{4,12},{8,0},{12,4},{16,24},{20,28},{24,16},{28,20},{1,9},{5... | collective-permute-start | bytes 1376264 | tf_op jit(solution)/shard_map/ppermute | solution.py:70
  140.8 14.9 %collective-permute-start.29 = (bf16[64,3584]{1,0:T(8,128)(2,1)}, bf16[64,3584]{1,0:T(8,128)(2,1)S(1)}, u32[]{:S(2)}, u32[]{:S(2)}) collective-permute-start(bf16[64,3584]{1,0:T(8,128)(2,1)} %get-tuple-element.153), channel_id=1, source_target_pairs={{0,16},{4,20},{8,24},{12,28},{16,0},{20,4},{24,8},{28,12},{1,17},{... | collective-permute-start | bytes 1376264 | tf_op jit(solution)/shard_map/ppermute | solution.py:70
  155.3 13.3 %collective-permute-start.30 = (bf16[64,3584]{1,0:T(8,128)(2,1)}, bf16[64,3584]{1,0:T(8,128)(2,1)S(1)}, u32[]{:S(2)}, u32[]{:S(2)}) collective-permute-start(bf16[64,3584]{1,0:T(8,128)(2,1)} %get-tuple-element.154), channel_id=1, source_target_pairs={{0,8},{4,12},{8,0},{12,4},{16,24},{20,28},{24,16},{28,20},{1,9},{5... | collective-permute-start | bytes 1376264 | tf_op jit(solution)/shard_map/ppermute | solution.py:70
  171.6 23.9 %collective-permute-start.33 = (bf16[64,3584]{1,0:T(8,128)(2,1)}, bf16[64,3584]{1,0:T(8,128)(2,1)S(1)}, u32[]{:S(2)}, u32[]{:S(2)}) collective-permute-start(bf16[64,3584]{1,0:T(8,128)(2,1)} %shard_map.112), channel_id=1, source_target_pairs={{0,2},{1,3},{2,0},{3,1},{4,6},{5,7},{6,4},{7,5},{8,10},{9,11},{10,... | collective-permute-start | bytes 1376264 | tf_op jit(solution)/shard_map/ppermute | solution.py:70
  175.1 25.5 %collective-permute-start.34 = (bf16[64,3584]{1,0:T(8,128)(2,1)}, bf16[64,3584]{1,0:T(8,128)(2,1)S(1)}, u32[]{:S(2)}, u32[]{:S(2)}) collective-permute-start(bf16[64,3584]{1,0:T(8,128)(2,1)} %shard_map.114), channel_id=1, source_target_pairs={{0,3},{1,2},{2,1},{3,0},{4,7},{5,6},{6,5},{7,4},{8,11},{9,10},{10,... | collective-permute-start | bytes 1376264 | tf_op jit(solution)/shard_map/ppermute | solution.py:70
  (46 other events, 779.3 us)

commit v4 on v3

--- a/solution.py
+++ b/solution.py
@@ -63,6 +63,8 @@
 
 
 PAIR, RIGHT, DOWN = 1, 2, 4
+VMEM_LIMIT = 60 * 1024 * 1024
+VMEM_ALL = 64 * 1024 * 1024 - 256 * 1024
 
 
 def swap(value, axis, mask):
@@ -85,7 +87,7 @@
     return pltpu.with_memory_space_constraint(array, pltpu.HBM)
 
 
-def add_rows(rows, jobs):
+def add_rows(rows, jobs, dtype=jnp.bfloat16):
     width = jobs[0][0][0].shape[1]
     steps = 2
     span = width // steps
@@ -96,9 +98,10 @@
     return pl.pallas_call(
         functools.partial(add_body, tuple(len(job) for job in jobs)),
         grid=(steps,),
-        out_shape=[pltpu.HBM((rows, width), jnp.bfloat16)] * len(jobs),
+        out_shape=[pltpu.HBM((rows, width), dtype)] * len(jobs),
         in_specs=[spec(block) for job in jobs for _, block in job],
         out_specs=[spec(0)] * len(jobs),
+        compiler_params=pltpu.CompilerParams(vmem_limit_bytes=VMEM_ALL),
         cost_estimate=pl.CostEstimate(
             flops=sum(map(len, jobs)) * rows * width,
             bytes_accessed=2 * (sum(map(len, jobs)) + len(jobs)) * rows * width,
@@ -112,6 +115,26 @@
 
 def tile_of(size, goal):
     return max(t for t in range(LANES, goal + 1, LANES) if size % t == 0)
+
+
+def table_body(tokens, ids, rates, out):
+    top, rows = ids.shape
+    width = tokens.shape[1]
+    expert = lax.broadcasted_iota(jnp.int32, (LANES, rows), 0)
+    table = jnp.zeros((LANES, rows), jnp.float32)
+    for k in range(top):
+        hit = ids[k : k + 1, :] == expert
+        table += jnp.where(hit, rates[k : k + 1, :].astype(jnp.float32), 0.0)
+    out[:, :width] = tokens[...]
+    out[:, width:] = table.T.astype(out.dtype)
+
+
+def with_table(tokens, ids, rates):
+    rows, width = tokens.shape
+    return pl.pallas_call(
+        table_body,
+        out_shape=jax.ShapeDtypeStruct((rows, width + LANES), tokens.dtype),
+    )(tokens, ids.T, rates.T)
 
 
 def expert_body(dims, *refs):
@@ -137,7 +160,7 @@
     copy = pltpu.make_async_copy
     f32, bf16 = jnp.float32, jnp.bfloat16
 
-    steps = [(part[0], part[1], None) for part in shared]
+    steps = [(part[0], part[1], low) for part, low in zip(shared, (0, shared_hidden))]
     steps += [
         (part[0].at[0], part[1].at[0], k * tile) for part in experts for k in range(hidden // tile)
     ]
@@ -148,9 +171,10 @@
 
     def step_copies(k):
         at = k % ring
-        low = steps[k][2] or 0
+        low = steps[k][2]
+        gate_low = 0 if k < len(shared) else low
         return [
-            copy(steps[k][0].at[:, pl.ds(low, tile)], gate.at[at], step_sem.at[0, at]),
+            copy(steps[k][0].at[:, pl.ds(gate_low, tile)], gate.at[at], step_sem.at[0, at]),
             copy(steps[k][1].at[:, pl.ds(low, tile)], up.at[at], step_sem.at[1, at]),
         ]
 
@@ -313,7 +337,7 @@
         ],
         out_specs=[pl.BlockSpec(memory_space=pl.ANY)] * (number * pieces_of),
         scratch_shapes=scratch,
-        compiler_params=pltpu.CompilerParams(vmem_limit_bytes=50 * 1024 * 1024),
+        compiler_params=pltpu.CompilerParams(vmem_limit_bytes=VMEM_LIMIT),
         cost_estimate=pl.CostEstimate(flops=flops, bytes_accessed=moved, transcendentals=0),
     )(*operands)
 
@@ -330,9 +354,7 @@
     block = tokens.shape[0]
     experts = lax.axis_size("ex") * lax.axis_size("ey")
     most = max(2, 2 * block * route_ids.shape[1] // experts)
-    hit = route_ids[:, :, None] == jnp.arange(LANES, dtype=jnp.int32)
-    table = jnp.sum(jnp.where(hit, route_weight[:, :, None], 0).astype(jnp.float32), axis=1)
-    own = jnp.concatenate([tokens, table.astype(tokens.dtype)], axis=1)
+    own = with_table(tokens, route_ids, route_weight)
     def right(value):
         return swap(value, "ex", RIGHT)
 
@@ -347,57 +369,55 @@
 
     tie = lax.optimization_barrier
     z2, r0, d0, w_gate_o, w_up_o = far(own, 2), right(own), down(own), pair(w_gate), pair(w_up)
-    z2, r0, d0, w_gate_o, w_up_o, w_down_t, shared_down_t = tie(
-        (z2, r0, d0, w_gate_o, w_up_o, w_down, shared_down)
-    )
-    r2, d2, z3, w_down_o, shared_down_o = (
-        right(z2), down(z2), far(z2, 1), pair(w_down_t), pair(shared_down_t)
-    )
-    r0, r2, d2, z3, w_down_o, shared_down_o, shared_gate_t, shared_up_t, own_t = tie(
-        (r0, r2, d2, z3, w_down_o, shared_down_o, shared_gate, shared_up, own)
-    )
-    a2, a0, z1, shared_gate_o, shared_up_o = (
-        right(d2), down(r0), far(own_t, 1), pair(shared_gate_t), pair(shared_up_t)
-    )
-    a2, a0, z1, shared_gate_o, shared_up_o, z3 = tie(
-        (a2, a0, z1, shared_gate_o, shared_up_o, z3)
-    )
+    packed = jnp.concatenate([shared_gate, shared_up], axis=1)
+    z2, r0, d0, w_gate_o, w_up_o, w_down_t, packed = tie(
+        (z2, r0, d0, w_gate_o, w_up_o, w_down, packed)
+    )
+    r2, d2, z3, w_down_o = right(z2), down(z2), far(z2, 1), pair(w_down_t)
+    r0, r2, d2, z3, w_down_o, packed, shared_down_t, own_t = tie(
+        (r0, r2, d2, z3, w_down_o, packed, shared_down, own)
+    )
+    a2, a0, z1, packed_o, shared_down_o = (
+        right(d2), down(r0), far(own_t, 1), pair(packed), pair(shared_down_t)
+    )
+    a2, a0, z1, packed_o, shared_down_o, z3 = tie((a2, a0, z1, packed_o, shared_down_o, z3))
     experts = [(w_gate, w_up, w_down), (w_gate_o, w_up_o, w_down_o)]
-    shared = [
-        (shared_gate, shared_up, shared_down),
-        (shared_gate_o, shared_up_o, shared_down_o),
-    ]
+    shared = [(shared_gate, shared_up, shared_down), (packed_o, packed_o, shared_down_o)]
     r3, d3, r1, d1 = right(z3), down(z3), right(z1), down(z1)
     out = run_experts([[own, r0, d0, a0], [z2, r2, d2, a2]], most, experts, shared)
     out, (r3, d3, r1, d1) = pin(out, (r3, d3, r1, d1))
     sum0, sum2 = out[:4], out[4:]
     a3, a1 = down(r3), right(d1)
     across0, across2 = down(sum0[3]), right(sum2[3])
-    (a3, a1), (across0, across2) = pin((a3, a1), (across0, across2))
+    a3, a1, across0, across2, plain0, plain2 = tie(
+        (a3, a1, across0, across2, sum0[2], sum2[1])
+    )
     full0, full2 = add_rows(
         block, [[(sum0[1], 0), (across0, 0)], [(sum2[2], 0), (across2, 0)]]
     )
     sent0, sent2 = right(full0), down(full2)
-    plain0, plain2 = down(sum0[2]), right(sum2[1])
+    plain0, plain2 = down(plain0), right(plain2)
     out = run_experts([[z3, r3, d3, a3], [z1, r1, d1, a1]], most, experts, [], (full0,))
     out, (full0, full2, plain0, plain2) = pin(out, (sent0, sent2, plain0, plain2))
     sum3, sum1 = out[:4], out[4:]
     across3, across1 = down(sum3[3]), right(sum1[3])
     part2 = add_rows(block, [[(sum2[0], 0), (plain2, 0), (full2, 0)]])
     (part2,), (across3, across1) = pin(part2, (across3, across1))
-    back2 = far(part2, 2)
+    hop2 = far(part2, 1)
     full3, full1 = add_rows(
         block, [[(sum3[1], 0), (across3, 0)], [(sum1[2], 0), (across1, 0)]]
     )
-    full3, plain3 = right(full3), down(sum3[2])
-    (part3,) = add_rows(block, [[(sum3[0], 0), (plain3, 0), (full3, 0)]])
-    full1, plain1, part3 = lax.optimization_barrier((full1, sum1[1], part3))
-    full1, plain1, back3 = down(full1), right(plain1), far(part3, 3)
-    part1 = add_rows(block, [[(sum1[0], 0), (plain1, 0), (full1, 0)]])
-    part1, (back2,) = pin(part1, (back2,))
-    back1 = far(part1[0], 1)
-    total = [(sum0[0], 0), (plain0, 0), (full0, 0), (back2, 0), (back3, 0), (back1, 0)]
-    return add_rows(block, [total])[0]
+    full3, plain3, plain1, full1 = tie((full3, sum3[2], sum1[1], full1))
+    full3, plain3 = right(full3), down(plain3)
+    full3, plain3, hop2, full1, plain1 = tie((full3, plain3, hop2, full1, plain1))
+    full1, plain1 = down(full1), right(plain1)
+    (part3,) = add_rows(block, [[(sum3[0], 0), (plain3, 0), (full3, 0), (hop2, 0)]])
+    back3 = far(part3, 3)
+    (part1,) = add_rows(block, [[(sum1[0], 0), (plain1, 0), (full1, 0)]])
+    back1 = far(part1, 1)
+    total = [(sum0[0], 0), (plain0, 0), (full0, 0), (back3, 0)]
+    (total,) = add_rows(block, [total], jnp.float32)
+    return add_rows(block, [[(total, 0), (back1, 0)]])[0]
 
 
 def solution(mesh):

time: 210 us -> 189 us (0.900)
  waiting for transfers between devices: 108 us -> 80.5 us
  local copies, waits for them, and re-layouts: 7.99 us -> 0.04 us
  starting transfers between devices: 31.3 us -> 38.3 us
  Pallas kernels: 58.4 us -> 65 us
    ppermute x36 -> x35, waiting for transfers between devices: 108 us -> 80.5 us  [swap(): return lax.ppermute(value, axis, [(i, i ^ mask) for i in range(size)])]
    unnamed x70 -> x22, local copies, waits for them, and re-layouts: 7.99 us -> 0.04 us
    ppermute x36 -> x35, starting transfers between devices: 31.3 us -> 38.3 us  [swap(): return lax.ppermute(value, axis, [(i, i ^ mask) for i in range(size)])]
    pallas_call x2, Pallas kernels: 44 us -> 46.9 us  [run_experts(): pl.pallas_call(functools.partial(expert_body, dims), out_shape=[pltpu.HBM...]
    pallas_call x6 -> x7, Pallas kernels: 14.4 us -> 16.2 us  [add_rows(): pl.pallas_call(functools.partial(add_body, tuple((len(job) for job in job...]
  transfers between devices with their start and end apart: 36 -> 35, of which waited for: 17 -> 17; matrix products, arithmetic and copies ran while one was open for 1% -> 1% of each run, Pallas kernels for 26% -> 31%
where the time goes in v4:
time: 189 us; the launch traced here: 186 us
  waiting for transfers between devices  80.5 us (43%)
  Pallas kernels  65 us (34%)
  starting transfers between devices  38.3 us (20%)
  other arithmetic  2.31 us (1%)
    ppermute x35, waiting for transfers between devices, swap(): return lax.ppermute(value, axis, [(i, i ^ mask) for i in range(size)])  80.5 us
    pallas_call x2, Pallas kernels, run_experts(): pl.pallas_call(functools.partial(expert_body, dims), out_shape=[pltpu.HBM...  46.9 us
    ppermute x35, starting transfers between devices, swap(): return lax.ppermute(value, axis, [(i, i ^ mask) for i in range(size)])  38.3 us
    pallas_call x7, Pallas kernels, add_rows(): pl.pallas_call(functools.partial(add_body, tuple((len(job) for job in job...  16.2 us
  transfers between devices with their start and end apart: 35, of which 17 were waited for; matrix products, arithmetic and copies ran while one was open for 1% of the time, Pallas kernels for 31%

profile of v4, /device:TPU:8, one launch (start us, length us, event | category | flops | bytes accessed | tf_op | source)
XLA Modules:
  0.0 186.4 jit_solution(5456241650318295827)
XLA Ops:
  0.5 1.9 %shard_map.109.refs_0_ = bf16[64,3712]{1,0:T(8,128)(2,1)} custom-call(bf16[64,3584]{1,0:T(8,128)(2,1)} %tokens.1, s32[8,64]{1,0:T(8,128)} %bitcast.2, bf16[8,64]{1,0:T(8,128)(2,1)} %bitcast.3), custom_call_target="tpu_custom_call" | custom-call | tf_op jit(solution)/shard_map/pallas_call | solution.py:134
  2.4 2.6 %collective-permute-start = (bf16[64,3712]{1,0:T(8,128)(2,1)}, bf16[64,3712]{1,0:T(8,128)(2,1)S(1)}, u32[]{:S(2)}, u32[]{:S(2)}) collective-permute-start(bf16[64,3712]{1,0:T(8,128)(2,1)} %shard_map.109.refs_0_), channel_id=1, source_target_pairs={{0,2},{1,3},{2,0},{3,1},{4,6},{5,7},{6,4},{7,5},{8,10},{9,11},{10,... | collective-permute-start | bytes 1425416 | tf_op jit(solution)/shard_map/ppermute | solution.py:72
  8.0 2.3 %pad_maximum_fusion = bf16[3584,512]{1,0:T(8,128)(2,1)S(1)} fusion(bf16[3584,256]{1,0:T(8,128)(2,1)} %refs_16_.1, bf16[3584,256]{1,0:T(8,128)(2,1)} %refs_15_.1), kind=kLoop, calls=%fused_computation | loop fusion | flops 7340032 | bytes 7340032 | tf_op jit(solution)/shard_map/concatenate | solution.py:372
  10.4 15.4 %collective-permute-done.refs_4_ = bf16[64,3712]{1,0:T(8,128)(2,1)S(1)} collective-permute-done((bf16[64,3712]{1,0:T(8,128)(2,1)}, bf16[64,3712]{1,0:T(8,128)(2,1)S(1)}, u32[]{:S(2)}, u32[]{:S(2)}) %collective-permute-start) | collective-permute-done | bytes 475168 | tf_op jit(solution)/shard_map/ppermute | solution.py:72
  30.2 9.0 %collective-permute-done.5.refs_5_ = bf16[64,3712]{1,0:T(8,128)(2,1)S(1)} collective-permute-done((bf16[64,3712]{1,0:T(8,128)(2,1)S(1)}, bf16[64,3712]{1,0:T(8,128)(2,1)S(1)}, u32[]{:S(2)}, u32[]{:S(2)}) %collective-permute-start.5) | collective-permute-done | bytes 475168 | tf_op jit(solution)/shard_map/ppermute | solution.py:72
  44.4 10.6 %collective-permute-done.10.refs_3_ = bf16[64,3712]{1,0:T(8,128)(2,1)S(1)} collective-permute-done((bf16[64,3712]{1,0:T(8,128)(2,1)S(1)}, bf16[64,3712]{1,0:T(8,128)(2,1)S(1)}, u32[]{:S(2)}, u32[]{:S(2)}) %collective-permute-start.10) | collective-permute-done | bytes 475168 | tf_op jit(solution)/shard_map/ppermute | solution.py:72
  60.7 24.8 %shard_map.110 = (bf16[64,3584]{1,0:T(8,128)(2,1)}, bf16[64,3584]{1,0:T(8,128)(2,1)}, bf16[64,3584]{1,0:T(8,128)(2,1)}, bf16[64,3584]{1,0:T(8,128)(2,1)}, bf16[6...) custom-call(bf16[64,3712]{1,0:T(8,128)(2,1)} %shard_map.109.refs_0_, ...), custom_call_target="tpu_custom_call" | custom-call | flops 15971909632 | bytes 66330624 | tf_op jit(solution)/shard_map/pallas_call | solution.py:332
  85.6 1.6 collective-permute-start.18
  89.7 16.6 %collective-permute-done.20.refs_1_ = bf16[64,3584]{1,0:T(8,128)(2,1)} collective-permute-done((bf16[64,3584]{1,0:T(8,128)(2,1)}, bf16[64,3584]{1,0:T(8,128)(2,1)}, u32[]{:S(2)}, u32[]{:S(2)}) %collective-permute-start.20) | collective-permute-done | bytes 458784 | tf_op jit(solution)/shard_map/ppermute | solution.py:72
  107.6 2.4 %shard_map.111 = (bf16[64,3584]{1,0:T(8,128)(2,1)}, bf16[64,3584]{1,0:T(8,128)(2,1)}) custom-call(bf16[64,3584]{1,0:T(8,128)(2,1)} %get-tuple-element.128.refs_0_, bf16[64,3584]{1,0:T(8,128)(2,1)} %collective-permute-done.20.refs_1_, bf16[64,3584]{1,0:T(8,128)(2,1)} %get-tuple-element.130.refs_2_, bf16[64,3584]{1,0:T(8,128)(2,1)} %collective-permute-done.21.refs_3_), custom_call_target="tpu_custom_call" | custom-call | flops 917504 | bytes 2752512 | tf_op jit(solution)/shard_map/pallas_call | solution.py:98
  114.0 22.1 %shard_map.112 = (bf16[64,3584]{1,0:T(8,128)(2,1)}, bf16[64,3584]{1,0:T(8,128)(2,1)}, bf16[64,3584]{1,0:T(8,128)(2,1)}, bf16[64,3584]{1,0:T(8,128)(2,1)}, bf16[6...) custom-call(bf16[64,3712]{1,0:T(8,128)(2,1)} %collective-permute-done.7.refs, ...), custom_call_target="tpu_custom_call" | custom-call | flops 13153337344 | bytes 51650560 | tf_op jit(solution)/shard_map/pallas_call | solution.py:332
  137.3 2.2 %shard_map.113 = bf16[64,3584]{1,0:T(8,128)(2,1)} custom-call(bf16[64,3584]{1,0:T(8,128)(2,1)} %get-tuple-element.148.refs_0_, bf16[64,3584]{1,0:T(8,128)(2,1)} %collective-permute-done.25.refs_1_, bf16[64,3584]{1,0:T(8,128)(2,1)} %collective-permute-done.23.refs_2_), custom_call_target="tpu_custom_call" | custom-call | flops 688128 | bytes 1835008 | tf_op jit(solution)/shard_map/pallas_call | solution.py:98
  139.6 5.5 %collective-permute-done.26.refs_1_ = bf16[64,3584]{1,0:T(8,128)(2,1)} collective-permute-done((bf16[64,3584]{1,0:T(8,128)(2,1)}, bf16[64,3584]{1,0:T(8,128)(2,1)}, u32[]{:S(2)}, u32[]{:S(2)}) %collective-permute-start.26) | collective-permute-done | bytes 458784 | tf_op jit(solution)/shard_map/ppermute | solution.py:72
  146.0 2.5 %shard_map.114 = (bf16[64,3584]{1,0:T(8,128)(2,1)}, bf16[64,3584]{1,0:T(8,128)(2,1)}) custom-call(bf16[64,3584]{1,0:T(8,128)(2,1)} %get-tuple-element.147.refs_0_, bf16[64,3584]{1,0:T(8,128)(2,1)} %collective-permute-done.26.refs_1_, bf16[64,3584]{1,0:T(8,128)(2,1)} %get-tuple-element.154.refs_2_, bf16[64,3584]{1,0:T(8,128)(2,1)} %collective-permute-done.27.refs_3_), custom_call_target="tpu_custom_call" | custom-call | flops 917504 | bytes 2752512 | tf_op jit(solution)/shard_map/pallas_call | solution.py:98
  151.9 8.4 %collective-permute-done.28.refs_2_ = bf16[64,3584]{1,0:T(8,128)(2,1)} collective-permute-done((bf16[64,3584]{1,0:T(8,128)(2,1)}, bf16[64,3584]{1,0:T(8,128)(2,1)}, u32[]{:S(2)}, u32[]{:S(2)}) %collective-permute-start.28) | collective-permute-done | bytes 458784 | tf_op jit(solution)/shard_map/ppermute | solution.py:72
  160.7 2.0 %collective-permute-start.32 = (bf16[64,3584]{1,0:T(8,128)(2,1)}, bf16[64,3584]{1,0:T(8,128)(2,1)}, u32[]{:S(2)}, u32[]{:S(2)}) collective-permute-start(bf16[64,3584]{1,0:T(8,128)(2,1)} %get-tuple-element.169), channel_id=1, source_target_pairs={{0,8},{4,12},{8,0},{12,4},{16,24},{20,28},{24,16},{28,20},{1,9},{5... | collective-permute-start | bytes 1376264 | tf_op jit(solution)/shard_map/ppermute | solution.py:72
  162.6 2.1 %collective-permute-start.33 = (bf16[64,3584]{1,0:T(8,128)(2,1)}, bf16[64,3584]{1,0:T(8,128)(2,1)}, u32[]{:S(2)}, u32[]{:S(2)}) collective-permute-start(bf16[64,3584]{1,0:T(8,128)(2,1)} %get-tuple-element.170), channel_id=1, source_target_pairs={{0,16},{4,20},{8,24},{12,28},{16,0},{20,4},{24,8},{28,12},{1,17},{... | collective-permute-start | bytes 1376264 | tf_op jit(solution)/shard_map/ppermute | solution.py:72
  164.8 2.4 %shard_map.115 = bf16[64,3584]{1,0:T(8,128)(2,1)} custom-call(bf16[64,3584]{1,0:T(8,128)(2,1)} %get-tuple-element.146.refs_0_, bf16[64,3584]{1,0:T(8,128)(2,1)} %collective-permute-done.29.refs_1_, bf16[64,3584]{1,0:T(8,128)(2,1)} %collective-permute-done.28.refs_2_, bf16[64,3584]{1,0:T(8,128)(2,1)} %collective-permute-done.30.refs_3_), custom_call_target="tpu_custom_call" | custom-call | flops 917504 | bytes 2293760 | tf_op jit(solution)/shard_map/pallas_call | solution.py:98
  167.1 2.1 %collective-permute-start.31 = (bf16[64,3584]{1,0:T(8,128)(2,1)}, bf16[64,3584]{1,0:T(8,128)(2,1)}, u32[]{:S(2)}, u32[]{:S(2)}) collective-permute-start(bf16[64,3584]{1,0:T(8,128)(2,1)} %shard_map.115), channel_id=1, source_target_pairs={{0,3},{1,2},{2,1},{3,0},{4,7},{5,6},{6,5},{7,4},{8,11},{9,10},{10,... | collective-permute-start | bytes 1376264 | tf_op jit(solution)/shard_map/ppermute | solution.py:72
  169.5 2.1 %collective-permute-done.33.refs_2_ = bf16[64,3584]{1,0:T(8,128)(2,1)} collective-permute-done((bf16[64,3584]{1,0:T(8,128)(2,1)}, bf16[64,3584]{1,0:T(8,128)(2,1)}, u32[]{:S(2)}, u32[]{:S(2)}) %collective-permute-start.33) | collective-permute-done | bytes 458784 | tf_op jit(solution)/shard_map/ppermute | solution.py:72
  171.5 2.2 %shard_map.117 = bf16[64,3584]{1,0:T(8,128)(2,1)} custom-call(bf16[64,3584]{1,0:T(8,128)(2,1)} %get-tuple-element.168.refs_0_, bf16[64,3584]{1,0:T(8,128)(2,1)} %collective-permute-done.32.refs_1_, bf16[64,3584]{1,0:T(8,128)(2,1)} %collective-permute-done.33.refs_2_), custom_call_target="tpu_custom_call" | custom-call | flops 688128 | bytes 1835008 | tf_op jit(solution)/shard_map/pallas_call | solution.py:98
  175.0 5.9 %collective-permute-done.31.refs_3_ = bf16[64,3584]{1,0:T(8,128)(2,1)} collective-permute-done((bf16[64,3584]{1,0:T(8,128)(2,1)}, bf16[64,3584]{1,0:T(8,128)(2,1)}, u32[]{:S(2)}, u32[]{:S(2)}) %collective-permute-start.31) | collective-permute-done | bytes 458784 | tf_op jit(solution)/shard_map/ppermute | solution.py:72
  181.0 2.5 %shard_map.116.refs_0_ = f32[64,3584]{1,0:T(8,128)} custom-call(bf16[64,3584]{1,0:T(8,128)(2,1)} %get-tuple-element.117.refs_0_, bf16[64,3584]{1,0:T(8,128)(2,1)} %collective-permute-done.24.refs_1_, bf16[64,3584]{1,0:T(8,128)(2,1)} %collective-permute-done.22.refs_2_, bf16[64,3584]{1,0:T(8,128)(2,1)} %collective-permute-done.31.refs_3_), custom_call_target="tpu_custom_call" | custom-call | flops 917504 | bytes 2293760 | tf_op jit(solution)/shard_map/pallas_call | solution.py:98
  184.4 2.1 %shard_map.118 = bf16[64,3584]{1,0:T(8,128)(2,1)} custom-call(f32[64,3584]{1,0:T(8,128)} %shard_map.116.refs_0_, bf16[64,3584]{1,0:T(8,128)(2,1)} %collective-permute-done.34.refs_1_), custom_call_target="tpu_custom_call" | custom-call | flops 458752 | bytes 1376256 | tf_op jit(solution)/shard_map/pallas_call | solution.py:98
  (79 shorter events, 35.1 us)
Async XLA Ops:
  0.0 25.7 %collective-permute-start.3 = (bf16[1,3584,1024]{2,1,0:T(8,128)(2,1)}, bf16[1,3584,1024]{2,1,0:T(8,128)(2,1)}, u32[]{:S(2)}, u32[]{:S(2)}) collective-permute-start(bf16[1,3584,1024]{2,1,0:T(8,128)(2,1)} %refs_9_.3), channel_id=1, source_target_pairs={{0,4},{4,0},{8,12},{12,8},{16,20},{20,16},{24,28},{28,24},{1,5},{5... | collective-permute-start | bytes 22020104 | tf_op jit(solution)/shard_map/ppermute | solution.py:72
  0.0 25.7 %collective-permute-start.4 = (bf16[1,3584,1024]{2,1,0:T(8,128)(2,1)}, bf16[1,3584,1024]{2,1,0:T(8,128)(2,1)}, u32[]{:S(2)}, u32[]{:S(2)}) collective-permute-start(bf16[1,3584,1024]{2,1,0:T(8,128)(2,1)} %refs_10_.3), channel_id=1, source_target_pairs={{0,4},{4,0},{8,12},{12,8},{16,20},{20,16},{24,28},{28,24},{1,5},{5... | collective-permute-start | bytes 22020104 | tf_op jit(solution)/shard_map/ppermute | solution.py:72
  2.4 23.3 %collective-permute-start = (bf16[64,3712]{1,0:T(8,128)(2,1)}, bf16[64,3712]{1,0:T(8,128)(2,1)S(1)}, u32[]{:S(2)}, u32[]{:S(2)}) collective-permute-start(bf16[64,3712]{1,0:T(8,128)(2,1)} %shard_map.109.refs_0_), channel_id=1, source_target_pairs={{0,2},{1,3},{2,0},{3,1},{4,6},{5,7},{6,4},{7,5},{8,10},{9,11},{10,... | collective-permute-start | bytes 1425416 | tf_op jit(solution)/shard_map/ppermute | solution.py:72
  5.0 20.7 %collective-permute-start.1 = (bf16[64,3712]{1,0:T(8,128)(2,1)}, bf16[64,3712]{1,0:T(8,128)(2,1)S(1)}, u32[]{:S(2)}, u32[]{:S(2)}) collective-permute-start(bf16[64,3712]{1,0:T(8,128)(2,1)} %shard_map.109.refs_0_), channel_id=1, source_target_pairs={{0,8},{4,12},{8,0},{12,4},{16,24},{20,28},{24,16},{28,20},{1,9},{5... | collective-permute-start | bytes 1425416 | tf_op jit(solution)/shard_map/ppermute | solution.py:72
  6.5 19.2 %collective-permute-start.2 = (bf16[64,3712]{1,0:T(8,128)(2,1)}, bf16[64,3712]{1,0:T(8,128)(2,1)S(1)}, u32[]{:S(2)}, u32[]{:S(2)}) collective-permute-start(bf16[64,3712]{1,0:T(8,128)(2,1)} %shard_map.109.refs_0_), channel_id=1, source_target_pairs={{0,16},{4,20},{8,24},{12,28},{16,0},{20,4},{24,8},{28,12},{1,17},{... | collective-permute-start | bytes 1425416 | tf_op jit(solution)/shard_map/ppermute | solution.py:72
  25.8 15.9 %collective-permute-start.8 = (bf16[1,1024,3584]{2,1,0:T(8,128)(2,1)S(1)}, bf16[1,1024,3584]{2,1,0:T(8,128)(2,1)S(1)}, u32[]{:S(2)}, u32[]{:S(2)}) collective-permute-start(bf16[1,1024,3584]{2,1,0:T(8,128)(2,1)S(1)} %copy-done.1), channel_id=1, source_target_pairs={{0,4},{4,0},{8,12},{12,8},{16,20},{20,16},{24,28},{28,24},{1,5},{5... | collective-permute-start | bytes 22020104 | tf_op jit(solution)/shard_map/ppermute | solution.py:72
  25.8 13.3 %collective-permute-start.5 = (bf16[64,3712]{1,0:T(8,128)(2,1)S(1)}, bf16[64,3712]{1,0:T(8,128)(2,1)S(1)}, u32[]{:S(2)}, u32[]{:S(2)}) collective-permute-start(bf16[64,3712]{1,0:T(8,128)(2,1)S(1)} %collective-permute-done.refs_4_), channel_id=1, source_target_pairs={{0,8},{4,12},{8,0},{12,4},{16,24},{20,28},{24,16},{28,20},{1,9},{5... | collective-permute-start | bytes 1425416 | tf_op jit(solution)/shard_map/ppermute | solution.py:72
  27.4 12.9 %collective-permute-start.6 = (bf16[64,3712]{1,0:T(8,128)(2,1)S(1)}, bf16[64,3712]{1,0:T(8,128)(2,1)S(1)}, u32[]{:S(2)}, u32[]{:S(2)}) collective-permute-start(bf16[64,3712]{1,0:T(8,128)(2,1)S(1)} %collective-permute-done.refs_4_), channel_id=1, source_target_pairs={{0,16},{4,20},{8,24},{12,28},{16,0},{20,4},{24,8},{28,12},{1,17},{... | collective-permute-start | bytes 1425416 | tf_op jit(solution)/shard_map/ppermute | solution.py:72
  41.7 14.2 %collective-permute-start.12 = (bf16[3584,512]{1,0:T(8,128)(2,1)S(1)}, bf16[3584,512]{1,0:T(8,128)(2,1)S(1)}, u32[]{:S(2)}, u32[]{:S(2)}) collective-permute-start(bf16[3584,512]{1,0:T(8,128)(2,1)S(1)} %pad_maximum_fusion), channel_id=1, source_target_pairs={{0,4},{4,0},{8,12},{12,8},{16,20},{20,16},{24,28},{28,24},{1,5},{5... | collective-permute-start | bytes 11010056 | tf_op jit(solution)/shard_map/ppermute | solution.py:72
  41.7 14.2 %collective-permute-start.13 = (bf16[256,3584]{1,0:T(8,128)(2,1)}, bf16[256,3584]{1,0:T(8,128)(2,1)S(1)}, u32[]{:S(2)}, u32[]{:S(2)}) collective-permute-start(bf16[256,3584]{1,0:T(8,128)(2,1)} %refs_17_.1), channel_id=1, source_target_pairs={{0,4},{4,0},{8,12},{12,8},{16,20},{20,16},{24,28},{28,24},{1,5},{5... | collective-permute-start | bytes 5505032 | tf_op jit(solution)/shard_map/ppermute | solution.py:72
  42.2 12.8 %collective-permute-start.10 = (bf16[64,3712]{1,0:T(8,128)(2,1)S(1)}, bf16[64,3712]{1,0:T(8,128)(2,1)S(1)}, u32[]{:S(2)}, u32[]{:S(2)}) collective-permute-start(bf16[64,3712]{1,0:T(8,128)(2,1)S(1)} %collective-permute-done.1.refs_1_), channel_id=1, source_target_pairs={{0,16},{4,20},{8,24},{12,28},{16,0},{20,4},{24,8},{28,12},{1,17},{... | collective-permute-start | bytes 1425416 | tf_op jit(solution)/shard_map/ppermute | solution.py:72
  55.9 29.7 %collective-permute-start.14 = (bf16[64,3712]{1,0:T(8,128)(2,1)}, bf16[64,3712]{1,0:T(8,128)(2,1)}, u32[]{:S(2)}, u32[]{:S(2)}) collective-permute-start(bf16[64,3712]{1,0:T(8,128)(2,1)} %collective-permute-done.7.refs_0_), channel_id=1, source_target_pairs={{0,8},{4,12},{8,0},{12,4},{16,24},{20,28},{24,16},{28,20},{1,9},{5... | collective-permute-start | bytes 1425416 | tf_op jit(solution)/shard_map/ppermute | solution.py:72
  57.4 28.1 %collective-permute-start.15 = (bf16[64,3712]{1,0:T(8,128)(2,1)}, bf16[64,3712]{1,0:T(8,128)(2,1)}, u32[]{:S(2)}, u32[]{:S(2)}) collective-permute-start(bf16[64,3712]{1,0:T(8,128)(2,1)} %collective-permute-done.7.refs_0_), channel_id=1, source_target_pairs={{0,16},{4,20},{8,24},{12,28},{16,0},{20,4},{24,8},{28,12},{1,17},{... | collective-permute-start | bytes 1425416 | tf_op jit(solution)/shard_map/ppermute | solution.py:72
  59.0 26.6 %collective-permute-start.16 = (bf16[64,3712]{1,0:T(8,128)(2,1)}, bf16[64,3712]{1,0:T(8,128)(2,1)}, u32[]{:S(2)}, u32[]{:S(2)}) collective-permute-start(bf16[64,3712]{1,0:T(8,128)(2,1)} %collective-permute-done.11.refs_4_), channel_id=1, source_target_pairs={{0,8},{4,12},{8,0},{12,4},{16,24},{20,28},{24,16},{28,20},{1,9},{5... | collective-permute-start | bytes 1425416 | tf_op jit(solution)/shard_map/ppermute | solution.py:72
  60.1 25.4 %collective-permute-start.17 = (bf16[64,3712]{1,0:T(8,128)(2,1)}, bf16[64,3712]{1,0:T(8,128)(2,1)}, u32[]{:S(2)}, u32[]{:S(2)}) collective-permute-start(bf16[64,3712]{1,0:T(8,128)(2,1)} %collective-permute-done.11.refs_4_), channel_id=1, source_target_pairs={{0,16},{4,20},{8,24},{12,28},{16,0},{20,4},{24,8},{28,12},{1,17},{... | collective-permute-start | bytes 1425416 | tf_op jit(solution)/shard_map/ppermute | solution.py:72
  85.6 22.0 %collective-permute-start.18 = (bf16[64,3712]{1,0:T(8,128)(2,1)}, bf16[64,3712]{1,0:T(8,128)(2,1)}, u32[]{:S(2)}, u32[]{:S(2)}) collective-permute-start(bf16[64,3712]{1,0:T(8,128)(2,1)} %collective-permute-done.14.refs_1_), channel_id=1, source_target_pairs={{0,16},{4,20},{8,24},{12,28},{16,0},{20,4},{24,8},{28,12},{1,17},{... | collective-permute-start | bytes 1425416 | tf_op jit(solution)/shard_map/ppermute | solution.py:72
  87.2 20.4 %collective-permute-start.19 = (bf16[64,3712]{1,0:T(8,128)(2,1)}, bf16[64,3712]{1,0:T(8,128)(2,1)}, u32[]{:S(2)}, u32[]{:S(2)}) collective-permute-start(bf16[64,3712]{1,0:T(8,128)(2,1)} %collective-permute-done.17.refs_6_), channel_id=1, source_target_pairs={{0,8},{4,12},{8,0},{12,4},{16,24},{20,28},{24,16},{28,20},{1,9},{5... | collective-permute-start | bytes 1425416 | tf_op jit(solution)/shard_map/ppermute | solution.py:72
  88.0 18.3 %collective-permute-start.20 = (bf16[64,3584]{1,0:T(8,128)(2,1)}, bf16[64,3584]{1,0:T(8,128)(2,1)}, u32[]{:S(2)}, u32[]{:S(2)}) collective-permute-start(bf16[64,3584]{1,0:T(8,128)(2,1)} %get-tuple-element.121), channel_id=1, source_target_pairs={{0,16},{4,20},{8,24},{12,28},{16,0},{20,4},{24,8},{28,12},{1,17},{... | collective-permute-start | bytes 1376264 | tf_op jit(solution)/shard_map/ppermute | solution.py:72
  88.6 19.0 %collective-permute-start.21 = (bf16[64,3584]{1,0:T(8,128)(2,1)}, bf16[64,3584]{1,0:T(8,128)(2,1)}, u32[]{:S(2)}, u32[]{:S(2)}) collective-permute-start(bf16[64,3584]{1,0:T(8,128)(2,1)} %get-tuple-element.122), channel_id=1, source_target_pairs={{0,8},{4,12},{8,0},{12,4},{16,24},{20,28},{24,16},{28,20},{1,9},{5... | collective-permute-start | bytes 1376264 | tf_op jit(solution)/shard_map/ppermute | solution.py:72
  110.0 26.1 %collective-permute-start.22 = (bf16[64,3584]{1,0:T(8,128)(2,1)}, bf16[64,3584]{1,0:T(8,128)(2,1)}, u32[]{:S(2)}, u32[]{:S(2)}) collective-permute-start(bf16[64,3584]{1,0:T(8,128)(2,1)} %get-tuple-element.132.refs_15_), channel_id=1, source_target_pairs={{0,8},{4,12},{8,0},{12,4},{16,24},{20,28},{24,16},{28,20},{1,9},{5... | collective-permute-start | bytes 1376264 | tf_op jit(solution)/shard_map/ppermute | solution.py:72
  110.6 25.5 %collective-permute-start.23 = (bf16[64,3584]{1,0:T(8,128)(2,1)}, bf16[64,3584]{1,0:T(8,128)(2,1)}, u32[]{:S(2)}, u32[]{:S(2)}) collective-permute-start(bf16[64,3584]{1,0:T(8,128)(2,1)} %get-tuple-element.141), channel_id=1, source_target_pairs={{0,16},{4,20},{8,24},{12,28},{16,0},{20,4},{24,8},{28,12},{1,17},{... | collective-permute-start | bytes 1376264 | tf_op jit(solution)/shard_map/ppermute | solution.py:72
  111.1 25.0 %collective-permute-start.24 = (bf16[64,3584]{1,0:T(8,128)(2,1)}, bf16[64,3584]{1,0:T(8,128)(2,1)}, u32[]{:S(2)}, u32[]{:S(2)}) collective-permute-start(bf16[64,3584]{1,0:T(8,128)(2,1)} %get-tuple-element.142), channel_id=1, source_target_pairs={{0,16},{4,20},{8,24},{12,28},{16,0},{20,4},{24,8},{28,12},{1,17},{... | collective-permute-start | bytes 1376264 | tf_op jit(solution)/shard_map/ppermute | solution.py:72
  112.6 23.5 %collective-permute-start.25 = (bf16[64,3584]{1,0:T(8,128)(2,1)}, bf16[64,3584]{1,0:T(8,128)(2,1)}, u32[]{:S(2)}, u32[]{:S(2)}) collective-permute-start(bf16[64,3584]{1,0:T(8,128)(2,1)} %get-tuple-element.143), channel_id=1, source_target_pairs={{0,8},{4,12},{8,0},{12,4},{16,24},{20,28},{24,16},{28,20},{1,9},{5... | collective-permute-start | bytes 1376264 | tf_op jit(solution)/shard_map/ppermute | solution.py:72
  167.1 13.8 %collective-permute-start.31 = (bf16[64,3584]{1,0:T(8,128)(2,1)}, bf16[64,3584]{1,0:T(8,128)(2,1)}, u32[]{:S(2)}, u32[]{:S(2)}) collective-permute-start(bf16[64,3584]{1,0:T(8,128)(2,1)} %shard_map.115), channel_id=1, source_target_pairs={{0,3},{1,2},{2,1},{3,0},{4,7},{5,6},{6,5},{7,4},{8,11},{9,10},{10,... | collective-permute-start | bytes 1376264 | tf_op jit(solution)/shard_map/ppermute | solution.py:72
  (22 other events, 314.2 us)

commit v5 on v4

--- a/solution.py
+++ b/solution.py
@@ -63,8 +63,7 @@
 
 
 PAIR, RIGHT, DOWN = 1, 2, 4
-VMEM_LIMIT = 60 * 1024 * 1024
-VMEM_ALL = 64 * 1024 * 1024 - 256 * 1024
+VMEM_LIMIT = 42 * 1024 * 1024
 
 
 def swap(value, axis, mask):
@@ -72,42 +71,15 @@
     return lax.ppermute(value, axis, [(i, i ^ mask) for i in range(size)])
 
 
-def add_body(jobs, *refs):
-    outs = refs[len(refs) - len(jobs) :]
-    at = 0
-    for out, job in zip(outs, jobs):
-        total = refs[at][...].astype(jnp.float32)
-        for k in range(1, job):
-            total += refs[at + k][...].astype(jnp.float32)
-        out[...] = total.astype(out.dtype)
-        at += job
-
-
 def in_hbm(array):
     return pltpu.with_memory_space_constraint(array, pltpu.HBM)
 
 
-def add_rows(rows, jobs, dtype=jnp.bfloat16):
-    width = jobs[0][0][0].shape[1]
-    steps = 2
-    span = width // steps
-
-    def spec(block):
-        return pl.BlockSpec((rows, span), lambda j: (block, j))
-
-    return pl.pallas_call(
-        functools.partial(add_body, tuple(len(job) for job in jobs)),
-        grid=(steps,),
-        out_shape=[pltpu.HBM((rows, width), dtype)] * len(jobs),
-        in_specs=[spec(block) for job in jobs for _, block in job],
-        out_specs=[spec(0)] * len(jobs),
-        compiler_params=pltpu.CompilerParams(vmem_limit_bytes=VMEM_ALL),
-        cost_estimate=pl.CostEstimate(
-            flops=sum(map(len, jobs)) * rows * width,
-            bytes_accessed=2 * (sum(map(len, jobs)) + len(jobs)) * rows * width,
-            transcendentals=0,
-        ),
-    )(*[in_hbm(array) for job in jobs for array, _ in job])
+def add_rows(*parts, dtype=jnp.bfloat16):
+    total = parts[0].astype(jnp.float32)
+    for part in parts[1:]:
+        total = total + part.astype(jnp.float32)
+    return total.astype(dtype)
 
 
 LANES = 128
@@ -138,8 +110,9 @@
 
 
 def expert_body(dims, *refs):
-    sides, block, most, width, hidden, shared_hidden, tile, span, ring = dims
+    lows, block, most, width, hidden, shared_hidden, tile, span, ring = dims
     pieces_of = 4
+    sides = len(lows) // pieces_of
     rows = pieces_of * block
     slots = pieces_of * most
     refs = list(refs)
@@ -167,7 +140,8 @@
     spans = width // span
 
     def piece_copy(k):
-        return copy(pieces[k], held.at[pl.ds(k * block, block), :], piece_sem.at[k])
+        rows_of = pl.ds(lows[k], block)
+        return copy(pieces[k].at[rows_of], held.at[pl.ds(k * block, block), :], piece_sem.at[k])
 
     def step_copies(k):
         at = k % ring
@@ -290,14 +264,15 @@
     )
 
 
-def run_experts(sides, most, experts, shared, after=()):
-    block, wide = sides[0][0].shape
+def run_experts(sides, block, most, experts, shared, after=()):
+    wide = sides[0][0][0].shape[1]
     width, hidden = wide - LANES, experts[0][0].shape[2]
     shared_hidden = shared[0][0].shape[1] if shared else 0
-    tile, span, ring = shared_hidden or tile_of(hidden, 256), tile_of(width, 512), 3
+    tile, span, ring = shared_hidden or tile_of(hidden, 256), tile_of(width, 1024), 3
     number, pieces_of = len(sides), len(sides[0])
     rows, slots = pieces_of * block, pieces_of * most
-    dims = (number, block, most, width, hidden, shared_hidden, tile, span, ring)
+    lows = tuple(at * block for side in sides for _, at in side)
+    dims = (lows, block, most, width, hidden, shared_hidden, tile, span, ring)
     bf16 = jnp.bfloat16
     vmem, sems = pltpu.VMEM, pltpu.SemaphoreType.DMA
     shared_rows = shared_hidden or 16
@@ -322,7 +297,7 @@
     before = (token[:, None] < token) & (token[:, None] // block == token // block)
     base = np.broadcast_to(token // block * most, (16, rows))
     before = jnp.asarray(np.concatenate([before, base], axis=0), bf16)
-    operands = [part for side in sides for part in side] + [before]
+    operands = [part for side in sides for part, _ in side] + [before]
     operands += [part for weights in (*experts, *shared) for part in weights]
     moved = 2 * (sum(part.size for part in operands) + number * rows * width)
     flops = 2 * number * (6 * slots * width * hidden + 4 * rows * slots * width)
@@ -383,41 +358,35 @@
     a2, a0, z1, packed_o, shared_down_o, z3 = tie((a2, a0, z1, packed_o, shared_down_o, z3))
     experts = [(w_gate, w_up, w_down), (w_gate_o, w_up_o, w_down_o)]
     shared = [(shared_gate, shared_up, shared_down), (packed_o, packed_o, shared_down_o)]
-    r3, d3, r1, d1 = right(z3), down(z3), right(z1), down(z1)
-    out = run_experts([[own, r0, d0, a0], [z2, r2, d2, a2]], most, experts, shared)
-    out, (r3, d3, r1, d1) = pin(out, (r3, d3, r1, d1))
+    pair31 = jnp.concatenate([z3, z1], axis=0)
+    r31, d31, a3, a1 = right(pair31), down(pair31), far(a2, 1), far(a0, 1)
+    sides = [[(own, 0), (r0, 0), (d0, 0), (a0, 0)], [(z2, 0), (r2, 0), (d2, 0), (a2, 0)]]
+    out = run_experts(sides, block, most, experts, shared)
+    out, (r31, d31, a3, a1) = pin(out, (r31, d31, a3, a1))
     sum0, sum2 = out[:4], out[4:]
-    a3, a1 = down(r3), right(d1)
-    across0, across2 = down(sum0[3]), right(sum2[3])
-    a3, a1, across0, across2, plain0, plain2 = tie(
-        (a3, a1, across0, across2, sum0[2], sum2[1])
-    )
-    full0, full2 = add_rows(
-        block, [[(sum0[1], 0), (across0, 0)], [(sum2[2], 0), (across2, 0)]]
-    )
-    sent0, sent2 = right(full0), down(full2)
-    plain0, plain2 = down(plain0), right(plain2)
-    out = run_experts([[z3, r3, d3, a3], [z1, r1, d1, a1]], most, experts, [], (full0,))
-    out, (full0, full2, plain0, plain2) = pin(out, (sent0, sent2, plain0, plain2))
+    sent0, sent2, plain0, plain2 = down(sum0[3]), right(sum2[3]), down(sum0[2]), right(sum2[1])
+    sides = [[(z3, 0), (r31, 0), (d31, 0), (a3, 0)], [(z1, 0), (r31, 1), (d31, 1), (a1, 0)]]
+    out = run_experts(sides, block, most, experts, [], (sum0[0],))
+    out, (across0, across2, plain0, plain2) = pin(out, (sent0, sent2, plain0, plain2))
     sum3, sum1 = out[:4], out[4:]
     across3, across1 = down(sum3[3]), right(sum1[3])
-    part2 = add_rows(block, [[(sum2[0], 0), (plain2, 0), (full2, 0)]])
-    (part2,), (across3, across1) = pin(part2, (across3, across1))
-    hop2 = far(part2, 1)
-    full3, full1 = add_rows(
-        block, [[(sum3[1], 0), (across3, 0)], [(sum1[2], 0), (across1, 0)]]
-    )
-    full3, plain3, plain1, full1 = tie((full3, sum3[2], sum1[1], full1))
+    full0, full2 = add_rows(sum0[1], across0), add_rows(sum2[2], across2)
+    full0, full2 = right(full0), down(full2)
+    across3, across1, full0, full2, plain3, plain1 = tie(
+        (across3, across1, full0, full2, sum3[2], sum1[1])
+    )
+    hop2 = far(add_rows(sum2[0], plain2, full2), 1)
+    full3, full1 = add_rows(sum3[1], across3), add_rows(sum1[2], across1)
+    full3, plain3, plain1, full1 = tie((full3, plain3, plain1, full1))
     full3, plain3 = right(full3), down(plain3)
     full3, plain3, hop2, full1, plain1 = tie((full3, plain3, hop2, full1, plain1))
     full1, plain1 = down(full1), right(plain1)
-    (part3,) = add_rows(block, [[(sum3[0], 0), (plain3, 0), (full3, 0), (hop2, 0)]])
+    part3 = add_rows(sum3[0], plain3, full3, hop2)
     back3 = far(part3, 3)
-    (part1,) = add_rows(block, [[(sum1[0], 0), (plain1, 0), (full1, 0)]])
+    part1 = add_rows(sum1[0], plain1, full1)
     back1 = far(part1, 1)
-    total = [(sum0[0], 0), (plain0, 0), (full0, 0), (back3, 0)]
-    (total,) = add_rows(block, [total], jnp.float32)
-    return add_rows(block, [[(total, 0), (back1, 0)]])[0]
+    total = add_rows(sum0[0], plain0, full0, back3, dtype=jnp.float32)
+    return add_rows(total, back1)
 
 
 def solution(mesh):

time: 189 us -> 167 us (0.88)
  Pallas kernels: 65 us -> 45.7 us
  waiting for transfers between devices: 80.5 us -> 74.6 us
  other arithmetic: 2.31 us -> 5.51 us
    pallas_call x7 -> x0, Pallas kernels: 16.2 us -> none  [add_rows(): pl.pallas_call(functools.partial(add_body, tuple((len(job) for job in job...]
    ppermute x35 -> x33, waiting for transfers between devices: 80.5 us -> 74.6 us  [swap(): return lax.ppermute(value, axis, [(i, i ^ mask) for i in range(size)])]
    convert_element_type x0 -> x7, other arithmetic: none -> 3.2 us  [add_rows(): return total.astype(dtype)]
    pallas_call x2, Pallas kernels: 46.9 us -> 43.7 us  [run_experts(): pl.pallas_call(functools.partial(expert_body, dims), out_shape=[pltpu.HBM...]
    ppermute x35 -> x33, starting transfers between devices: 38.3 us -> 39.1 us  [swap(): return lax.ppermute(value, axis, [(i, i ^ mask) for i in range(size)])]
  transfers between devices with their start and end apart: 35 -> 33, of which waited for: 17 -> 16; matrix products, arithmetic and copies ran while one was open for 1% -> 2% of each run, Pallas kernels for 31% -> 28%
where the time goes in v5:
time: 167 us; the launch traced here: 165 us
  waiting for transfers between devices  74.6 us (45%)
  Pallas kernels  45.7 us (27%)
  starting transfers between devices  39.1 us (23%)
  other arithmetic  5.51 us (3%)
    ppermute x33, waiting for transfers between devices, swap(): return lax.ppermute(value, axis, [(i, i ^ mask) for i in range(size)])  74.6 us
    pallas_call x2, Pallas kernels, run_experts(): pl.pallas_call(functools.partial(expert_body, dims), out_shape=[pltpu.HBM...  43.7 us
    ppermute x33, starting transfers between devices, swap(): return lax.ppermute(value, axis, [(i, i ^ mask) for i in range(size)])  39.1 us
  transfers between devices with their start and end apart: 33, of which 16 were waited for; matrix products, arithmetic and copies ran while one was open for 2% of the time, Pallas kernels for 28%

profile of v5, /device:TPU:8, one launch (start us, length us, event | category | flops | bytes accessed | tf_op | source)
XLA Modules:
  0.0 165.4 jit_solution(2434092327064951590)
XLA Ops:
  0.5 1.9 %shard_map.109.refs_0_ = bf16[64,3712]{1,0:T(8,128)(2,1)} custom-call(bf16[64,3584]{1,0:T(8,128)(2,1)} %tokens.1, s32[8,64]{1,0:T(8,128)} %bitcast.2, bf16[8,64]{1,0:T(8,128)(2,1)} %bitcast.3), custom_call_target="tpu_custom_call" | custom-call | tf_op jit(solution)/shard_map/pallas_call | solution.py:106
  2.5 2.6 %collective-permute-start = (bf16[64,3712]{1,0:T(8,128)(2,1)}, bf16[64,3712]{1,0:T(8,128)(2,1)S(1)}, u32[]{:S(2)}, u32[]{:S(2)}) collective-permute-start(bf16[64,3712]{1,0:T(8,128)(2,1)} %shard_map.109.refs_0_), channel_id=1, source_target_pairs={{0,2},{1,3},{2,0},{3,1},{4,6},{5,7},{6,4},{7,5},{8,10},{9,11},{10,... | collective-permute-start | bytes 1425416 | tf_op jit(solution)/shard_map/ppermute | solution.py:71
  6.5 1.5 collective-permute-start.2
  8.1 2.3 %pad_maximum_fusion = bf16[3584,512]{1,0:T(8,128)(2,1)S(1)} fusion(bf16[3584,256]{1,0:T(8,128)(2,1)} %refs_16_.1, bf16[3584,256]{1,0:T(8,128)(2,1)} %refs_15_.1), kind=kLoop, calls=%fused_computation | loop fusion | flops 7340032 | bytes 7340032 | tf_op jit(solution)/shard_map/concatenate | solution.py:347
  10.4 15.4 %collective-permute-done.refs_4_ = bf16[64,3712]{1,0:T(8,128)(2,1)S(1)} collective-permute-done((bf16[64,3712]{1,0:T(8,128)(2,1)}, bf16[64,3712]{1,0:T(8,128)(2,1)S(1)}, u32[]{:S(2)}, u32[]{:S(2)}) %collective-permute-start) | collective-permute-done | bytes 475168 | tf_op jit(solution)/shard_map/ppermute | solution.py:71
  25.9 1.5 collective-permute-start.5
  30.2 9.0 %collective-permute-done.5.refs_5_ = bf16[64,3712]{1,0:T(8,128)(2,1)S(1)} collective-permute-done((bf16[64,3712]{1,0:T(8,128)(2,1)S(1)}, bf16[64,3712]{1,0:T(8,128)(2,1)S(1)}, u32[]{:S(2)}, u32[]{:S(2)}) %collective-permute-start.5) | collective-permute-done | bytes 475168 | tf_op jit(solution)/shard_map/ppermute | solution.py:71
  44.5 10.6 %collective-permute-done.9.refs_7_ = bf16[64,3712]{1,0:T(8,128)(2,1)S(1)} collective-permute-done((bf16[64,3712]{1,0:T(8,128)(2,1)S(1)}, bf16[64,3712]{1,0:T(8,128)(2,1)S(1)}, u32[]{:S(2)}, u32[]{:S(2)}) %collective-permute-start.9) | collective-permute-done | bytes 475168 | tf_op jit(solution)/shard_map/ppermute | solution.py:71
  55.6 1.6 collective-permute-start.14
  57.2 1.5 collective-permute-start.15
  60.8 23.4 %shard_map.110 = (bf16[64,3584]{1,0:T(8,128)(2,1)}, bf16[64,3584]{1,0:T(8,128)(2,1)}, bf16[64,3584]{1,0:T(8,128)(2,1)}, bf16[64,3584]{1,0:T(8,128)(2,1)}, bf16[6...) custom-call(bf16[64,3712]{1,0:T(8,128)(2,1)} %shard_map.109.refs_0_, ...), custom_call_target="tpu_custom_call" | custom-call | flops 15971909632 | bytes 66330624 | tf_op jit(solution)/shard_map/pallas_call | solution.py:307
  85.5 1.5 collective-permute-start.20
  88.5 20.3 %shard_map.111 = (bf16[64,3584]{1,0:T(8,128)(2,1)}, bf16[64,3584]{1,0:T(8,128)(2,1)}, bf16[64,3584]{1,0:T(8,128)(2,1)}, bf16[64,3584]{1,0:T(8,128)(2,1)}, bf16[6...) custom-call(bf16[64,3712]{1,0:T(8,128)(2,1)} %copy-done.6, ...), custom_call_target="tpu_custom_call" | custom-call | flops 13153337344 | bytes 53551104 | tf_op jit(solution)/shard_map/pallas_call | solution.py:307
  110.1 1.6 collective-permute-start.24
  111.8 1.6 collective-permute-start.25
  113.4 9.2 %collective-permute-done.22 = bf16[64,3584]{1,0:T(8,128)(2,1)S(1)} collective-permute-done((bf16[64,3584]{1,0:T(8,128)(2,1)}, bf16[64,3584]{1,0:T(8,128)(2,1)S(1)}, u32[]{:S(2)}, u32[]{:S(2)}) %collective-permute-start.22) | collective-permute-done | bytes 458784 | tf_op jit(solution)/shard_map/ppermute | solution.py:71
  123.2 5.6 %collective-permute-done.24 = bf16[64,3584]{1,0:T(8,128)(2,1)S(1)} collective-permute-done((bf16[64,3584]{1,0:T(8,128)(2,1)S(1)}, bf16[64,3584]{1,0:T(8,128)(2,1)S(1)}, u32[]{:S(2)}, u32[]{:S(2)}) %collective-permute-start.24) | collective-permute-done | bytes 458784 | tf_op jit(solution)/shard_map/ppermute | solution.py:71
  130.8 1.5 collective-permute-start.27
  133.8 6.5 %collective-permute-done.26 = bf16[64,3584]{1,0:T(8,128)(2,1)S(1)} collective-permute-done((bf16[64,3584]{1,0:T(8,128)(2,1)S(1)}, bf16[64,3584]{1,0:T(8,128)(2,1)S(1)}, u32[]{:S(2)}, u32[]{:S(2)}) %collective-permute-start.26) | collective-permute-done | bytes 458784 | tf_op jit(solution)/shard_map/ppermute | solution.py:71
  141.8 2.3 %collective-permute-start.31 = (bf16[64,3584]{1,0:T(8,128)(2,1)S(1)}, bf16[64,3584]{1,0:T(8,128)(2,1)S(1)}, u32[]{:S(2)}, u32[]{:S(2)}) collective-permute-start(bf16[64,3584]{1,0:T(8,128)(2,1)S(1)} %get-tuple-element.156), channel_id=1, source_target_pairs={{0,16},{4,20},{8,24},{12,28},{16,0},{20,4},{24,8},{28,12},{1,17},{... | collective-permute-start | bytes 1376264 | tf_op jit(solution)/shard_map/ppermute | solution.py:71
  145.8 3.7 %collective-permute-start.29 = (bf16[64,3584]{1,0:T(8,128)(2,1)S(1)}, bf16[64,3584]{1,0:T(8,128)(2,1)S(1)}, u32[]{:S(2)}, u32[]{:S(2)}) collective-permute-start(bf16[64,3584]{1,0:T(8,128)(2,1)S(1)} %add_convert_fusion.2), channel_id=1, source_target_pairs={{0,3},{1,2},{2,1},{3,0},{4,7},{5,6},{6,5},{7,4},{8,11},{9,10},{10,... | collective-permute-start | bytes 1376264 | tf_op jit(solution)/shard_map/ppermute | solution.py:71
  150.6 2.0 %collective-permute-done.30 = bf16[64,3584]{1,0:T(8,128)(2,1)S(1)} collective-permute-done((bf16[64,3584]{1,0:T(8,128)(2,1)S(1)}, bf16[64,3584]{1,0:T(8,128)(2,1)S(1)}, u32[]{:S(2)}, u32[]{:S(2)}) %collective-permute-start.30) | collective-permute-done | bytes 458784 | tf_op jit(solution)/shard_map/ppermute | solution.py:71
  154.1 6.9 %collective-permute-done.29 = bf16[64,3584]{1,0:T(8,128)(2,1)S(1)} collective-permute-done((bf16[64,3584]{1,0:T(8,128)(2,1)S(1)}, bf16[64,3584]{1,0:T(8,128)(2,1)S(1)}, u32[]{:S(2)}, u32[]{:S(2)}) %collective-permute-start.29) | collective-permute-done | bytes 458784 | tf_op jit(solution)/shard_map/ppermute | solution.py:71
  161.0 3.4 %collective-permute-done.32 = bf16[64,3584]{1,0:T(8,128)(2,1)S(1)} collective-permute-done((bf16[64,3584]{1,0:T(8,128)(2,1)S(1)}, bf16[64,3584]{1,0:T(8,128)(2,1)S(1)}, u32[]{:S(2)}, u32[]{:S(2)}) %collective-permute-start.32) | collective-permute-done | bytes 458784 | tf_op jit(solution)/shard_map/ppermute | solution.py:71
  (109 shorter events, 27.4 us)
Async XLA Ops:
  0.0 25.8 %collective-permute-start.3 = (bf16[1,3584,1024]{2,1,0:T(8,128)(2,1)}, bf16[1,3584,1024]{2,1,0:T(8,128)(2,1)}, u32[]{:S(2)}, u32[]{:S(2)}) collective-permute-start(bf16[1,3584,1024]{2,1,0:T(8,128)(2,1)} %refs_9_.3), channel_id=1, source_target_pairs={{0,4},{4,0},{8,12},{12,8},{16,20},{20,16},{24,28},{28,24},{1,5},{5... | collective-permute-start | bytes 22020104 | tf_op jit(solution)/shard_map/ppermute | solution.py:71
  0.0 25.8 %collective-permute-start.4 = (bf16[1,3584,1024]{2,1,0:T(8,128)(2,1)}, bf16[1,3584,1024]{2,1,0:T(8,128)(2,1)}, u32[]{:S(2)}, u32[]{:S(2)}) collective-permute-start(bf16[1,3584,1024]{2,1,0:T(8,128)(2,1)} %refs_10_.3), channel_id=1, source_target_pairs={{0,4},{4,0},{8,12},{12,8},{16,20},{20,16},{24,28},{28,24},{1,5},{5... | collective-permute-start | bytes 22020104 | tf_op jit(solution)/shard_map/ppermute | solution.py:71
  2.5 23.3 %collective-permute-start = (bf16[64,3712]{1,0:T(8,128)(2,1)}, bf16[64,3712]{1,0:T(8,128)(2,1)S(1)}, u32[]{:S(2)}, u32[]{:S(2)}) collective-permute-start(bf16[64,3712]{1,0:T(8,128)(2,1)} %shard_map.109.refs_0_), channel_id=1, source_target_pairs={{0,2},{1,3},{2,0},{3,1},{4,6},{5,7},{6,4},{7,5},{8,10},{9,11},{10,... | collective-permute-start | bytes 1425416 | tf_op jit(solution)/shard_map/ppermute | solution.py:71
  5.1 20.7 %collective-permute-start.1 = (bf16[64,3712]{1,0:T(8,128)(2,1)}, bf16[64,3712]{1,0:T(8,128)(2,1)S(1)}, u32[]{:S(2)}, u32[]{:S(2)}) collective-permute-start(bf16[64,3712]{1,0:T(8,128)(2,1)} %shard_map.109.refs_0_), channel_id=1, source_target_pairs={{0,8},{4,12},{8,0},{12,4},{16,24},{20,28},{24,16},{28,20},{1,9},{5... | collective-permute-start | bytes 1425416 | tf_op jit(solution)/shard_map/ppermute | solution.py:71
  6.5 19.2 %collective-permute-start.2 = (bf16[64,3712]{1,0:T(8,128)(2,1)}, bf16[64,3712]{1,0:T(8,128)(2,1)S(1)}, u32[]{:S(2)}, u32[]{:S(2)}) collective-permute-start(bf16[64,3712]{1,0:T(8,128)(2,1)} %shard_map.109.refs_0_), channel_id=1, source_target_pairs={{0,16},{4,20},{8,24},{12,28},{16,0},{20,4},{24,8},{28,12},{1,17},{... | collective-permute-start | bytes 1425416 | tf_op jit(solution)/shard_map/ppermute | solution.py:71
  25.8 15.8 %collective-permute-start.8 = (bf16[1,1024,3584]{2,1,0:T(8,128)(2,1)}, bf16[1,1024,3584]{2,1,0:T(8,128)(2,1)S(1)}, u32[]{:S(2)}, u32[]{:S(2)}) collective-permute-start(bf16[1,1024,3584]{2,1,0:T(8,128)(2,1)} %refs_11_.3), channel_id=1, source_target_pairs={{0,4},{4,0},{8,12},{12,8},{16,20},{20,16},{24,28},{28,24},{1,5},{5... | collective-permute-start | bytes 22020104 | tf_op jit(solution)/shard_map/ppermute | solution.py:71
  25.9 13.3 %collective-permute-start.5 = (bf16[64,3712]{1,0:T(8,128)(2,1)S(1)}, bf16[64,3712]{1,0:T(8,128)(2,1)S(1)}, u32[]{:S(2)}, u32[]{:S(2)}) collective-permute-start(bf16[64,3712]{1,0:T(8,128)(2,1)S(1)} %collective-permute-done.refs_4_), channel_id=1, source_target_pairs={{0,8},{4,12},{8,0},{12,4},{16,24},{20,28},{24,16},{28,20},{1,9},{5... | collective-permute-start | bytes 1425416 | tf_op jit(solution)/shard_map/ppermute | solution.py:71
  27.4 12.9 %collective-permute-start.6 = (bf16[64,3712]{1,0:T(8,128)(2,1)S(1)}, bf16[64,3712]{1,0:T(8,128)(2,1)S(1)}, u32[]{:S(2)}, u32[]{:S(2)}) collective-permute-start(bf16[64,3712]{1,0:T(8,128)(2,1)S(1)} %collective-permute-done.refs_4_), channel_id=1, source_target_pairs={{0,16},{4,20},{8,24},{12,28},{16,0},{20,4},{24,8},{28,12},{1,17},{... | collective-permute-start | bytes 1425416 | tf_op jit(solution)/shard_map/ppermute | solution.py:71
  41.6 13.9 %collective-permute-start.12 = (bf16[3584,512]{1,0:T(8,128)(2,1)S(1)}, bf16[3584,512]{1,0:T(8,128)(2,1)S(1)}, u32[]{:S(2)}, u32[]{:S(2)}) collective-permute-start(bf16[3584,512]{1,0:T(8,128)(2,1)S(1)} %pad_maximum_fusion), channel_id=1, source_target_pairs={{0,4},{4,0},{8,12},{12,8},{16,20},{20,16},{24,28},{28,24},{1,5},{5... | collective-permute-start | bytes 11010056 | tf_op jit(solution)/shard_map/ppermute | solution.py:71
  41.7 13.8 %collective-permute-start.13 = (bf16[256,3584]{1,0:T(8,128)(2,1)S(1)}, bf16[256,3584]{1,0:T(8,128)(2,1)S(1)}, u32[]{:S(2)}, u32[]{:S(2)}) collective-permute-start(bf16[256,3584]{1,0:T(8,128)(2,1)S(1)} %copy-done.8), channel_id=1, source_target_pairs={{0,4},{4,0},{8,12},{12,8},{16,20},{20,16},{24,28},{28,24},{1,5},{5... | collective-permute-start | bytes 5505032 | tf_op jit(solution)/shard_map/ppermute | solution.py:71
  42.2 12.9 %collective-permute-start.9 = (bf16[64,3712]{1,0:T(8,128)(2,1)S(1)}, bf16[64,3712]{1,0:T(8,128)(2,1)S(1)}, u32[]{:S(2)}, u32[]{:S(2)}) collective-permute-start(bf16[64,3712]{1,0:T(8,128)(2,1)S(1)} %collective-permute-done.6.refs_6_), channel_id=1, source_target_pairs={{0,8},{4,12},{8,0},{12,4},{16,24},{20,28},{24,16},{28,20},{1,9},{5... | collective-permute-start | bytes 1425416 | tf_op jit(solution)/shard_map/ppermute | solution.py:71
  55.6 28.7 %collective-permute-start.14 = (bf16[128,3712]{1,0:T(8,128)(2,1)S(1)}, bf16[128,3712]{1,0:T(8,128)(2,1)S(1)}, u32[]{:S(2)}, u32[]{:S(2)}) collective-permute-start(bf16[128,3712]{1,0:T(8,128)(2,1)S(1)} %constant_dynamic-update-slice_fusion), channel_id=1, source_target_pairs={{0,8},{4,12},{8,0},{12,4},{16,24},{20,28},{24,16},{28,20},{1,9},{5... | collective-permute-start | bytes 2850824 | tf_op jit(solution)/shard_map/ppermute | solution.py:71
  57.2 27.1 %collective-permute-start.15 = (bf16[128,3712]{1,0:T(8,128)(2,1)S(1)}, bf16[128,3712]{1,0:T(8,128)(2,1)S(1)}, u32[]{:S(2)}, u32[]{:S(2)}) collective-permute-start(bf16[128,3712]{1,0:T(8,128)(2,1)S(1)} %constant_dynamic-update-slice_fusion), channel_id=1, source_target_pairs={{0,16},{4,20},{8,24},{12,28},{16,0},{20,4},{24,8},{28,12},{1,17},{... | collective-permute-start | bytes 2850824 | tf_op jit(solution)/shard_map/ppermute | solution.py:71
  58.7 25.6 %collective-permute-start.16 = (bf16[64,3712]{1,0:T(8,128)(2,1)S(1)}, bf16[64,3712]{1,0:T(8,128)(2,1)S(1)}, u32[]{:S(2)}, u32[]{:S(2)}) collective-permute-start(bf16[64,3712]{1,0:T(8,128)(2,1)S(1)} %collective-permute-done.9.refs_7_), channel_id=1, source_target_pairs={{0,1},{1,0},{2,3},{3,2},{4,5},{5,4},{6,7},{7,6},{8,9},{9,8},{10,11... | collective-permute-start | bytes 1425416 | tf_op jit(solution)/shard_map/ppermute | solution.py:71
  60.0 24.3 %collective-permute-start.17 = (bf16[64,3712]{1,0:T(8,128)(2,1)S(1)}, bf16[64,3712]{1,0:T(8,128)(2,1)S(1)}, u32[]{:S(2)}, u32[]{:S(2)}) collective-permute-start(bf16[64,3712]{1,0:T(8,128)(2,1)S(1)} %collective-permute-done.10.refs_3_), channel_id=1, source_target_pairs={{0,1},{1,0},{2,3},{3,2},{4,5},{5,4},{6,7},{7,6},{8,9},{9,8},{10,11... | collective-permute-start | bytes 1425416 | tf_op jit(solution)/shard_map/ppermute | solution.py:71
  84.4 24.5 %collective-permute-start.18 = (bf16[64,3584]{1,0:T(8,128)(2,1)}, bf16[64,3584]{1,0:T(8,128)(2,1)S(1)}, u32[]{:S(2)}, u32[]{:S(2)}) collective-permute-start(bf16[64,3584]{1,0:T(8,128)(2,1)} %get-tuple-element.123), channel_id=1, source_target_pairs={{0,16},{4,20},{8,24},{12,28},{16,0},{20,4},{24,8},{28,12},{1,17},{... | collective-permute-start | bytes 1376264 | tf_op jit(solution)/shard_map/ppermute | solution.py:71
  85.0 23.9 %collective-permute-start.19 = (bf16[64,3584]{1,0:T(8,128)(2,1)}, bf16[64,3584]{1,0:T(8,128)(2,1)S(1)}, u32[]{:S(2)}, u32[]{:S(2)}) collective-permute-start(bf16[64,3584]{1,0:T(8,128)(2,1)} %get-tuple-element.124), channel_id=1, source_target_pairs={{0,8},{4,12},{8,0},{12,4},{16,24},{20,28},{24,16},{28,20},{1,9},{5... | collective-permute-start | bytes 1376264 | tf_op jit(solution)/shard_map/ppermute | solution.py:71
  85.5 23.4 %collective-permute-start.20 = (bf16[64,3584]{1,0:T(8,128)(2,1)}, bf16[64,3584]{1,0:T(8,128)(2,1)S(1)}, u32[]{:S(2)}, u32[]{:S(2)}) collective-permute-start(bf16[64,3584]{1,0:T(8,128)(2,1)} %get-tuple-element.125), channel_id=1, source_target_pairs={{0,16},{4,20},{8,24},{12,28},{16,0},{20,4},{24,8},{28,12},{1,17},{... | collective-permute-start | bytes 1376264 | tf_op jit(solution)/shard_map/ppermute | solution.py:71
  87.0 21.9 %collective-permute-start.21 = (bf16[64,3584]{1,0:T(8,128)(2,1)}, bf16[64,3584]{1,0:T(8,128)(2,1)S(1)}, u32[]{:S(2)}, u32[]{:S(2)}) collective-permute-start(bf16[64,3584]{1,0:T(8,128)(2,1)} %get-tuple-element.126), channel_id=1, source_target_pairs={{0,8},{4,12},{8,0},{12,4},{16,24},{20,28},{24,16},{28,20},{1,9},{5... | collective-permute-start | bytes 1376264 | tf_op jit(solution)/shard_map/ppermute | solution.py:71
  108.9 13.7 %collective-permute-start.22 = (bf16[64,3584]{1,0:T(8,128)(2,1)}, bf16[64,3584]{1,0:T(8,128)(2,1)S(1)}, u32[]{:S(2)}, u32[]{:S(2)}) collective-permute-start(bf16[64,3584]{1,0:T(8,128)(2,1)} %get-tuple-element.128), channel_id=1, source_target_pairs={{0,16},{4,20},{8,24},{12,28},{16,0},{20,4},{24,8},{28,12},{1,17},{... | collective-permute-start | bytes 1376264 | tf_op jit(solution)/shard_map/ppermute | solution.py:71
  109.5 13.7 %collective-permute-start.23 = (bf16[64,3584]{1,0:T(8,128)(2,1)}, bf16[64,3584]{1,0:T(8,128)(2,1)S(1)}, u32[]{:S(2)}, u32[]{:S(2)}) collective-permute-start(bf16[64,3584]{1,0:T(8,128)(2,1)} %get-tuple-element.129), channel_id=1, source_target_pairs={{0,8},{4,12},{8,0},{12,4},{16,24},{20,28},{24,16},{28,20},{1,9},{5... | collective-permute-start | bytes 1376264 | tf_op jit(solution)/shard_map/ppermute | solution.py:71
  110.1 18.6 %collective-permute-start.24 = (bf16[64,3584]{1,0:T(8,128)(2,1)S(1)}, bf16[64,3584]{1,0:T(8,128)(2,1)S(1)}, u32[]{:S(2)}, u32[]{:S(2)}) collective-permute-start(bf16[64,3584]{1,0:T(8,128)(2,1)S(1)} %add_convert_fusion.7), channel_id=1, source_target_pairs={{0,8},{4,12},{8,0},{12,4},{16,24},{20,28},{24,16},{28,20},{1,9},{5... | collective-permute-start | bytes 1376264 | tf_op jit(solution)/shard_map/ppermute | solution.py:71
  111.8 16.9 %collective-permute-start.25 = (bf16[64,3584]{1,0:T(8,128)(2,1)S(1)}, bf16[64,3584]{1,0:T(8,128)(2,1)S(1)}, u32[]{:S(2)}, u32[]{:S(2)}) collective-permute-start(bf16[64,3584]{1,0:T(8,128)(2,1)S(1)} %add_convert_fusion.6), channel_id=1, source_target_pairs={{0,16},{4,20},{8,24},{12,28},{16,0},{20,4},{24,8},{28,12},{1,17},{... | collective-permute-start | bytes 1376264 | tf_op jit(solution)/shard_map/ppermute | solution.py:71
  145.8 15.1 %collective-permute-start.29 = (bf16[64,3584]{1,0:T(8,128)(2,1)S(1)}, bf16[64,3584]{1,0:T(8,128)(2,1)S(1)}, u32[]{:S(2)}, u32[]{:S(2)}) collective-permute-start(bf16[64,3584]{1,0:T(8,128)(2,1)S(1)} %add_convert_fusion.2), channel_id=1, source_target_pairs={{0,3},{1,2},{2,1},{3,0},{4,7},{5,6},{6,5},{7,4},{8,11},{9,10},{10,... | collective-permute-start | bytes 1376264 | tf_op jit(solution)/shard_map/ppermute | solution.py:71
  (36 other events, 756.6 us)

commit v6 on v5

--- a/solution.py
+++ b/solution.py
@@ -110,7 +110,7 @@
 
 
 def expert_body(dims, *refs):
-    lows, block, most, width, hidden, shared_hidden, tile, span, ring = dims
+    lows, packed, block, most, width, hidden, shared_hidden, tile, span, ring = dims
     pieces_of = 4
     sides = len(lows) // pieces_of
     rows = pieces_of * block
@@ -126,8 +126,9 @@
     (before_ref,) = take(1)
     experts = [take(3), take(3)]
     shared = [take(3), take(3)] if shared_hidden else []
-    take(len(refs) - 15 - sides * pieces_of)
-    outs = take(sides * pieces_of)
+    outs_of = pieces_of if packed else sides * pieces_of
+    take(len(refs) - 15 - outs_of)
+    outs = take(outs_of)
     held, chosen, gate, up, down, down_s, act, act_s, back, result = take(10)
     piece_sem, step_sem, span_sem, span_s_sem, out_sem = take(5)
     copy = pltpu.make_async_copy
@@ -165,11 +166,13 @@
         ]
 
     def out_copy(side, piece, k):
-        return copy(
-            result.at[side, k, pl.ds(piece * block, block), :],
-            outs[side * pieces_of + piece].at[:, pl.ds(k * span, span)],
-            out_sem.at[side, piece, k],
-        )
+        columns = pl.ds(k * span, span)
+        if packed:
+            out = outs[piece].at[pl.ds(side * block, block), columns]
+        else:
+            out = outs[side * pieces_of + piece].at[:, columns]
+        rows_of = pl.ds(piece * block, block)
+        return copy(result.at[side, k, rows_of, :], out, out_sem.at[side, piece, k])
 
     def start(copies):
         for one in copies:
@@ -264,7 +267,7 @@
     )
 
 
-def run_experts(sides, block, most, experts, shared, after=()):
+def run_experts(sides, block, most, experts, shared, packed, after=()):
     wide = sides[0][0][0].shape[1]
     width, hidden = wide - LANES, experts[0][0].shape[2]
     shared_hidden = shared[0][0].shape[1] if shared else 0
@@ -272,7 +275,7 @@
     number, pieces_of = len(sides), len(sides[0])
     rows, slots = pieces_of * block, pieces_of * most
     lows = tuple(at * block for side in sides for _, at in side)
-    dims = (lows, block, most, width, hidden, shared_hidden, tile, span, ring)
+    dims = (lows, packed, block, most, width, hidden, shared_hidden, tile, span, ring)
     bf16 = jnp.bfloat16
     vmem, sems = pltpu.VMEM, pltpu.SemaphoreType.DMA
     shared_rows = shared_hidden or 16
@@ -306,11 +309,13 @@
     operands = [part if part is before else in_hbm(part) for part in operands]
     return pl.pallas_call(
         functools.partial(expert_body, dims),
-        out_shape=[pltpu.HBM((block, width), bf16)] * (number * pieces_of),
+        out_shape=[pltpu.HBM((block * number, width), bf16)] * pieces_of
+        if packed
+        else [pltpu.HBM((block, width), bf16)] * (number * pieces_of),
         in_specs=[
             pl.BlockSpec(memory_space=pltpu.VMEM if part is before else pl.ANY) for part in operands
         ],
-        out_specs=[pl.BlockSpec(memory_space=pl.ANY)] * (number * pieces_of),
+        out_specs=[pl.BlockSpec(memory_space=pl.ANY)] * (pieces_of * (1 if packed else number)),
         scratch_shapes=scratch,
         compiler_params=pltpu.CompilerParams(vmem_limit_bytes=VMEM_LIMIT),
         cost_estimate=pl.CostEstimate(flops=flops, bytes_accessed=moved, transcendentals=0),
@@ -361,31 +366,28 @@
     pair31 = jnp.concatenate([z3, z1], axis=0)
     r31, d31, a3, a1 = right(pair31), down(pair31), far(a2, 1), far(a0, 1)
     sides = [[(own, 0), (r0, 0), (d0, 0), (a0, 0)], [(z2, 0), (r2, 0), (d2, 0), (a2, 0)]]
-    out = run_experts(sides, block, most, experts, shared)
+    out = run_experts(sides, block, most, experts, shared, True)
     out, (r31, d31, a3, a1) = pin(out, (r31, d31, a3, a1))
-    sum0, sum2 = out[:4], out[4:]
-    sent0, sent2, plain0, plain2 = down(sum0[3]), right(sum2[3]), down(sum0[2]), right(sum2[1])
-    sides = [[(z3, 0), (r31, 0), (d31, 0), (a3, 0)], [(z1, 0), (r31, 1), (d31, 1), (a1, 0)]]
-    out = run_experts(sides, block, most, experts, [], (sum0[0],))
-    out, (across0, across2, plain0, plain2) = pin(out, (sent0, sent2, plain0, plain2))
-    sum3, sum1 = out[:4], out[4:]
-    across3, across1 = down(sum3[3]), right(sum1[3])
-    full0, full2 = add_rows(sum0[1], across0), add_rows(sum2[2], across2)
-    full0, full2 = right(full0), down(full2)
-    across3, across1, full0, full2, plain3, plain1 = tie(
-        (across3, across1, full0, full2, sum3[2], sum1[1])
-    )
-    hop2 = far(add_rows(sum2[0], plain2, full2), 1)
+    sums = out[0]
+    from_right, from_down, from_far = right(out[1]), down(out[2]), far(out[3], 1)
+    sides = [[(z1, 0), (r31, 1), (d31, 1), (a1, 0)], [(z3, 0), (r31, 0), (d31, 0), (a3, 0)]]
+    out = run_experts(sides, block, most, experts, [], False, (sums,))
+    out, (from_right, from_down, from_far) = pin(out, (from_right, from_down, from_far))
+    sum1, sum3 = out[:4], out[4:]
+    across3 = down(add_rows(sum3[3], from_far[block:]))
+    across1 = right(add_rows(sum1[3], from_far[:block]))
+    hop2 = far(add_rows(sums[block:], from_right[block:], from_down[block:]), 1)
+    across3, across1, hop2, plain3, plain1 = tie((across3, across1, hop2, sum3[2], sum1[1]))
     full3, full1 = add_rows(sum3[1], across3), add_rows(sum1[2], across1)
     full3, plain3, plain1, full1 = tie((full3, plain3, plain1, full1))
     full3, plain3 = right(full3), down(plain3)
-    full3, plain3, hop2, full1, plain1 = tie((full3, plain3, hop2, full1, plain1))
+    full3, plain3, full1, plain1 = tie((full3, plain3, full1, plain1))
     full1, plain1 = down(full1), right(plain1)
     part3 = add_rows(sum3[0], plain3, full3, hop2)
     back3 = far(part3, 3)
     part1 = add_rows(sum1[0], plain1, full1)
     back1 = far(part1, 1)
-    total = add_rows(sum0[0], plain0, full0, back3, dtype=jnp.float32)
+    total = add_rows(sums[:block], from_right[:block], from_down[:block], back3, dtype=jnp.float32)
     return add_rows(total, back1)
 
 

time: 167 us -> 157 us (0.940)
  starting transfers between devices: 39.1 us -> 30.2 us
  waiting for transfers between devices: 74.6 us -> 72 us
    ppermute x33 -> x30, starting transfers between devices: 39.1 us -> 30.2 us  [swap(): return lax.ppermute(value, axis, [(i, i ^ mask) for i in range(size)])]
    ppermute x33 -> x30, waiting for transfers between devices: 74.6 us -> 72 us  [swap(): return lax.ppermute(value, axis, [(i, i ^ mask) for i in range(size)])]
    convert_element_type x7 -> x6, other arithmetic: 3.2 us -> 3.36 us  [add_rows(): return total.astype(dtype)]
  transfers between devices with their start and end apart: 33 -> 30, of which waited for: 16 -> 15; matrix products, arithmetic and copies ran while one was open for 2% -> 2% of each run, Pallas kernels for 28% -> 30%
where the time goes in v6:
time: 157 us; the launch traced here: 154 us
  waiting for transfers between devices  72 us (46%)
  Pallas kernels  45.6 us (29%)
  starting transfers between devices  30.2 us (19%)
  other arithmetic  5.67 us (4%)
    ppermute x30, waiting for transfers between devices, swap(): return lax.ppermute(value, axis, [(i, i ^ mask) for i in range(size)])  72 us
    pallas_call x2, Pallas kernels, run_experts(): pl.pallas_call(functools.partial(expert_body, dims), out_shape=[pltpu.HBM...  43.7 us
    ppermute x30, starting transfers between devices, swap(): return lax.ppermute(value, axis, [(i, i ^ mask) for i in range(size)])  30.2 us
    convert_element_type x6, other arithmetic, add_rows(): return total.astype(dtype)  3.36 us
  transfers between devices with their start and end apart: 30, of which 15 were waited for; matrix products, arithmetic and copies ran while one was open for 2% of the time, Pallas kernels for 30%

profile of v6, /device:TPU:8, one launch (start us, length us, event | category | flops | bytes accessed | tf_op | source)
XLA Modules:
  0.0 154.1 jit_solution(17420876449514385655)
XLA Ops:
  0.5 1.9 %shard_map.109.refs_0_ = bf16[64,3712]{1,0:T(8,128)(2,1)} custom-call(bf16[64,3584]{1,0:T(8,128)(2,1)} %tokens.1, s32[8,64]{1,0:T(8,128)} %bitcast.2, bf16[8,64]{1,0:T(8,128)(2,1)} %bitcast.3), custom_call_target="tpu_custom_call" | custom-call | tf_op jit(solution)/shard_map/pallas_call | solution.py:106
  2.4 2.6 %collective-permute-start = (bf16[64,3712]{1,0:T(8,128)(2,1)}, bf16[64,3712]{1,0:T(8,128)(2,1)S(1)}, u32[]{:S(2)}, u32[]{:S(2)}) collective-permute-start(bf16[64,3712]{1,0:T(8,128)(2,1)} %shard_map.109.refs_0_), channel_id=1, source_target_pairs={{0,2},{1,3},{2,0},{3,1},{4,6},{5,7},{6,4},{7,5},{8,10},{9,11},{10,... | collective-permute-start | bytes 1425416 | tf_op jit(solution)/shard_map/ppermute | solution.py:71
  5.0 1.5 collective-permute-start.1
  6.5 1.5 collective-permute-start.2
  8.0 2.3 %pad_maximum_fusion = bf16[3584,512]{1,0:T(8,128)(2,1)S(1)} fusion(bf16[3584,256]{1,0:T(8,128)(2,1)} %refs_16_.1, bf16[3584,256]{1,0:T(8,128)(2,1)} %refs_15_.1), kind=kLoop, calls=%fused_computation | loop fusion | flops 7340032 | bytes 7340032 | tf_op jit(solution)/shard_map/concatenate | solution.py:352
  10.4 15.4 %collective-permute-done.refs_4_ = bf16[64,3712]{1,0:T(8,128)(2,1)S(1)} collective-permute-done((bf16[64,3712]{1,0:T(8,128)(2,1)}, bf16[64,3712]{1,0:T(8,128)(2,1)S(1)}, u32[]{:S(2)}, u32[]{:S(2)}) %collective-permute-start) | collective-permute-done | bytes 475168 | tf_op jit(solution)/shard_map/ppermute | solution.py:71
  25.8 1.5 %collective-permute-start.5 = (bf16[64,3712]{1,0:T(8,128)(2,1)S(1)}, bf16[64,3712]{1,0:T(8,128)(2,1)S(1)}, u32[]{:S(2)}, u32[]{:S(2)}) collective-permute-start(bf16[64,3712]{1,0:T(8,128)(2,1)S(1)} %collective-permute-done.refs_4_), channel_id=1, source_target_pairs={{0,8},{4,12},{8,0},{12,4},{16,24},{20,28},{24,16},{28,20},{1,9},{5... | collective-permute-start | bytes 1425416 | tf_op jit(solution)/shard_map/ppermute | solution.py:71
  27.4 1.5 collective-permute-start.6
  30.2 9.0 %collective-permute-done.5.refs_5_ = bf16[64,3712]{1,0:T(8,128)(2,1)S(1)} collective-permute-done((bf16[64,3712]{1,0:T(8,128)(2,1)S(1)}, bf16[64,3712]{1,0:T(8,128)(2,1)S(1)}, u32[]{:S(2)}, u32[]{:S(2)}) %collective-permute-start.5) | collective-permute-done | bytes 475168 | tf_op jit(solution)/shard_map/ppermute | solution.py:71
  44.4 10.6 %collective-permute-done.9.refs_7_ = bf16[64,3712]{1,0:T(8,128)(2,1)S(1)} collective-permute-done((bf16[64,3712]{1,0:T(8,128)(2,1)S(1)}, bf16[64,3712]{1,0:T(8,128)(2,1)S(1)}, u32[]{:S(2)}, u32[]{:S(2)}) %collective-permute-start.9) | collective-permute-done | bytes 475168 | tf_op jit(solution)/shard_map/ppermute | solution.py:71
  55.6 1.6 %collective-permute-start.14 = (bf16[128,3712]{1,0:T(8,128)(2,1)S(1)}, bf16[128,3712]{1,0:T(8,128)(2,1)S(1)}, u32[]{:S(2)}, u32[]{:S(2)}) collective-permute-start(bf16[128,3712]{1,0:T(8,128)(2,1)S(1)} %constant_dynamic-update-slice_fusion), channel_id=1, source_target_pairs={{0,8},{4,12},{8,0},{12,4},{16,24},{20,28},{24,16},{28,20},{1,9},{5... | collective-permute-start | bytes 2850824 | tf_op jit(solution)/shard_map/ppermute | solution.py:71
  57.2 1.5 collective-permute-start.15
  60.8 23.5 %shard_map.110 = (bf16[128,3584]{1,0:T(8,128)(2,1)}, bf16[128,3584]{1,0:T(8,128)(2,1)}, bf16[128,3584]{1,0:T(8,128)(2,1)}, bf16[128,3584]{1,0:T(8,128)(2,1)}) custom-call(bf16[64,3712]{1,0:T(8,128)(2,1)} %shard_map.109.refs_0_, bf16[64,3712]{1,0:T(8,128)(2,1)} %copy-done.12, bf16[64,3712]{1,0:T(8,128)(2,1)} %copy-done.13, bf16[64,3712]{1,0:T(8,128)(2,1)} %copy-done.17, ...), custom_call_target="tpu_custom_call" | custom-call | flops 15971909632 | bytes 66330624 | tf_op jit(solution)/shard_map/pallas_call | solution.py:310
  86.8 20.2 %shard_map.111 = (bf16[64,3584]{1,0:T(8,128)(2,1)}, bf16[64,3584]{1,0:T(8,128)(2,1)}, bf16[64,3584]{1,0:T(8,128)(2,1)}, bf16[64,3584]{1,0:T(8,128)(2,1)}, bf16[6...) custom-call(bf16[64,3712]{1,0:T(8,128)(2,1)} %copy-done.8, ...), custom_call_target="tpu_custom_call" | custom-call | flops 13153337344 | bytes 53551104 | tf_op jit(solution)/shard_map/pallas_call | solution.py:310
  107.1 1.5 %add_convert_fusion.6 = (bf16[64,3584]{1,0:T(8,128)(2,1)S(1)}, bf16[64,3584]{1,0:T(8,128)(2,1)S(1)}) fusion(bf16[64,3584]{1,0:T(8,128)(2,1)} %get-tuple-element.117, bf16[128,3584]{1,0:T(8,128)(2,1)S(1)} %collective-permute-done.20, bf16[64,3584]{1,0:T(8,128)(2,1)} %get-tuple-element.115), kind=kLoop, calls=%fused_computation.7 | loop fusion | flops 1835008 | bytes 2752512 | tf_op jit(solution)/shard_map/convert_element_type | solution.py:82
  108.6 1.6 %collective-permute-start.21 = (bf16[64,3584]{1,0:T(8,128)(2,1)S(1)}, bf16[64,3584]{1,0:T(8,128)(2,1)S(1)}, u32[]{:S(2)}, u32[]{:S(2)}) collective-permute-start(bf16[64,3584]{1,0:T(8,128)(2,1)S(1)} %get-tuple-element.136), channel_id=1, source_target_pairs={{0,16},{4,20},{8,24},{12,28},{16,0},{20,4},{24,8},{28,12},{1,17},{... | collective-permute-start | bytes 1376264 | tf_op jit(solution)/shard_map/ppermute | solution.py:71
  110.2 1.5 collective-permute-start.22
  112.8 5.3 %collective-permute-done.21 = bf16[64,3584]{1,0:T(8,128)(2,1)S(1)} collective-permute-done((bf16[64,3584]{1,0:T(8,128)(2,1)S(1)}, bf16[64,3584]{1,0:T(8,128)(2,1)S(1)}, u32[]{:S(2)}, u32[]{:S(2)}) %collective-permute-start.21) | collective-permute-done | bytes 458784 | tf_op jit(solution)/shard_map/ppermute | solution.py:71
  122.5 9.1 %collective-permute-done.24 = bf16[64,3584]{1,0:T(8,128)(2,1)S(1)} collective-permute-done((bf16[64,3584]{1,0:T(8,128)(2,1)S(1)}, bf16[64,3584]{1,0:T(8,128)(2,1)S(1)}, u32[]{:S(2)}, u32[]{:S(2)}) %collective-permute-start.24) | collective-permute-done | bytes 458784 | tf_op jit(solution)/shard_map/ppermute | solution.py:71
  131.6 3.4 %collective-permute-done.25 = bf16[64,3584]{1,0:T(8,128)(2,1)S(1)} collective-permute-done((bf16[64,3584]{1,0:T(8,128)(2,1)S(1)}, bf16[64,3584]{1,0:T(8,128)(2,1)S(1)}, u32[]{:S(2)}, u32[]{:S(2)}) %collective-permute-start.25) | collective-permute-done | bytes 458784 | tf_op jit(solution)/shard_map/ppermute | solution.py:71
  135.5 2.7 %collective-permute-start.26 = (bf16[64,3584]{1,0:T(8,128)(2,1)S(1)}, bf16[64,3584]{1,0:T(8,128)(2,1)S(1)}, u32[]{:S(2)}, u32[]{:S(2)}) collective-permute-start(bf16[64,3584]{1,0:T(8,128)(2,1)S(1)} %add_convert_fusion.2), channel_id=1, source_target_pairs={{0,3},{1,2},{2,1},{3,0},{4,7},{5,6},{6,5},{7,4},{8,11},{9,10},{10,... | collective-permute-start | bytes 1376264 | tf_op jit(solution)/shard_map/ppermute | solution.py:71
  138.1 5.4 %collective-permute-done.28 = bf16[64,3584]{1,0:T(8,128)(2,1)S(1)} collective-permute-done((bf16[64,3584]{1,0:T(8,128)(2,1)S(1)}, bf16[64,3584]{1,0:T(8,128)(2,1)S(1)}, u32[]{:S(2)}, u32[]{:S(2)}) %collective-permute-start.28) | collective-permute-done | bytes 458784 | tf_op jit(solution)/shard_map/ppermute | solution.py:71
  144.5 4.8 %collective-permute-done.26 = bf16[64,3584]{1,0:T(8,128)(2,1)S(1)} collective-permute-done((bf16[64,3584]{1,0:T(8,128)(2,1)S(1)}, bf16[64,3584]{1,0:T(8,128)(2,1)S(1)}, u32[]{:S(2)}, u32[]{:S(2)}) %collective-permute-start.26) | collective-permute-done | bytes 458784 | tf_op jit(solution)/shard_map/ppermute | solution.py:71
  149.4 3.7 %collective-permute-done.29 = bf16[64,3584]{1,0:T(8,128)(2,1)S(1)} collective-permute-done((bf16[64,3584]{1,0:T(8,128)(2,1)S(1)}, bf16[64,3584]{1,0:T(8,128)(2,1)S(1)}, u32[]{:S(2)}, u32[]{:S(2)}) %collective-permute-start.29) | collective-permute-done | bytes 458784 | tf_op jit(solution)/shard_map/ppermute | solution.py:71
  (100 shorter events, 20.1 us)
Async XLA Ops:
  0.0 25.7 %collective-permute-start.3 = (bf16[1,3584,1024]{2,1,0:T(8,128)(2,1)}, bf16[1,3584,1024]{2,1,0:T(8,128)(2,1)}, u32[]{:S(2)}, u32[]{:S(2)}) collective-permute-start(bf16[1,3584,1024]{2,1,0:T(8,128)(2,1)} %refs_9_.3), channel_id=1, source_target_pairs={{0,4},{4,0},{8,12},{12,8},{16,20},{20,16},{24,28},{28,24},{1,5},{5... | collective-permute-start | bytes 22020104 | tf_op jit(solution)/shard_map/ppermute | solution.py:71
  0.0 25.7 %collective-permute-start.4 = (bf16[1,3584,1024]{2,1,0:T(8,128)(2,1)}, bf16[1,3584,1024]{2,1,0:T(8,128)(2,1)}, u32[]{:S(2)}, u32[]{:S(2)}) collective-permute-start(bf16[1,3584,1024]{2,1,0:T(8,128)(2,1)} %refs_10_.3), channel_id=1, source_target_pairs={{0,4},{4,0},{8,12},{12,8},{16,20},{20,16},{24,28},{28,24},{1,5},{5... | collective-permute-start | bytes 22020104 | tf_op jit(solution)/shard_map/ppermute | solution.py:71
  2.4 23.3 %collective-permute-start = (bf16[64,3712]{1,0:T(8,128)(2,1)}, bf16[64,3712]{1,0:T(8,128)(2,1)S(1)}, u32[]{:S(2)}, u32[]{:S(2)}) collective-permute-start(bf16[64,3712]{1,0:T(8,128)(2,1)} %shard_map.109.refs_0_), channel_id=1, source_target_pairs={{0,2},{1,3},{2,0},{3,1},{4,6},{5,7},{6,4},{7,5},{8,10},{9,11},{10,... | collective-permute-start | bytes 1425416 | tf_op jit(solution)/shard_map/ppermute | solution.py:71
  5.0 20.7 %collective-permute-start.1 = (bf16[64,3712]{1,0:T(8,128)(2,1)}, bf16[64,3712]{1,0:T(8,128)(2,1)S(1)}, u32[]{:S(2)}, u32[]{:S(2)}) collective-permute-start(bf16[64,3712]{1,0:T(8,128)(2,1)} %shard_map.109.refs_0_), channel_id=1, source_target_pairs={{0,8},{4,12},{8,0},{12,4},{16,24},{20,28},{24,16},{28,20},{1,9},{5... | collective-permute-start | bytes 1425416 | tf_op jit(solution)/shard_map/ppermute | solution.py:71
  6.5 19.2 %collective-permute-start.2 = (bf16[64,3712]{1,0:T(8,128)(2,1)}, bf16[64,3712]{1,0:T(8,128)(2,1)S(1)}, u32[]{:S(2)}, u32[]{:S(2)}) collective-permute-start(bf16[64,3712]{1,0:T(8,128)(2,1)} %shard_map.109.refs_0_), channel_id=1, source_target_pairs={{0,16},{4,20},{8,24},{12,28},{16,0},{20,4},{24,8},{28,12},{1,17},{... | collective-permute-start | bytes 1425416 | tf_op jit(solution)/shard_map/ppermute | solution.py:71
  25.8 15.8 %collective-permute-start.8 = (bf16[1,1024,3584]{2,1,0:T(8,128)(2,1)}, bf16[1,1024,3584]{2,1,0:T(8,128)(2,1)S(1)}, u32[]{:S(2)}, u32[]{:S(2)}) collective-permute-start(bf16[1,1024,3584]{2,1,0:T(8,128)(2,1)} %refs_11_.3), channel_id=1, source_target_pairs={{0,4},{4,0},{8,12},{12,8},{16,20},{20,16},{24,28},{28,24},{1,5},{5... | collective-permute-start | bytes 22020104 | tf_op jit(solution)/shard_map/ppermute | solution.py:71
  25.8 13.3 %collective-permute-start.5 = (bf16[64,3712]{1,0:T(8,128)(2,1)S(1)}, bf16[64,3712]{1,0:T(8,128)(2,1)S(1)}, u32[]{:S(2)}, u32[]{:S(2)}) collective-permute-start(bf16[64,3712]{1,0:T(8,128)(2,1)S(1)} %collective-permute-done.refs_4_), channel_id=1, source_target_pairs={{0,8},{4,12},{8,0},{12,4},{16,24},{20,28},{24,16},{28,20},{1,9},{5... | collective-permute-start | bytes 1425416 | tf_op jit(solution)/shard_map/ppermute | solution.py:71
  27.4 12.9 %collective-permute-start.6 = (bf16[64,3712]{1,0:T(8,128)(2,1)S(1)}, bf16[64,3712]{1,0:T(8,128)(2,1)S(1)}, u32[]{:S(2)}, u32[]{:S(2)}) collective-permute-start(bf16[64,3712]{1,0:T(8,128)(2,1)S(1)} %collective-permute-done.refs_4_), channel_id=1, source_target_pairs={{0,16},{4,20},{8,24},{12,28},{16,0},{20,4},{24,8},{28,12},{1,17},{... | collective-permute-start | bytes 1425416 | tf_op jit(solution)/shard_map/ppermute | solution.py:71
  28.9 12.7 %collective-permute-start.7 = (bf16[64,3712]{1,0:T(8,128)(2,1)S(1)}, bf16[64,3712]{1,0:T(8,128)(2,1)S(1)}, u32[]{:S(2)}, u32[]{:S(2)}) collective-permute-start(bf16[64,3712]{1,0:T(8,128)(2,1)S(1)} %collective-permute-done.refs_4_), channel_id=1, source_target_pairs={{0,1},{1,0},{2,3},{3,2},{4,5},{5,4},{6,7},{7,6},{8,9},{9,8},{10,11... | collective-permute-start | bytes 1425416 | tf_op jit(solution)/shard_map/ppermute | solution.py:71
  41.6 13.9 %collective-permute-start.12 = (bf16[3584,512]{1,0:T(8,128)(2,1)S(1)}, bf16[3584,512]{1,0:T(8,128)(2,1)S(1)}, u32[]{:S(2)}, u32[]{:S(2)}) collective-permute-start(bf16[3584,512]{1,0:T(8,128)(2,1)S(1)} %pad_maximum_fusion), channel_id=1, source_target_pairs={{0,4},{4,0},{8,12},{12,8},{16,20},{20,16},{24,28},{28,24},{1,5},{5... | collective-permute-start | bytes 11010056 | tf_op jit(solution)/shard_map/ppermute | solution.py:71
  41.7 13.8 %collective-permute-start.13 = (bf16[256,3584]{1,0:T(8,128)(2,1)S(1)}, bf16[256,3584]{1,0:T(8,128)(2,1)S(1)}, u32[]{:S(2)}, u32[]{:S(2)}) collective-permute-start(bf16[256,3584]{1,0:T(8,128)(2,1)S(1)} %copy-done.9), channel_id=1, source_target_pairs={{0,4},{4,0},{8,12},{12,8},{16,20},{20,16},{24,28},{28,24},{1,5},{5... | collective-permute-start | bytes 5505032 | tf_op jit(solution)/shard_map/ppermute | solution.py:71
  42.2 12.9 %collective-permute-start.9 = (bf16[64,3712]{1,0:T(8,128)(2,1)S(1)}, bf16[64,3712]{1,0:T(8,128)(2,1)S(1)}, u32[]{:S(2)}, u32[]{:S(2)}) collective-permute-start(bf16[64,3712]{1,0:T(8,128)(2,1)S(1)} %collective-permute-done.6.refs_6_), channel_id=1, source_target_pairs={{0,8},{4,12},{8,0},{12,4},{16,24},{20,28},{24,16},{28,20},{1,9},{5... | collective-permute-start | bytes 1425416 | tf_op jit(solution)/shard_map/ppermute | solution.py:71
  42.7 12.6 %collective-permute-start.10 = (bf16[64,3712]{1,0:T(8,128)(2,1)S(1)}, bf16[64,3712]{1,0:T(8,128)(2,1)S(1)}, u32[]{:S(2)}, u32[]{:S(2)}) collective-permute-start(bf16[64,3712]{1,0:T(8,128)(2,1)S(1)} %collective-permute-done.1.refs_1_), channel_id=1, source_target_pairs={{0,16},{4,20},{8,24},{12,28},{16,0},{20,4},{24,8},{28,12},{1,17},{... | collective-permute-start | bytes 1425416 | tf_op jit(solution)/shard_map/ppermute | solution.py:71
  43.2 12.3 %collective-permute-start.11 = (bf16[64,3712]{1,0:T(8,128)(2,1)S(1)}, bf16[64,3712]{1,0:T(8,128)(2,1)S(1)}, u32[]{:S(2)}, u32[]{:S(2)}) collective-permute-start(bf16[64,3712]{1,0:T(8,128)(2,1)S(1)} %copy-done.6), channel_id=1, source_target_pairs={{0,1},{1,0},{2,3},{3,2},{4,5},{5,4},{6,7},{7,6},{8,9},{9,8},{10,11... | collective-permute-start | bytes 1425416 | tf_op jit(solution)/shard_map/ppermute | solution.py:71
  55.6 28.8 %collective-permute-start.14 = (bf16[128,3712]{1,0:T(8,128)(2,1)S(1)}, bf16[128,3712]{1,0:T(8,128)(2,1)S(1)}, u32[]{:S(2)}, u32[]{:S(2)}) collective-permute-start(bf16[128,3712]{1,0:T(8,128)(2,1)S(1)} %constant_dynamic-update-slice_fusion), channel_id=1, source_target_pairs={{0,8},{4,12},{8,0},{12,4},{16,24},{20,28},{24,16},{28,20},{1,9},{5... | collective-permute-start | bytes 2850824 | tf_op jit(solution)/shard_map/ppermute | solution.py:71
  57.2 27.2 %collective-permute-start.15 = (bf16[128,3712]{1,0:T(8,128)(2,1)S(1)}, bf16[128,3712]{1,0:T(8,128)(2,1)S(1)}, u32[]{:S(2)}, u32[]{:S(2)}) collective-permute-start(bf16[128,3712]{1,0:T(8,128)(2,1)S(1)} %constant_dynamic-update-slice_fusion), channel_id=1, source_target_pairs={{0,16},{4,20},{8,24},{12,28},{16,0},{20,4},{24,8},{28,12},{1,17},{... | collective-permute-start | bytes 2850824 | tf_op jit(solution)/shard_map/ppermute | solution.py:71
  58.7 25.6 %collective-permute-start.16 = (bf16[64,3712]{1,0:T(8,128)(2,1)S(1)}, bf16[64,3712]{1,0:T(8,128)(2,1)S(1)}, u32[]{:S(2)}, u32[]{:S(2)}) collective-permute-start(bf16[64,3712]{1,0:T(8,128)(2,1)S(1)} %collective-permute-done.9.refs_7_), channel_id=1, source_target_pairs={{0,1},{1,0},{2,3},{3,2},{4,5},{5,4},{6,7},{7,6},{8,9},{9,8},{10,11... | collective-permute-start | bytes 1425416 | tf_op jit(solution)/shard_map/ppermute | solution.py:71
  59.9 24.4 %collective-permute-start.17 = (bf16[64,3712]{1,0:T(8,128)(2,1)S(1)}, bf16[64,3712]{1,0:T(8,128)(2,1)S(1)}, u32[]{:S(2)}, u32[]{:S(2)}) collective-permute-start(bf16[64,3712]{1,0:T(8,128)(2,1)S(1)} %collective-permute-done.10.refs_3_), channel_id=1, source_target_pairs={{0,1},{1,0},{2,3},{3,2},{4,5},{5,4},{6,7},{7,6},{8,9},{9,8},{10,11... | collective-permute-start | bytes 1425416 | tf_op jit(solution)/shard_map/ppermute | solution.py:71
  84.4 22.6 %collective-permute-start.18 = (bf16[128,3584]{1,0:T(8,128)(2,1)}, bf16[128,3584]{1,0:T(8,128)(2,1)S(1)}, u32[]{:S(2)}, u32[]{:S(2)}) collective-permute-start(bf16[128,3584]{1,0:T(8,128)(2,1)} %get-tuple-element.108), channel_id=1, source_target_pairs={{0,8},{4,12},{8,0},{12,4},{16,24},{20,28},{24,16},{28,20},{1,9},{5... | collective-permute-start | bytes 2752520 | tf_op jit(solution)/shard_map/ppermute | solution.py:71
  85.0 22.0 %collective-permute-start.19 = (bf16[128,3584]{1,0:T(8,128)(2,1)}, bf16[128,3584]{1,0:T(8,128)(2,1)S(1)}, u32[]{:S(2)}, u32[]{:S(2)}) collective-permute-start(bf16[128,3584]{1,0:T(8,128)(2,1)} %get-tuple-element.109), channel_id=1, source_target_pairs={{0,16},{4,20},{8,24},{12,28},{16,0},{20,4},{24,8},{28,12},{1,17},{... | collective-permute-start | bytes 2752520 | tf_op jit(solution)/shard_map/ppermute | solution.py:71
  85.5 21.5 %collective-permute-start.20 = (bf16[128,3584]{1,0:T(8,128)(2,1)}, bf16[128,3584]{1,0:T(8,128)(2,1)S(1)}, u32[]{:S(2)}, u32[]{:S(2)}) collective-permute-start(bf16[128,3584]{1,0:T(8,128)(2,1)} %get-tuple-element.110), channel_id=1, source_target_pairs={{0,1},{1,0},{2,3},{3,2},{4,5},{5,4},{6,7},{7,6},{8,9},{9,8},{10,11... | collective-permute-start | bytes 2752520 | tf_op jit(solution)/shard_map/ppermute | solution.py:71
  120.7 10.9 %collective-permute-start.24 = (bf16[64,3584]{1,0:T(8,128)(2,1)S(1)}, bf16[64,3584]{1,0:T(8,128)(2,1)S(1)}, u32[]{:S(2)}, u32[]{:S(2)}) collective-permute-start(bf16[64,3584]{1,0:T(8,128)(2,1)S(1)} %get-tuple-element.125), channel_id=1, source_target_pairs={{0,8},{4,12},{8,0},{12,4},{16,24},{20,28},{24,16},{28,20},{1,9},{5... | collective-permute-start | bytes 1376264 | tf_op jit(solution)/shard_map/ppermute | solution.py:71
  122.2 12.8 %collective-permute-start.25 = (bf16[64,3584]{1,0:T(8,128)(2,1)S(1)}, bf16[64,3584]{1,0:T(8,128)(2,1)S(1)}, u32[]{:S(2)}, u32[]{:S(2)}) collective-permute-start(bf16[64,3584]{1,0:T(8,128)(2,1)S(1)} %copy-done.25), channel_id=1, source_target_pairs={{0,16},{4,20},{8,24},{12,28},{16,0},{20,4},{24,8},{28,12},{1,17},{... | collective-permute-start | bytes 1376264 | tf_op jit(solution)/shard_map/ppermute | solution.py:71
  135.5 13.9 %collective-permute-start.26 = (bf16[64,3584]{1,0:T(8,128)(2,1)S(1)}, bf16[64,3584]{1,0:T(8,128)(2,1)S(1)}, u32[]{:S(2)}, u32[]{:S(2)}) collective-permute-start(bf16[64,3584]{1,0:T(8,128)(2,1)S(1)} %add_convert_fusion.2), channel_id=1, source_target_pairs={{0,3},{1,2},{2,1},{3,0},{4,7},{5,6},{6,5},{7,4},{8,11},{9,10},{10,... | collective-permute-start | bytes 1376264 | tf_op jit(solution)/shard_map/ppermute | solution.py:71
  (32 other events, 621.3 us)

commit v7 on v6

--- a/solution.py
+++ b/solution.py
@@ -63,7 +63,7 @@
 
 
 PAIR, RIGHT, DOWN = 1, 2, 4
-VMEM_LIMIT = 42 * 1024 * 1024
+VMEM_LIMIT = 39 * 1024 * 1024
 
 
 def swap(value, axis, mask):
@@ -364,13 +364,13 @@
     experts = [(w_gate, w_up, w_down), (w_gate_o, w_up_o, w_down_o)]
     shared = [(shared_gate, shared_up, shared_down), (packed_o, packed_o, shared_down_o)]
     pair31 = jnp.concatenate([z3, z1], axis=0)
-    r31, d31, a3, a1 = right(pair31), down(pair31), far(a2, 1), far(a0, 1)
+    r31, d31, a31 = right(pair31), down(pair31), far(jnp.concatenate([a2, a0], axis=0), 1)
     sides = [[(own, 0), (r0, 0), (d0, 0), (a0, 0)], [(z2, 0), (r2, 0), (d2, 0), (a2, 0)]]
     out = run_experts(sides, block, most, experts, shared, True)
-    out, (r31, d31, a3, a1) = pin(out, (r31, d31, a3, a1))
+    out, (r31, d31, a31) = pin(out, (r31, d31, a31))
     sums = out[0]
     from_right, from_down, from_far = right(out[1]), down(out[2]), far(out[3], 1)
-    sides = [[(z1, 0), (r31, 1), (d31, 1), (a1, 0)], [(z3, 0), (r31, 0), (d31, 0), (a3, 0)]]
+    sides = [[(z1, 0), (r31, 1), (d31, 1), (a31, 1)], [(z3, 0), (r31, 0), (d31, 0), (a31, 0)]]
     out = run_experts(sides, block, most, experts, [], False, (sums,))
     out, (from_right, from_down, from_far) = pin(out, (from_right, from_down, from_far))
     sum1, sum3 = out[:4], out[4:]
@@ -379,7 +379,6 @@
     hop2 = far(add_rows(sums[block:], from_right[block:], from_down[block:]), 1)
     across3, across1, hop2, plain3, plain1 = tie((across3, across1, hop2, sum3[2], sum1[1]))
     full3, full1 = add_rows(sum3[1], across3), add_rows(sum1[2], across1)
-    full3, plain3, plain1, full1 = tie((full3, plain3, plain1, full1))
     full3, plain3 = right(full3), down(plain3)
     full3, plain3, full1, plain1 = tie((full3, plain3, full1, plain1))
     full1, plain1 = down(full1), right(plain1)

time: 157 us -> 156 us (level)
  waiting for transfers between devices: 72 us -> 69 us
  starting transfers between devices: 30.2 us -> 32 us
    ppermute x30 -> x29, waiting for transfers between devices: 72 us -> 69 us  [swap(): return lax.ppermute(value, axis, [(i, i ^ mask) for i in range(size)])]
    ppermute x30 -> x29, starting transfers between devices: 30.2 us -> 32 us  [swap(): return lax.ppermute(value, axis, [(i, i ^ mask) for i in range(size)])]
    convert_element_type x6 -> x7, other arithmetic: 3.36 us -> 3.42 us  [add_rows(): return total.astype(dtype)]
  transfers between devices with their start and end apart: 30 -> 29, of which waited for: 15 -> 16; matrix products, arithmetic and copies ran while one was open for 2% -> 2% of each run, Pallas kernels for 30% -> 30%
where the time goes in v7:
time: 156 us; the launch traced here: 153 us
  waiting for transfers between devices  69 us (44%)
  Pallas kernels  45.7 us (29%)
  starting transfers between devices  32 us (21%)
  other arithmetic  5.81 us (4%)
    ppermute x29, waiting for transfers between devices, swap(): return lax.ppermute(value, axis, [(i, i ^ mask) for i in range(size)])  69 us
    pallas_call x2, Pallas kernels, run_experts(): pl.pallas_call(functools.partial(expert_body, dims), out_shape=[pltpu.HBM...  43.8 us
    ppermute x29, starting transfers between devices, swap(): return lax.ppermute(value, axis, [(i, i ^ mask) for i in range(size)])  32 us
    convert_element_type x7, other arithmetic, add_rows(): return total.astype(dtype)  3.42 us
  transfers between devices with their start and end apart: 29, of which 16 were waited for; matrix products, arithmetic and copies ran while one was open for 2% of the time, Pallas kernels for 30%

profile of v7, /device:TPU:8, one launch (start us, length us, event | category | flops | bytes accessed | tf_op | source)
XLA Modules:
  0.0 153.0 jit_solution(7000328225995734361)
XLA Ops:
  0.5 1.9 %shard_map.109.refs_0_ = bf16[64,3712]{1,0:T(8,128)(2,1)} custom-call(bf16[64,3584]{1,0:T(8,128)(2,1)} %tokens.1, s32[8,64]{1,0:T(8,128)} %bitcast.2, bf16[8,64]{1,0:T(8,128)(2,1)} %bitcast.3), custom_call_target="tpu_custom_call" | custom-call | tf_op jit(solution)/shard_map/pallas_call | solution.py:106
  2.4 2.6 %collective-permute-start = (bf16[64,3712]{1,0:T(8,128)(2,1)}, bf16[64,3712]{1,0:T(8,128)(2,1)S(1)}, u32[]{:S(2)}, u32[]{:S(2)}) collective-permute-start(bf16[64,3712]{1,0:T(8,128)(2,1)} %shard_map.109.refs_0_), channel_id=1, source_target_pairs={{0,2},{1,3},{2,0},{3,1},{4,6},{5,7},{6,4},{7,5},{8,10},{9,11},{10,... | collective-permute-start | bytes 1425416 | tf_op jit(solution)/shard_map/ppermute | solution.py:71
  5.0 1.5 collective-permute-start.1
  6.5 1.5 collective-permute-start.2
  8.1 2.3 %pad_maximum_fusion = bf16[3584,512]{1,0:T(8,128)(2,1)S(1)} fusion(bf16[3584,256]{1,0:T(8,128)(2,1)} %refs_16_.1, bf16[3584,256]{1,0:T(8,128)(2,1)} %refs_15_.1), kind=kLoop, calls=%fused_computation | loop fusion | flops 7340032 | bytes 7340032 | tf_op jit(solution)/shard_map/concatenate | solution.py:352
  10.4 15.3 %collective-permute-done.refs_4_ = bf16[64,3712]{1,0:T(8,128)(2,1)S(1)} collective-permute-done((bf16[64,3712]{1,0:T(8,128)(2,1)}, bf16[64,3712]{1,0:T(8,128)(2,1)S(1)}, u32[]{:S(2)}, u32[]{:S(2)}) %collective-permute-start) | collective-permute-done | bytes 475168 | tf_op jit(solution)/shard_map/ppermute | solution.py:71
  25.9 1.5 %collective-permute-start.5 = (bf16[64,3712]{1,0:T(8,128)(2,1)S(1)}, bf16[64,3712]{1,0:T(8,128)(2,1)S(1)}, u32[]{:S(2)}, u32[]{:S(2)}) collective-permute-start(bf16[64,3712]{1,0:T(8,128)(2,1)S(1)} %collective-permute-done.refs_4_), channel_id=1, source_target_pairs={{0,8},{4,12},{8,0},{12,4},{16,24},{20,28},{24,16},{28,20},{1,9},{5... | collective-permute-start | bytes 1425416 | tf_op jit(solution)/shard_map/ppermute | solution.py:71
  27.4 1.5 collective-permute-start.6
  30.2 9.0 %collective-permute-done.5.refs_5_ = bf16[64,3712]{1,0:T(8,128)(2,1)S(1)} collective-permute-done((bf16[64,3712]{1,0:T(8,128)(2,1)S(1)}, bf16[64,3712]{1,0:T(8,128)(2,1)S(1)}, u32[]{:S(2)}, u32[]{:S(2)}) %collective-permute-start.5) | collective-permute-done | bytes 475168 | tf_op jit(solution)/shard_map/ppermute | solution.py:71
  44.4 10.6 %collective-permute-done.9.refs_7_ = bf16[64,3712]{1,0:T(8,128)(2,1)S(1)} collective-permute-done((bf16[64,3712]{1,0:T(8,128)(2,1)S(1)}, bf16[64,3712]{1,0:T(8,128)(2,1)S(1)}, u32[]{:S(2)}, u32[]{:S(2)}) %collective-permute-start.9) | collective-permute-done | bytes 475168 | tf_op jit(solution)/shard_map/ppermute | solution.py:71
  55.8 1.6 %collective-permute-start.14 = (bf16[128,3712]{1,0:T(8,128)(2,1)S(1)}, bf16[128,3712]{1,0:T(8,128)(2,1)S(1)}, u32[]{:S(2)}, u32[]{:S(2)}) collective-permute-start(bf16[128,3712]{1,0:T(8,128)(2,1)S(1)} %constant_dynamic-update-slice_fusion), channel_id=1, source_target_pairs={{0,8},{4,12},{8,0},{12,4},{16,24},{20,28},{24,16},{28,20},{1,9},{5... | collective-permute-start | bytes 2850824 | tf_op jit(solution)/shard_map/ppermute | solution.py:71
  57.4 1.5 collective-permute-start.15
  60.4 23.5 %shard_map.110 = (bf16[128,3584]{1,0:T(8,128)(2,1)}, bf16[128,3584]{1,0:T(8,128)(2,1)}, bf16[128,3584]{1,0:T(8,128)(2,1)}, bf16[128,3584]{1,0:T(8,128)(2,1)}) custom-call(bf16[64,3712]{1,0:T(8,128)(2,1)} %shard_map.109.refs_0_, bf16[64,3712]{1,0:T(8,128)(2,1)} %copy-done.14, bf16[64,3712]{1,0:T(8,128)(2,1)} %copy-done.15, bf16[64,3712]{1,0:T(8,128)(2,1)} %copy-done.9, ...), custom_call_target="tpu_custom_call" | custom-call | flops 15971909632 | bytes 66330624 | tf_op jit(solution)/shard_map/pallas_call | solution.py:310
  86.2 20.2 %shard_map.111 = (bf16[64,3584]{1,0:T(8,128)(2,1)}, bf16[64,3584]{1,0:T(8,128)(2,1)}, bf16[64,3584]{1,0:T(8,128)(2,1)}, bf16[64,3584]{1,0:T(8,128)(2,1)}, bf16[6...) custom-call(bf16[64,3712]{1,0:T(8,128)(2,1)} %copy-done.11, ...), custom_call_target="tpu_custom_call" | custom-call | flops 13153337344 | bytes 54501376 | tf_op jit(solution)/shard_map/pallas_call | solution.py:310
  106.5 1.5 %add_convert_fusion.6 = (bf16[64,3584]{1,0:T(8,128)(2,1)S(1)}, bf16[64,3584]{1,0:T(8,128)(2,1)S(1)}) fusion(bf16[64,3584]{1,0:T(8,128)(2,1)} %get-tuple-element.111, bf16[128,3584]{1,0:T(8,128)(2,1)S(1)} %collective-permute-done.19, bf16[64,3584]{1,0:T(8,128)(2,1)} %get-tuple-element.109), kind=kLoop, calls=%fused_computation.8 | loop fusion | flops 1835008 | bytes 2752512 | tf_op jit(solution)/shard_map/convert_element_type | solution.py:82
  109.4 1.5 collective-permute-start.21
  112.4 5.9 %collective-permute-done.20 = bf16[64,3584]{1,0:T(8,128)(2,1)S(1)} collective-permute-done((bf16[64,3584]{1,0:T(8,128)(2,1)S(1)}, bf16[64,3584]{1,0:T(8,128)(2,1)S(1)}, u32[]{:S(2)}, u32[]{:S(2)}) %collective-permute-start.20) | collective-permute-done | bytes 458784 | tf_op jit(solution)/shard_map/ppermute | solution.py:71
  122.4 6.6 %collective-permute-done.23 = bf16[64,3584]{1,0:T(8,128)(2,1)S(1)} collective-permute-done((bf16[64,3584]{1,0:T(8,128)(2,1)S(1)}, bf16[64,3584]{1,0:T(8,128)(2,1)S(1)}, u32[]{:S(2)}, u32[]{:S(2)}) %collective-permute-start.23) | collective-permute-done | bytes 458784 | tf_op jit(solution)/shard_map/ppermute | solution.py:71
  128.9 3.5 %collective-permute-done.24 = bf16[64,3584]{1,0:T(8,128)(2,1)S(1)} collective-permute-done((bf16[64,3584]{1,0:T(8,128)(2,1)S(1)}, bf16[64,3584]{1,0:T(8,128)(2,1)S(1)}, u32[]{:S(2)}, u32[]{:S(2)}) %collective-permute-start.24) | collective-permute-done | bytes 458784 | tf_op jit(solution)/shard_map/ppermute | solution.py:71
  134.0 2.5 %collective-permute-start.25 = (bf16[64,3584]{1,0:T(8,128)(2,1)S(1)}, bf16[64,3584]{1,0:T(8,128)(2,1)S(1)}, u32[]{:S(2)}, u32[]{:S(2)}) collective-permute-start(bf16[64,3584]{1,0:T(8,128)(2,1)S(1)} %add_convert_fusion.2), channel_id=1, source_target_pairs={{0,3},{1,2},{2,1},{3,0},{4,7},{5,6},{6,5},{7,4},{8,11},{9,10},{10,... | collective-permute-start | bytes 1376264 | tf_op jit(solution)/shard_map/ppermute | solution.py:71
  136.5 4.4 %collective-permute-done.27 = bf16[64,3584]{1,0:T(8,128)(2,1)S(1)} collective-permute-done((bf16[64,3584]{1,0:T(8,128)(2,1)S(1)}, bf16[64,3584]{1,0:T(8,128)(2,1)S(1)}, u32[]{:S(2)}, u32[]{:S(2)}) %collective-permute-start.27) | collective-permute-done | bytes 458784 | tf_op jit(solution)/shard_map/ppermute | solution.py:71
  141.6 1.9 %collective-permute-start.28 = (bf16[64,3584]{1,0:T(8,128)(2,1)S(1)}, bf16[64,3584]{1,0:T(8,128)(2,1)S(1)}, u32[]{:S(2)}, u32[]{:S(2)}) collective-permute-start(bf16[64,3584]{1,0:T(8,128)(2,1)S(1)} %add_convert_fusion.1), channel_id=1, source_target_pairs={{0,1},{1,0},{2,3},{3,2},{4,5},{5,4},{6,7},{7,6},{8,9},{9,8},{10,11... | collective-permute-start | bytes 1376264 | tf_op jit(solution)/shard_map/ppermute | solution.py:71
  143.5 5.6 %collective-permute-done.25 = bf16[64,3584]{1,0:T(8,128)(2,1)S(1)} collective-permute-done((bf16[64,3584]{1,0:T(8,128)(2,1)S(1)}, bf16[64,3584]{1,0:T(8,128)(2,1)S(1)}, u32[]{:S(2)}, u32[]{:S(2)}) %collective-permute-start.25) | collective-permute-done | bytes 458784 | tf_op jit(solution)/shard_map/ppermute | solution.py:71
  149.1 2.8 %collective-permute-done.28 = bf16[64,3584]{1,0:T(8,128)(2,1)S(1)} collective-permute-done((bf16[64,3584]{1,0:T(8,128)(2,1)S(1)}, bf16[64,3584]{1,0:T(8,128)(2,1)S(1)}, u32[]{:S(2)}, u32[]{:S(2)}) %collective-permute-start.28) | collective-permute-done | bytes 458784 | tf_op jit(solution)/shard_map/ppermute | solution.py:71
  (96 shorter events, 21.7 us)
Async XLA Ops:
  0.0 25.7 %collective-permute-start.3 = (bf16[1,3584,1024]{2,1,0:T(8,128)(2,1)}, bf16[1,3584,1024]{2,1,0:T(8,128)(2,1)}, u32[]{:S(2)}, u32[]{:S(2)}) collective-permute-start(bf16[1,3584,1024]{2,1,0:T(8,128)(2,1)} %refs_9_.3), channel_id=1, source_target_pairs={{0,4},{4,0},{8,12},{12,8},{16,20},{20,16},{24,28},{28,24},{1,5},{5... | collective-permute-start | bytes 22020104 | tf_op jit(solution)/shard_map/ppermute | solution.py:71
  0.0 25.8 %collective-permute-start.4 = (bf16[1,3584,1024]{2,1,0:T(8,128)(2,1)}, bf16[1,3584,1024]{2,1,0:T(8,128)(2,1)}, u32[]{:S(2)}, u32[]{:S(2)}) collective-permute-start(bf16[1,3584,1024]{2,1,0:T(8,128)(2,1)} %refs_10_.3), channel_id=1, source_target_pairs={{0,4},{4,0},{8,12},{12,8},{16,20},{20,16},{24,28},{28,24},{1,5},{5... | collective-permute-start | bytes 22020104 | tf_op jit(solution)/shard_map/ppermute | solution.py:71
  2.4 23.3 %collective-permute-start = (bf16[64,3712]{1,0:T(8,128)(2,1)}, bf16[64,3712]{1,0:T(8,128)(2,1)S(1)}, u32[]{:S(2)}, u32[]{:S(2)}) collective-permute-start(bf16[64,3712]{1,0:T(8,128)(2,1)} %shard_map.109.refs_0_), channel_id=1, source_target_pairs={{0,2},{1,3},{2,0},{3,1},{4,6},{5,7},{6,4},{7,5},{8,10},{9,11},{10,... | collective-permute-start | bytes 1425416 | tf_op jit(solution)/shard_map/ppermute | solution.py:71
  5.0 20.7 %collective-permute-start.1 = (bf16[64,3712]{1,0:T(8,128)(2,1)}, bf16[64,3712]{1,0:T(8,128)(2,1)S(1)}, u32[]{:S(2)}, u32[]{:S(2)}) collective-permute-start(bf16[64,3712]{1,0:T(8,128)(2,1)} %shard_map.109.refs_0_), channel_id=1, source_target_pairs={{0,8},{4,12},{8,0},{12,4},{16,24},{20,28},{24,16},{28,20},{1,9},{5... | collective-permute-start | bytes 1425416 | tf_op jit(solution)/shard_map/ppermute | solution.py:71
  6.5 19.2 %collective-permute-start.2 = (bf16[64,3712]{1,0:T(8,128)(2,1)}, bf16[64,3712]{1,0:T(8,128)(2,1)S(1)}, u32[]{:S(2)}, u32[]{:S(2)}) collective-permute-start(bf16[64,3712]{1,0:T(8,128)(2,1)} %shard_map.109.refs_0_), channel_id=1, source_target_pairs={{0,16},{4,20},{8,24},{12,28},{16,0},{20,4},{24,8},{28,12},{1,17},{... | collective-permute-start | bytes 1425416 | tf_op jit(solution)/shard_map/ppermute | solution.py:71
  25.8 15.8 %collective-permute-start.8 = (bf16[1,1024,3584]{2,1,0:T(8,128)(2,1)S(1)}, bf16[1,1024,3584]{2,1,0:T(8,128)(2,1)S(1)}, u32[]{:S(2)}, u32[]{:S(2)}) collective-permute-start(bf16[1,1024,3584]{2,1,0:T(8,128)(2,1)S(1)} %copy-done.1), channel_id=1, source_target_pairs={{0,4},{4,0},{8,12},{12,8},{16,20},{20,16},{24,28},{28,24},{1,5},{5... | collective-permute-start | bytes 22020104 | tf_op jit(solution)/shard_map/ppermute | solution.py:71
  25.9 13.3 %collective-permute-start.5 = (bf16[64,3712]{1,0:T(8,128)(2,1)S(1)}, bf16[64,3712]{1,0:T(8,128)(2,1)S(1)}, u32[]{:S(2)}, u32[]{:S(2)}) collective-permute-start(bf16[64,3712]{1,0:T(8,128)(2,1)S(1)} %collective-permute-done.refs_4_), channel_id=1, source_target_pairs={{0,8},{4,12},{8,0},{12,4},{16,24},{20,28},{24,16},{28,20},{1,9},{5... | collective-permute-start | bytes 1425416 | tf_op jit(solution)/shard_map/ppermute | solution.py:71
  27.4 12.9 %collective-permute-start.6 = (bf16[64,3712]{1,0:T(8,128)(2,1)S(1)}, bf16[64,3712]{1,0:T(8,128)(2,1)S(1)}, u32[]{:S(2)}, u32[]{:S(2)}) collective-permute-start(bf16[64,3712]{1,0:T(8,128)(2,1)S(1)} %collective-permute-done.refs_4_), channel_id=1, source_target_pairs={{0,16},{4,20},{8,24},{12,28},{16,0},{20,4},{24,8},{28,12},{1,17},{... | collective-permute-start | bytes 1425416 | tf_op jit(solution)/shard_map/ppermute | solution.py:71
  28.9 12.7 %collective-permute-start.7 = (bf16[64,3712]{1,0:T(8,128)(2,1)S(1)}, bf16[64,3712]{1,0:T(8,128)(2,1)S(1)}, u32[]{:S(2)}, u32[]{:S(2)}) collective-permute-start(bf16[64,3712]{1,0:T(8,128)(2,1)S(1)} %collective-permute-done.refs_4_), channel_id=1, source_target_pairs={{0,1},{1,0},{2,3},{3,2},{4,5},{5,4},{6,7},{7,6},{8,9},{9,8},{10,11... | collective-permute-start | bytes 1425416 | tf_op jit(solution)/shard_map/ppermute | solution.py:71
  41.6 14.1 %collective-permute-start.12 = (bf16[3584,512]{1,0:T(8,128)(2,1)S(1)}, bf16[3584,512]{1,0:T(8,128)(2,1)S(1)}, u32[]{:S(2)}, u32[]{:S(2)}) collective-permute-start(bf16[3584,512]{1,0:T(8,128)(2,1)S(1)} %pad_maximum_fusion), channel_id=1, source_target_pairs={{0,4},{4,0},{8,12},{12,8},{16,20},{20,16},{24,28},{28,24},{1,5},{5... | collective-permute-start | bytes 11010056 | tf_op jit(solution)/shard_map/ppermute | solution.py:71
  41.7 14.0 %collective-permute-start.13 = (bf16[256,3584]{1,0:T(8,128)(2,1)}, bf16[256,3584]{1,0:T(8,128)(2,1)S(1)}, u32[]{:S(2)}, u32[]{:S(2)}) collective-permute-start(bf16[256,3584]{1,0:T(8,128)(2,1)} %refs_17_.1), channel_id=1, source_target_pairs={{0,4},{4,0},{8,12},{12,8},{16,20},{20,16},{24,28},{28,24},{1,5},{5... | collective-permute-start | bytes 5505032 | tf_op jit(solution)/shard_map/ppermute | solution.py:71
  42.2 12.9 %collective-permute-start.9 = (bf16[64,3712]{1,0:T(8,128)(2,1)S(1)}, bf16[64,3712]{1,0:T(8,128)(2,1)S(1)}, u32[]{:S(2)}, u32[]{:S(2)}) collective-permute-start(bf16[64,3712]{1,0:T(8,128)(2,1)S(1)} %collective-permute-done.6.refs_6_), channel_id=1, source_target_pairs={{0,8},{4,12},{8,0},{12,4},{16,24},{20,28},{24,16},{28,20},{1,9},{5... | collective-permute-start | bytes 1425416 | tf_op jit(solution)/shard_map/ppermute | solution.py:71
  42.7 12.6 %collective-permute-start.10 = (bf16[64,3712]{1,0:T(8,128)(2,1)S(1)}, bf16[64,3712]{1,0:T(8,128)(2,1)S(1)}, u32[]{:S(2)}, u32[]{:S(2)}) collective-permute-start(bf16[64,3712]{1,0:T(8,128)(2,1)S(1)} %collective-permute-done.1.refs_1_), channel_id=1, source_target_pairs={{0,16},{4,20},{8,24},{12,28},{16,0},{20,4},{24,8},{28,12},{1,17},{... | collective-permute-start | bytes 1425416 | tf_op jit(solution)/shard_map/ppermute | solution.py:71
  43.2 12.5 %collective-permute-start.11 = (bf16[64,3712]{1,0:T(8,128)(2,1)}, bf16[64,3712]{1,0:T(8,128)(2,1)S(1)}, u32[]{:S(2)}, u32[]{:S(2)}) collective-permute-start(bf16[64,3712]{1,0:T(8,128)(2,1)} %shard_map.109.refs_0_), channel_id=1, source_target_pairs={{0,1},{1,0},{2,3},{3,2},{4,5},{5,4},{6,7},{7,6},{8,9},{9,8},{10,11... | collective-permute-start | bytes 1425416 | tf_op jit(solution)/shard_map/ppermute | solution.py:71
  55.8 28.1 %collective-permute-start.14 = (bf16[128,3712]{1,0:T(8,128)(2,1)S(1)}, bf16[128,3712]{1,0:T(8,128)(2,1)S(1)}, u32[]{:S(2)}, u32[]{:S(2)}) collective-permute-start(bf16[128,3712]{1,0:T(8,128)(2,1)S(1)} %constant_dynamic-update-slice_fusion), channel_id=1, source_target_pairs={{0,8},{4,12},{8,0},{12,4},{16,24},{20,28},{24,16},{28,20},{1,9},{5... | collective-permute-start | bytes 2850824 | tf_op jit(solution)/shard_map/ppermute | solution.py:71
  57.4 26.6 %collective-permute-start.15 = (bf16[128,3712]{1,0:T(8,128)(2,1)S(1)}, bf16[128,3712]{1,0:T(8,128)(2,1)S(1)}, u32[]{:S(2)}, u32[]{:S(2)}) collective-permute-start(bf16[128,3712]{1,0:T(8,128)(2,1)S(1)} %constant_dynamic-update-slice_fusion), channel_id=1, source_target_pairs={{0,16},{4,20},{8,24},{12,28},{16,0},{20,4},{24,8},{28,12},{1,17},{... | collective-permute-start | bytes 2850824 | tf_op jit(solution)/shard_map/ppermute | solution.py:71
  59.0 25.0 %collective-permute-start.16 = (bf16[128,3712]{1,0:T(8,128)(2,1)S(1)}, bf16[128,3712]{1,0:T(8,128)(2,1)S(1)}, u32[]{:S(2)}, u32[]{:S(2)}) collective-permute-start(bf16[128,3712]{1,0:T(8,128)(2,1)S(1)} %pad_maximum_fusion.1), channel_id=1, source_target_pairs={{0,1},{1,0},{2,3},{3,2},{4,5},{5,4},{6,7},{7,6},{8,9},{9,8},{10,11... | collective-permute-start | bytes 2850824 | tf_op jit(solution)/shard_map/ppermute | solution.py:71
  84.0 22.4 %collective-permute-start.17 = (bf16[128,3584]{1,0:T(8,128)(2,1)}, bf16[128,3584]{1,0:T(8,128)(2,1)S(1)}, u32[]{:S(2)}, u32[]{:S(2)}) collective-permute-start(bf16[128,3584]{1,0:T(8,128)(2,1)} %get-tuple-element.102), channel_id=1, source_target_pairs={{0,8},{4,12},{8,0},{12,4},{16,24},{20,28},{24,16},{28,20},{1,9},{5... | collective-permute-start | bytes 2752520 | tf_op jit(solution)/shard_map/ppermute | solution.py:71
  84.6 21.8 %collective-permute-start.18 = (bf16[128,3584]{1,0:T(8,128)(2,1)}, bf16[128,3584]{1,0:T(8,128)(2,1)S(1)}, u32[]{:S(2)}, u32[]{:S(2)}) collective-permute-start(bf16[128,3584]{1,0:T(8,128)(2,1)} %get-tuple-element.103), channel_id=1, source_target_pairs={{0,16},{4,20},{8,24},{12,28},{16,0},{20,4},{24,8},{28,12},{1,17},{... | collective-permute-start | bytes 2752520 | tf_op jit(solution)/shard_map/ppermute | solution.py:71
  85.1 21.4 %collective-permute-start.19 = (bf16[128,3584]{1,0:T(8,128)(2,1)}, bf16[128,3584]{1,0:T(8,128)(2,1)S(1)}, u32[]{:S(2)}, u32[]{:S(2)}) collective-permute-start(bf16[128,3584]{1,0:T(8,128)(2,1)} %get-tuple-element.104), channel_id=1, source_target_pairs={{0,1},{1,0},{2,3},{3,2},{4,5},{5,4},{6,7},{7,6},{8,9},{9,8},{10,11... | collective-permute-start | bytes 2752520 | tf_op jit(solution)/shard_map/ppermute | solution.py:71
  108.1 10.2 %collective-permute-start.20 = (bf16[64,3584]{1,0:T(8,128)(2,1)S(1)}, bf16[64,3584]{1,0:T(8,128)(2,1)S(1)}, u32[]{:S(2)}, u32[]{:S(2)}) collective-permute-start(bf16[64,3584]{1,0:T(8,128)(2,1)S(1)} %get-tuple-element.126), channel_id=1, source_target_pairs={{0,16},{4,20},{8,24},{12,28},{16,0},{20,4},{24,8},{28,12},{1,17},{... | collective-permute-start | bytes 1376264 | tf_op jit(solution)/shard_map/ppermute | solution.py:71
  121.1 11.3 %collective-permute-start.24 = (bf16[64,3584]{1,0:T(8,128)(2,1)S(1)}, bf16[64,3584]{1,0:T(8,128)(2,1)S(1)}, u32[]{:S(2)}, u32[]{:S(2)}) collective-permute-start(bf16[64,3584]{1,0:T(8,128)(2,1)S(1)} %copy-done.23), channel_id=1, source_target_pairs={{0,16},{4,20},{8,24},{12,28},{16,0},{20,4},{24,8},{28,12},{1,17},{... | collective-permute-start | bytes 1376264 | tf_op jit(solution)/shard_map/ppermute | solution.py:71
  134.0 15.2 %collective-permute-start.25 = (bf16[64,3584]{1,0:T(8,128)(2,1)S(1)}, bf16[64,3584]{1,0:T(8,128)(2,1)S(1)}, u32[]{:S(2)}, u32[]{:S(2)}) collective-permute-start(bf16[64,3584]{1,0:T(8,128)(2,1)S(1)} %add_convert_fusion.2), channel_id=1, source_target_pairs={{0,3},{1,2},{2,1},{3,0},{4,7},{5,6},{6,5},{7,4},{8,11},{9,10},{10,... | collective-permute-start | bytes 1376264 | tf_op jit(solution)/shard_map/ppermute | solution.py:71
  141.6 10.4 %collective-permute-start.28 = (bf16[64,3584]{1,0:T(8,128)(2,1)S(1)}, bf16[64,3584]{1,0:T(8,128)(2,1)S(1)}, u32[]{:S(2)}, u32[]{:S(2)}) collective-permute-start(bf16[64,3584]{1,0:T(8,128)(2,1)S(1)} %add_convert_fusion.1), channel_id=1, source_target_pairs={{0,1},{1,0},{2,3},{3,2},{4,5},{5,4},{6,7},{7,6},{8,9},{9,8},{10,11... | collective-permute-start | bytes 1376264 | tf_op jit(solution)/shard_map/ppermute | solution.py:71
  (29 other events, 535.9 us)

commit v8 on v7

--- a/solution.py
+++ b/solution.py
@@ -380,7 +380,8 @@
     across3, across1, hop2, plain3, plain1 = tie((across3, across1, hop2, sum3[2], sum1[1]))
     full3, full1 = add_rows(sum3[1], across3), add_rows(sum1[2], across1)
     full3, plain3 = right(full3), down(plain3)
-    full3, plain3, full1, plain1 = tie((full3, plain3, full1, plain1))
+    full3, plain1 = tie((full3, plain1))
+    plain3, full1 = tie((plain3, full1))
     full1, plain1 = down(full1), right(plain1)
     part3 = add_rows(sum3[0], plain3, full3, hop2)
     back3 = far(part3, 3)

time: 156 us -> 155 us (level)
  transfers between devices with their start and end apart: 29 -> 29, of which waited for: 16 -> 15; matrix products, arithmetic and copies ran while one was open for 2% -> 2% of each run, Pallas kernels for 30% -> 30%
where the time goes in v8:
time: 155 us; the launch traced here: 153 us
  waiting for transfers between devices  68.5 us (44%)
  Pallas kernels  45.7 us (29%)
  starting transfers between devices  32.2 us (21%)
  other arithmetic  5.81 us (4%)
    ppermute x29, waiting for transfers between devices, swap(): return lax.ppermute(value, axis, [(i, i ^ mask) for i in range(size)])  68.5 us
    pallas_call x2, Pallas kernels, run_experts(): pl.pallas_call(functools.partial(expert_body, dims), out_shape=[pltpu.HBM...  43.8 us
    ppermute x29, starting transfers between devices, swap(): return lax.ppermute(value, axis, [(i, i ^ mask) for i in range(size)])  32.2 us
    convert_element_type x7, other arithmetic, add_rows(): return total.astype(dtype)  3.42 us
  transfers between devices with their start and end apart: 29, of which 15 were waited for; matrix products, arithmetic and copies ran while one was open for 2% of the time, Pallas kernels for 30%

profile of v8, /device:TPU:8, one launch (start us, length us, event | category | flops | bytes accessed | tf_op | source)
XLA Modules:
  0.0 152.7 jit_solution(12619458411307520148)
XLA Ops:
  0.5 1.9 %shard_map.109.refs_0_ = bf16[64,3712]{1,0:T(8,128)(2,1)} custom-call(bf16[64,3584]{1,0:T(8,128)(2,1)} %tokens.1, s32[8,64]{1,0:T(8,128)} %bitcast.2, bf16[8,64]{1,0:T(8,128)(2,1)} %bitcast.3), custom_call_target="tpu_custom_call" | custom-call | tf_op jit(solution)/shard_map/pallas_call | solution.py:106
  2.4 2.6 %collective-permute-start = (bf16[64,3712]{1,0:T(8,128)(2,1)}, bf16[64,3712]{1,0:T(8,128)(2,1)S(1)}, u32[]{:S(2)}, u32[]{:S(2)}) collective-permute-start(bf16[64,3712]{1,0:T(8,128)(2,1)} %shard_map.109.refs_0_), channel_id=1, source_target_pairs={{0,2},{1,3},{2,0},{3,1},{4,6},{5,7},{6,4},{7,5},{8,10},{9,11},{10,... | collective-permute-start | bytes 1425416 | tf_op jit(solution)/shard_map/ppermute | solution.py:71
  5.0 1.5 collective-permute-start.1
  6.5 1.5 collective-permute-start.2
  8.1 2.3 %pad_maximum_fusion = bf16[3584,512]{1,0:T(8,128)(2,1)S(1)} fusion(bf16[3584,256]{1,0:T(8,128)(2,1)} %refs_16_.1, bf16[3584,256]{1,0:T(8,128)(2,1)} %refs_15_.1), kind=kLoop, calls=%fused_computation | loop fusion | flops 7340032 | bytes 7340032 | tf_op jit(solution)/shard_map/concatenate | solution.py:352
  10.4 15.3 %collective-permute-done.refs_4_ = bf16[64,3712]{1,0:T(8,128)(2,1)S(1)} collective-permute-done((bf16[64,3712]{1,0:T(8,128)(2,1)}, bf16[64,3712]{1,0:T(8,128)(2,1)S(1)}, u32[]{:S(2)}, u32[]{:S(2)}) %collective-permute-start) | collective-permute-done | bytes 475168 | tf_op jit(solution)/shard_map/ppermute | solution.py:71
  25.9 1.5 %collective-permute-start.5 = (bf16[64,3712]{1,0:T(8,128)(2,1)S(1)}, bf16[64,3712]{1,0:T(8,128)(2,1)S(1)}, u32[]{:S(2)}, u32[]{:S(2)}) collective-permute-start(bf16[64,3712]{1,0:T(8,128)(2,1)S(1)} %collective-permute-done.refs_4_), channel_id=1, source_target_pairs={{0,8},{4,12},{8,0},{12,4},{16,24},{20,28},{24,16},{28,20},{1,9},{5... | collective-permute-start | bytes 1425416 | tf_op jit(solution)/shard_map/ppermute | solution.py:71
  27.4 1.5 collective-permute-start.6
  30.2 9.0 %collective-permute-done.5.refs_5_ = bf16[64,3712]{1,0:T(8,128)(2,1)S(1)} collective-permute-done((bf16[64,3712]{1,0:T(8,128)(2,1)S(1)}, bf16[64,3712]{1,0:T(8,128)(2,1)S(1)}, u32[]{:S(2)}, u32[]{:S(2)}) %collective-permute-start.5) | collective-permute-done | bytes 475168 | tf_op jit(solution)/shard_map/ppermute | solution.py:71
  44.4 10.6 %collective-permute-done.9.refs_7_ = bf16[64,3712]{1,0:T(8,128)(2,1)S(1)} collective-permute-done((bf16[64,3712]{1,0:T(8,128)(2,1)S(1)}, bf16[64,3712]{1,0:T(8,128)(2,1)S(1)}, u32[]{:S(2)}, u32[]{:S(2)}) %collective-permute-start.9) | collective-permute-done | bytes 475168 | tf_op jit(solution)/shard_map/ppermute | solution.py:71
  55.8 1.6 %collective-permute-start.14 = (bf16[128,3712]{1,0:T(8,128)(2,1)S(1)}, bf16[128,3712]{1,0:T(8,128)(2,1)S(1)}, u32[]{:S(2)}, u32[]{:S(2)}) collective-permute-start(bf16[128,3712]{1,0:T(8,128)(2,1)S(1)} %constant_dynamic-update-slice_fusion), channel_id=1, source_target_pairs={{0,8},{4,12},{8,0},{12,4},{16,24},{20,28},{24,16},{28,20},{1,9},{5... | collective-permute-start | bytes 2850824 | tf_op jit(solution)/shard_map/ppermute | solution.py:71
  57.4 1.5 collective-permute-start.15
  60.4 23.5 %shard_map.110 = (bf16[128,3584]{1,0:T(8,128)(2,1)}, bf16[128,3584]{1,0:T(8,128)(2,1)}, bf16[128,3584]{1,0:T(8,128)(2,1)}, bf16[128,3584]{1,0:T(8,128)(2,1)}) custom-call(bf16[64,3712]{1,0:T(8,128)(2,1)} %shard_map.109.refs_0_, bf16[64,3712]{1,0:T(8,128)(2,1)} %copy-done.14, bf16[64,3712]{1,0:T(8,128)(2,1)} %copy-done.15, bf16[64,3712]{1,0:T(8,128)(2,1)} %copy-done.9, ...), custom_call_target="tpu_custom_call" | custom-call | flops 15971909632 | bytes 66330624 | tf_op jit(solution)/shard_map/pallas_call | solution.py:310
  86.2 20.2 %shard_map.111 = (bf16[64,3584]{1,0:T(8,128)(2,1)}, bf16[64,3584]{1,0:T(8,128)(2,1)}, bf16[64,3584]{1,0:T(8,128)(2,1)}, bf16[64,3584]{1,0:T(8,128)(2,1)}, bf16[6...) custom-call(bf16[64,3712]{1,0:T(8,128)(2,1)} %copy-done.11, ...), custom_call_target="tpu_custom_call" | custom-call | flops 13153337344 | bytes 54501376 | tf_op jit(solution)/shard_map/pallas_call | solution.py:310
  106.5 1.5 %add_convert_fusion.6 = (bf16[64,3584]{1,0:T(8,128)(2,1)S(1)}, bf16[64,3584]{1,0:T(8,128)(2,1)S(1)}) fusion(bf16[64,3584]{1,0:T(8,128)(2,1)} %get-tuple-element.110, bf16[128,3584]{1,0:T(8,128)(2,1)S(1)} %collective-permute-done.19, bf16[64,3584]{1,0:T(8,128)(2,1)} %get-tuple-element.108), kind=kLoop, calls=%fused_computation.8 | loop fusion | flops 1835008 | bytes 2752512 | tf_op jit(solution)/shard_map/convert_element_type | solution.py:82
  109.4 1.5 collective-permute-start.21
  112.4 6.2 %collective-permute-done.20 = bf16[64,3584]{1,0:T(8,128)(2,1)S(1)} collective-permute-done((bf16[64,3584]{1,0:T(8,128)(2,1)S(1)}, bf16[64,3584]{1,0:T(8,128)(2,1)S(1)}, u32[]{:S(2)}, u32[]{:S(2)}) %collective-permute-start.20) | collective-permute-done | bytes 458784 | tf_op jit(solution)/shard_map/ppermute | solution.py:71
  120.7 1.6 %collective-permute-start.24 = (bf16[64,3584]{1,0:T(8,128)(2,1)S(1)}, bf16[64,3584]{1,0:T(8,128)(2,1)S(1)}, u32[]{:S(2)}, u32[]{:S(2)}) collective-permute-start(bf16[64,3584]{1,0:T(8,128)(2,1)S(1)} %add_convert_fusion.3), channel_id=1, source_target_pairs={{0,8},{4,12},{8,0},{12,4},{16,24},{20,28},{24,16},{28,20},{1,9},{5... | collective-permute-start | bytes 1376264 | tf_op jit(solution)/shard_map/ppermute | solution.py:71
  122.4 8.8 %collective-permute-done.23 = bf16[64,3584]{1,0:T(8,128)(2,1)S(1)} collective-permute-done((bf16[64,3584]{1,0:T(8,128)(2,1)S(1)}, bf16[64,3584]{1,0:T(8,128)(2,1)S(1)}, u32[]{:S(2)}, u32[]{:S(2)}) %collective-permute-start.23) | collective-permute-done | bytes 458784 | tf_op jit(solution)/shard_map/ppermute | solution.py:71
  133.2 2.7 %collective-permute-start.25 = (bf16[64,3584]{1,0:T(8,128)(2,1)S(1)}, bf16[64,3584]{1,0:T(8,128)(2,1)S(1)}, u32[]{:S(2)}, u32[]{:S(2)}) collective-permute-start(bf16[64,3584]{1,0:T(8,128)(2,1)S(1)} %add_convert_fusion.2), channel_id=1, source_target_pairs={{0,3},{1,2},{2,1},{3,0},{4,7},{5,6},{6,5},{7,4},{8,11},{9,10},{10,... | collective-permute-start | bytes 1376264 | tf_op jit(solution)/shard_map/ppermute | solution.py:71
  135.8 3.8 %collective-permute-done.27 = bf16[64,3584]{1,0:T(8,128)(2,1)S(1)} collective-permute-done((bf16[64,3584]{1,0:T(8,128)(2,1)S(1)}, bf16[64,3584]{1,0:T(8,128)(2,1)S(1)}, u32[]{:S(2)}, u32[]{:S(2)}) %collective-permute-start.27) | collective-permute-done | bytes 458784 | tf_op jit(solution)/shard_map/ppermute | solution.py:71
  140.3 1.7 %collective-permute-start.28 = (bf16[64,3584]{1,0:T(8,128)(2,1)S(1)}, bf16[64,3584]{1,0:T(8,128)(2,1)S(1)}, u32[]{:S(2)}, u32[]{:S(2)}) collective-permute-start(bf16[64,3584]{1,0:T(8,128)(2,1)S(1)} %add_convert_fusion.1), channel_id=1, source_target_pairs={{0,1},{1,0},{2,3},{3,2},{4,5},{5,4},{6,7},{7,6},{8,9},{9,8},{10,11... | collective-permute-start | bytes 1376264 | tf_op jit(solution)/shard_map/ppermute | solution.py:71
  142.0 7.0 %collective-permute-done.25 = bf16[64,3584]{1,0:T(8,128)(2,1)S(1)} collective-permute-done((bf16[64,3584]{1,0:T(8,128)(2,1)S(1)}, bf16[64,3584]{1,0:T(8,128)(2,1)S(1)}, u32[]{:S(2)}, u32[]{:S(2)}) %collective-permute-start.25) | collective-permute-done | bytes 458784 | tf_op jit(solution)/shard_map/ppermute | solution.py:71
  149.0 2.6 %collective-permute-done.28 = bf16[64,3584]{1,0:T(8,128)(2,1)S(1)} collective-permute-done((bf16[64,3584]{1,0:T(8,128)(2,1)S(1)}, bf16[64,3584]{1,0:T(8,128)(2,1)S(1)}, u32[]{:S(2)}, u32[]{:S(2)}) %collective-permute-start.28) | collective-permute-done | bytes 458784 | tf_op jit(solution)/shard_map/ppermute | solution.py:71
  (96 shorter events, 20.4 us)
Async XLA Ops:
  0.0 25.7 %collective-permute-start.3 = (bf16[1,3584,1024]{2,1,0:T(8,128)(2,1)}, bf16[1,3584,1024]{2,1,0:T(8,128)(2,1)}, u32[]{:S(2)}, u32[]{:S(2)}) collective-permute-start(bf16[1,3584,1024]{2,1,0:T(8,128)(2,1)} %refs_9_.3), channel_id=1, source_target_pairs={{0,4},{4,0},{8,12},{12,8},{16,20},{20,16},{24,28},{28,24},{1,5},{5... | collective-permute-start | bytes 22020104 | tf_op jit(solution)/shard_map/ppermute | solution.py:71
  0.0 25.8 %collective-permute-start.4 = (bf16[1,3584,1024]{2,1,0:T(8,128)(2,1)}, bf16[1,3584,1024]{2,1,0:T(8,128)(2,1)}, u32[]{:S(2)}, u32[]{:S(2)}) collective-permute-start(bf16[1,3584,1024]{2,1,0:T(8,128)(2,1)} %refs_10_.3), channel_id=1, source_target_pairs={{0,4},{4,0},{8,12},{12,8},{16,20},{20,16},{24,28},{28,24},{1,5},{5... | collective-permute-start | bytes 22020104 | tf_op jit(solution)/shard_map/ppermute | solution.py:71
  2.4 23.3 %collective-permute-start = (bf16[64,3712]{1,0:T(8,128)(2,1)}, bf16[64,3712]{1,0:T(8,128)(2,1)S(1)}, u32[]{:S(2)}, u32[]{:S(2)}) collective-permute-start(bf16[64,3712]{1,0:T(8,128)(2,1)} %shard_map.109.refs_0_), channel_id=1, source_target_pairs={{0,2},{1,3},{2,0},{3,1},{4,6},{5,7},{6,4},{7,5},{8,10},{9,11},{10,... | collective-permute-start | bytes 1425416 | tf_op jit(solution)/shard_map/ppermute | solution.py:71
  5.0 20.7 %collective-permute-start.1 = (bf16[64,3712]{1,0:T(8,128)(2,1)}, bf16[64,3712]{1,0:T(8,128)(2,1)S(1)}, u32[]{:S(2)}, u32[]{:S(2)}) collective-permute-start(bf16[64,3712]{1,0:T(8,128)(2,1)} %shard_map.109.refs_0_), channel_id=1, source_target_pairs={{0,8},{4,12},{8,0},{12,4},{16,24},{20,28},{24,16},{28,20},{1,9},{5... | collective-permute-start | bytes 1425416 | tf_op jit(solution)/shard_map/ppermute | solution.py:71
  6.5 19.2 %collective-permute-start.2 = (bf16[64,3712]{1,0:T(8,128)(2,1)}, bf16[64,3712]{1,0:T(8,128)(2,1)S(1)}, u32[]{:S(2)}, u32[]{:S(2)}) collective-permute-start(bf16[64,3712]{1,0:T(8,128)(2,1)} %shard_map.109.refs_0_), channel_id=1, source_target_pairs={{0,16},{4,20},{8,24},{12,28},{16,0},{20,4},{24,8},{28,12},{1,17},{... | collective-permute-start | bytes 1425416 | tf_op jit(solution)/shard_map/ppermute | solution.py:71
  25.8 15.8 %collective-permute-start.8 = (bf16[1,1024,3584]{2,1,0:T(8,128)(2,1)S(1)}, bf16[1,1024,3584]{2,1,0:T(8,128)(2,1)S(1)}, u32[]{:S(2)}, u32[]{:S(2)}) collective-permute-start(bf16[1,1024,3584]{2,1,0:T(8,128)(2,1)S(1)} %copy-done.1), channel_id=1, source_target_pairs={{0,4},{4,0},{8,12},{12,8},{16,20},{20,16},{24,28},{28,24},{1,5},{5... | collective-permute-start | bytes 22020104 | tf_op jit(solution)/shard_map/ppermute | solution.py:71
  25.9 13.3 %collective-permute-start.5 = (bf16[64,3712]{1,0:T(8,128)(2,1)S(1)}, bf16[64,3712]{1,0:T(8,128)(2,1)S(1)}, u32[]{:S(2)}, u32[]{:S(2)}) collective-permute-start(bf16[64,3712]{1,0:T(8,128)(2,1)S(1)} %collective-permute-done.refs_4_), channel_id=1, source_target_pairs={{0,8},{4,12},{8,0},{12,4},{16,24},{20,28},{24,16},{28,20},{1,9},{5... | collective-permute-start | bytes 1425416 | tf_op jit(solution)/shard_map/ppermute | solution.py:71
  27.4 12.9 %collective-permute-start.6 = (bf16[64,3712]{1,0:T(8,128)(2,1)S(1)}, bf16[64,3712]{1,0:T(8,128)(2,1)S(1)}, u32[]{:S(2)}, u32[]{:S(2)}) collective-permute-start(bf16[64,3712]{1,0:T(8,128)(2,1)S(1)} %collective-permute-done.refs_4_), channel_id=1, source_target_pairs={{0,16},{4,20},{8,24},{12,28},{16,0},{20,4},{24,8},{28,12},{1,17},{... | collective-permute-start | bytes 1425416 | tf_op jit(solution)/shard_map/ppermute | solution.py:71
  28.9 12.7 %collective-permute-start.7 = (bf16[64,3712]{1,0:T(8,128)(2,1)S(1)}, bf16[64,3712]{1,0:T(8,128)(2,1)S(1)}, u32[]{:S(2)}, u32[]{:S(2)}) collective-permute-start(bf16[64,3712]{1,0:T(8,128)(2,1)S(1)} %collective-permute-done.refs_4_), channel_id=1, source_target_pairs={{0,1},{1,0},{2,3},{3,2},{4,5},{5,4},{6,7},{7,6},{8,9},{9,8},{10,11... | collective-permute-start | bytes 1425416 | tf_op jit(solution)/shard_map/ppermute | solution.py:71
  41.6 14.1 %collective-permute-start.12 = (bf16[3584,512]{1,0:T(8,128)(2,1)S(1)}, bf16[3584,512]{1,0:T(8,128)(2,1)S(1)}, u32[]{:S(2)}, u32[]{:S(2)}) collective-permute-start(bf16[3584,512]{1,0:T(8,128)(2,1)S(1)} %pad_maximum_fusion), channel_id=1, source_target_pairs={{0,4},{4,0},{8,12},{12,8},{16,20},{20,16},{24,28},{28,24},{1,5},{5... | collective-permute-start | bytes 11010056 | tf_op jit(solution)/shard_map/ppermute | solution.py:71
  41.7 14.0 %collective-permute-start.13 = (bf16[256,3584]{1,0:T(8,128)(2,1)}, bf16[256,3584]{1,0:T(8,128)(2,1)S(1)}, u32[]{:S(2)}, u32[]{:S(2)}) collective-permute-start(bf16[256,3584]{1,0:T(8,128)(2,1)} %refs_17_.1), channel_id=1, source_target_pairs={{0,4},{4,0},{8,12},{12,8},{16,20},{20,16},{24,28},{28,24},{1,5},{5... | collective-permute-start | bytes 5505032 | tf_op jit(solution)/shard_map/ppermute | solution.py:71
  42.2 12.9 %collective-permute-start.9 = (bf16[64,3712]{1,0:T(8,128)(2,1)S(1)}, bf16[64,3712]{1,0:T(8,128)(2,1)S(1)}, u32[]{:S(2)}, u32[]{:S(2)}) collective-permute-start(bf16[64,3712]{1,0:T(8,128)(2,1)S(1)} %collective-permute-done.6.refs_6_), channel_id=1, source_target_pairs={{0,8},{4,12},{8,0},{12,4},{16,24},{20,28},{24,16},{28,20},{1,9},{5... | collective-permute-start | bytes 1425416 | tf_op jit(solution)/shard_map/ppermute | solution.py:71
  42.7 12.6 %collective-permute-start.10 = (bf16[64,3712]{1,0:T(8,128)(2,1)S(1)}, bf16[64,3712]{1,0:T(8,128)(2,1)S(1)}, u32[]{:S(2)}, u32[]{:S(2)}) collective-permute-start(bf16[64,3712]{1,0:T(8,128)(2,1)S(1)} %collective-permute-done.1.refs_1_), channel_id=1, source_target_pairs={{0,16},{4,20},{8,24},{12,28},{16,0},{20,4},{24,8},{28,12},{1,17},{... | collective-permute-start | bytes 1425416 | tf_op jit(solution)/shard_map/ppermute | solution.py:71
  43.2 12.5 %collective-permute-start.11 = (bf16[64,3712]{1,0:T(8,128)(2,1)}, bf16[64,3712]{1,0:T(8,128)(2,1)S(1)}, u32[]{:S(2)}, u32[]{:S(2)}) collective-permute-start(bf16[64,3712]{1,0:T(8,128)(2,1)} %shard_map.109.refs_0_), channel_id=1, source_target_pairs={{0,1},{1,0},{2,3},{3,2},{4,5},{5,4},{6,7},{7,6},{8,9},{9,8},{10,11... | collective-permute-start | bytes 1425416 | tf_op jit(solution)/shard_map/ppermute | solution.py:71
  55.8 28.1 %collective-permute-start.14 = (bf16[128,3712]{1,0:T(8,128)(2,1)S(1)}, bf16[128,3712]{1,0:T(8,128)(2,1)S(1)}, u32[]{:S(2)}, u32[]{:S(2)}) collective-permute-start(bf16[128,3712]{1,0:T(8,128)(2,1)S(1)} %constant_dynamic-update-slice_fusion), channel_id=1, source_target_pairs={{0,8},{4,12},{8,0},{12,4},{16,24},{20,28},{24,16},{28,20},{1,9},{5... | collective-permute-start | bytes 2850824 | tf_op jit(solution)/shard_map/ppermute | solution.py:71
  57.4 26.6 %collective-permute-start.15 = (bf16[128,3712]{1,0:T(8,128)(2,1)S(1)}, bf16[128,3712]{1,0:T(8,128)(2,1)S(1)}, u32[]{:S(2)}, u32[]{:S(2)}) collective-permute-start(bf16[128,3712]{1,0:T(8,128)(2,1)S(1)} %constant_dynamic-update-slice_fusion), channel_id=1, source_target_pairs={{0,16},{4,20},{8,24},{12,28},{16,0},{20,4},{24,8},{28,12},{1,17},{... | collective-permute-start | bytes 2850824 | tf_op jit(solution)/shard_map/ppermute | solution.py:71
  59.0 25.0 %collective-permute-start.16 = (bf16[128,3712]{1,0:T(8,128)(2,1)S(1)}, bf16[128,3712]{1,0:T(8,128)(2,1)S(1)}, u32[]{:S(2)}, u32[]{:S(2)}) collective-permute-start(bf16[128,3712]{1,0:T(8,128)(2,1)S(1)} %pad_maximum_fusion.1), channel_id=1, source_target_pairs={{0,1},{1,0},{2,3},{3,2},{4,5},{5,4},{6,7},{7,6},{8,9},{9,8},{10,11... | collective-permute-start | bytes 2850824 | tf_op jit(solution)/shard_map/ppermute | solution.py:71
  84.0 22.4 %collective-permute-start.17 = (bf16[128,3584]{1,0:T(8,128)(2,1)}, bf16[128,3584]{1,0:T(8,128)(2,1)S(1)}, u32[]{:S(2)}, u32[]{:S(2)}) collective-permute-start(bf16[128,3584]{1,0:T(8,128)(2,1)} %get-tuple-element.102), channel_id=1, source_target_pairs={{0,8},{4,12},{8,0},{12,4},{16,24},{20,28},{24,16},{28,20},{1,9},{5... | collective-permute-start | bytes 2752520 | tf_op jit(solution)/shard_map/ppermute | solution.py:71
  84.6 21.8 %collective-permute-start.18 = (bf16[128,3584]{1,0:T(8,128)(2,1)}, bf16[128,3584]{1,0:T(8,128)(2,1)S(1)}, u32[]{:S(2)}, u32[]{:S(2)}) collective-permute-start(bf16[128,3584]{1,0:T(8,128)(2,1)} %get-tuple-element.103), channel_id=1, source_target_pairs={{0,16},{4,20},{8,24},{12,28},{16,0},{20,4},{24,8},{28,12},{1,17},{... | collective-permute-start | bytes 2752520 | tf_op jit(solution)/shard_map/ppermute | solution.py:71
  85.1 21.4 %collective-permute-start.19 = (bf16[128,3584]{1,0:T(8,128)(2,1)}, bf16[128,3584]{1,0:T(8,128)(2,1)S(1)}, u32[]{:S(2)}, u32[]{:S(2)}) collective-permute-start(bf16[128,3584]{1,0:T(8,128)(2,1)} %get-tuple-element.104), channel_id=1, source_target_pairs={{0,1},{1,0},{2,3},{3,2},{4,5},{5,4},{6,7},{7,6},{8,9},{9,8},{10,11... | collective-permute-start | bytes 2752520 | tf_op jit(solution)/shard_map/ppermute | solution.py:71
  119.9 11.2 %collective-permute-start.23 = (bf16[64,3584]{1,0:T(8,128)(2,1)S(1)}, bf16[64,3584]{1,0:T(8,128)(2,1)S(1)}, u32[]{:S(2)}, u32[]{:S(2)}) collective-permute-start(bf16[64,3584]{1,0:T(8,128)(2,1)S(1)} %copy-done.23), channel_id=1, source_target_pairs={{0,16},{4,20},{8,24},{12,28},{16,0},{20,4},{24,8},{28,12},{1,17},{... | collective-permute-start | bytes 1376264 | tf_op jit(solution)/shard_map/ppermute | solution.py:71
  120.7 11.0 %collective-permute-start.24 = (bf16[64,3584]{1,0:T(8,128)(2,1)S(1)}, bf16[64,3584]{1,0:T(8,128)(2,1)S(1)}, u32[]{:S(2)}, u32[]{:S(2)}) collective-permute-start(bf16[64,3584]{1,0:T(8,128)(2,1)S(1)} %add_convert_fusion.3), channel_id=1, source_target_pairs={{0,8},{4,12},{8,0},{12,4},{16,24},{20,28},{24,16},{28,20},{1,9},{5... | collective-permute-start | bytes 1376264 | tf_op jit(solution)/shard_map/ppermute | solution.py:71
  133.2 15.8 %collective-permute-start.25 = (bf16[64,3584]{1,0:T(8,128)(2,1)S(1)}, bf16[64,3584]{1,0:T(8,128)(2,1)S(1)}, u32[]{:S(2)}, u32[]{:S(2)}) collective-permute-start(bf16[64,3584]{1,0:T(8,128)(2,1)S(1)} %add_convert_fusion.2), channel_id=1, source_target_pairs={{0,3},{1,2},{2,1},{3,0},{4,7},{5,6},{6,5},{7,4},{8,11},{9,10},{10,... | collective-permute-start | bytes 1376264 | tf_op jit(solution)/shard_map/ppermute | solution.py:71
  140.3 11.3 %collective-permute-start.28 = (bf16[64,3584]{1,0:T(8,128)(2,1)S(1)}, bf16[64,3584]{1,0:T(8,128)(2,1)S(1)}, u32[]{:S(2)}, u32[]{:S(2)}) collective-permute-start(bf16[64,3584]{1,0:T(8,128)(2,1)S(1)} %add_convert_fusion.1), channel_id=1, source_target_pairs={{0,1},{1,0},{2,3},{3,2},{4,5},{5,4},{6,7},{7,6},{8,9},{9,8},{10,11... | collective-permute-start | bytes 1376264 | tf_op jit(solution)/shard_map/ppermute | solution.py:71
  (29 other events, 533.4 us)
